TPU v7x, 32 devices: a whole 2x2x4 slice. The times are simulated.
32 devices in a mesh: groups: 2 (over y), fsdp: 4 (over z), dp: 2 (over x), rep: 2 (over core).
Axes of the slice: x: 2, y: 2, z: 4, core: 2. Of those that a mesh axis runs over, the one named last changes fastest.
Arguments:
- hidden_in: bfloat16 [8, 2048, 8192], P(('groups', 'dp'), 'rep', 'fsdp'), parts along dimension 0, may hold values from -6 to 6
- query_grad: bfloat16 [8, 2048, 8192], P(('groups', 'dp'), 'rep', 'fsdp'), parts along dimension 0, may hold values from -6 to 6
- value_grad: bfloat16 [8, 2048, 1024], P(('groups', 'dp'), 'rep', 'fsdp'), parts along dimension 0, may hold values from -6 to 6
- query_down: bfloat16 [8192, 64], P('fsdp'), may hold values from -0.0625 to 0.0625
- query_up: bfloat16 [64, 8192], P(None, 'fsdp'), may hold values from -0.0625 to 0.0625
- value_down: bfloat16 [8192, 64], P('fsdp'), may hold values from -0.0625 to 0.0625
- value_up: bfloat16 [64, 1024], P(None, 'fsdp'), may hold values from -0.1875 to 0.1875
- lengths: int32 [8], P(('groups', 'dp')), parts along dimension 0, may hold values from 1 to 2048, 4100 in all
- owners: int32 [8], P('groups'), parts along dimension 0, may hold values from 0 to 3, each once
- proj_seed: int32 [1], replicated, may hold values from 0 to 999999
- offsets: int32 [7], replicated, may hold values from 0 to 1048575
Outputs:
- projected: float32 [8, 8192], P(('groups', 'dp'), ('fsdp', 'rep')), parts along dimension 0
There are 2 independent parts, one for each index of `groups`. A program takes and returns all parts, laid end to end along the dimension named above; an argument that names none is the same for every part. Nothing has to cross between parts.
Inputs may be any that keep to these rules, and one draw needn't show every extreme that they name: `lengths`: every example has at least one live position, and some example has 2048; the total given with the table holds within each group's 4 examples, not over the groups together. owners names every row once.
All inputs are finite; a program needn't handle non-finite values.
Results may differ from a plain program's by a relative error of at most 0.0003.
Values sent between devices are 32-bit elements; how exact they have to be, the bound alone decides.
No kernel may reach another device: no remote copies, remote signals or barrier semaphores. Data moves between devices by JAX's collectives and lax.ppermute only.
A program may use at most 128 MiB of HBM per device.

v0:
```python
import jax
import jax.numpy as jnp
from jax import lax
from jax.sharding import PartitionSpec as P

D = 8192
DQ = 8192
DV = 1024
R = 64
KP = 512
KR = 4
LMAX = 2048


def mix_bits(values):
    values = values ^ values >> 15 & 131071
    values = values * -2048144777
    values = values ^ values >> 13 & 524287
    values = values * -1028477379
    values = values ^ values >> 16 & 65535
    return values


def table_block(seed_value, offset, row_start, rows, cols):
    row_index = lax.broadcasted_iota(jnp.int32, (rows, cols), 0) + row_start
    col_index = lax.broadcasted_iota(jnp.int32, (rows, cols), 1)
    counter = offset + row_index * cols + col_index
    hashed = mix_bits(counter * -1640531535 + seed_value * 668265263)
    levels = (hashed & 255).astype(jnp.float32)
    return ((levels - 127.5) / 128.0).astype(jnp.bfloat16)


def per_device(
    hidden_in,
    query_grad,
    value_grad,
    query_down,
    query_up,
    value_down,
    value_up,
    lengths,
    owners,
    proj_seed,
    offsets,
):
    high = lax.Precision.HIGHEST
    seed_value = proj_seed[0]
    shard_pos = lax.axis_index("fsdp")
    half_pos = lax.axis_index("rep")
    data_pos = lax.axis_index("dp")
    local_count = hidden_in.shape[0]
    rows = hidden_in.shape[1]
    in_cols = hidden_in.shape[2]
    q_cols = query_grad.shape[2]
    v_cols = value_grad.shape[2]
    wide_in = table_block(seed_value, offsets[0], shard_pos * in_cols, in_cols, KP)
    wide_query = table_block(seed_value, offsets[1], shard_pos * q_cols, q_cols, KP)
    wide_value = table_block(seed_value, offsets[2], shard_pos * v_cols, v_cols, KP)
    rank_tables = [
        table_block(seed_value, offsets[3 + k], 0, R, KR).astype(jnp.float32) for k in range(4)
    ]
    rank_scale = (R / 3.0) ** (-0.5)
    token_weights = jnp.concatenate([wide_in, query_down, value_down], axis=1)
    query_weights = jnp.concatenate([wide_query, query_up.T], axis=1)
    value_weights = jnp.concatenate([wide_value, value_up.T], axis=1)

    def project_sides(low_rank):
        return jnp.concatenate(
            [
                jnp.dot(low_rank[:, k * R : (k + 1) * R], rank_tables[k], precision=high)
                for k in range(4)
            ],
            axis=1,
        )

    wides = []
    partials = []
    for item in range(local_count):
        tokens = hidden_in[item]
        qgrad = query_grad[item]
        vgrad = value_grad[item]
        from_tokens = jnp.dot(tokens, token_weights, preferred_element_type=jnp.float32)
        from_query = jnp.dot(qgrad, query_weights, preferred_element_type=jnp.float32)
        from_value = jnp.dot(vgrad, value_weights, preferred_element_type=jnp.float32)
        from_tokens, from_query, from_value = (from_tokens, from_query, from_value)
        wide_x = from_tokens[:, :KP] * (D / 3.0) ** (-0.5)
        wide_q = from_query[:, :KP] * (DQ / 3.0) ** (-0.5)
        wide_v = from_value[:, :KP] * (DV / 3.0) ** (-0.5)
        wides.append((wide_x, wide_q, wide_v))
        partials.append(
            jnp.concatenate(
                [
                    from_query[:, KP:],
                    from_value[:, KP:],
                    from_tokens[:, KP : KP + R],
                    from_tokens[:, KP + R :],
                ],
                axis=1,
            )
        )
    partial_rank = jnp.stack(partials)
    projected_rank = jnp.stack([project_sides(partial_rank[item]) for item in range(local_count)])
    sides = lax.psum(projected_rank, "fsdp")
    positions = half_pos * rows + lax.broadcasted_iota(jnp.int32, (rows, 1), 0)
    feat_rows = []
    for item in range(local_count):
        wide_x, wide_q, wide_v = wides[item]
        mask = (positions < lengths[item]).astype(jnp.float32)
        side = sides[item] * rank_scale * mask
        pair_blocks = jnp.dot(wide_x.T, side[:, : 2 * KR], precision=high)
        pair_blocks = pair_blocks.reshape(KP, 2, KR).transpose(1, 0, 2)
        query_block = jnp.dot(wide_q.T, side[:, 2 * KR : 3 * KR], precision=high)
        value_block = jnp.dot(wide_v.T, side[:, 3 * KR :], precision=high)
        feat_rows.append(
            jnp.concatenate(
                [pair_blocks.reshape(-1), query_block.reshape(-1), value_block.reshape(-1)]
            )
        )
    feats = jnp.stack(feat_rows) * LMAX ** (-0.5)
    examples = owners.shape[0]
    targets = lax.dynamic_slice_in_dim(owners, data_pos * local_count, local_count, 0)
    one_hot = (
        lax.broadcasted_iota(jnp.int32, (examples, local_count), 0) == targets[None, :]
    ).astype(jnp.float32)
    shares = lax.psum_scatter(feats, ("fsdp", "rep"), scatter_dimension=1, tiled=True)
    result = lax.psum_scatter(
        jnp.dot(one_hot, shares, precision=high), "dp", scatter_dimension=0, tiled=True
    )
    return result


def solution(mesh):
    placed = (
        P(("groups", "dp"), "rep", "fsdp"),
        P(("groups", "dp"), "rep", "fsdp"),
        P(("groups", "dp"), "rep", "fsdp"),
        P("fsdp", None),
        P(None, "fsdp"),
        P("fsdp", None),
        P(None, "fsdp"),
        P(("groups", "dp")),
        P("groups"),
        P(),
        P(),
    )
    return jax.shard_map(
        per_device,
        mesh=mesh,
        in_specs=placed,
        out_specs=P(("groups", "dp"), ("fsdp", "rep")),
        check_vma=False,
    )
```

profile of v0, /device:TPU:0, one launch (start us, length us, event | category | flops | bytes accessed | tf_op | source)
XLA Modules:
  0.0 175.6 jit_solution(15548919012007125474)
XLA Ops:
  6.5 1.6 fusion.186
  10.0 1.2 copy.36
  11.3 1.2 copy.37
  12.5 5.0 %multiply_convert_fusion = (bf16[2048,512]{1,0:T(8,128)(2,1)S(1)}, bf16[2048,512]{1,0:T(8,128)(2,1)S(1)}) fusion(s32[2048]{0:T(1024)S(1)} %fusion.66, s32[]{:T(128)} %bitcast.1, s32[2048]{0:T(1024)S(1)} %fusion.67), kind=kLoop, calls=%fused_computation.11 | loop fusion | flops 39845888 | bytes 4210692 | tf_op jit(solution)/shard_map/convert_element_type | solution.py:30
  17.5 5.5 %fusion.18 = f32[1024,640]{0,1:T(8,128)S(1)} fusion(bf16[2,1024,2048]{2,1,0:T(8,128)(2,1)} %param.11, bf16[2048,64]{1,0:T(8,128)(2,1)S(1)} %copy.37, bf16[2048,64]{1,0:T(8,128)(2,1)S(1)} %copy.36, bf16[2048,512]{1,0:T(8,128)(2,1)S(1)} %get-tuple-element.17), kind=kOutput, calls=%fused_computation.28 | convolution fusion | flops 2692218880 | bytes 9437184 | tf_op jit(solution)/shard_map/dot_general | solution.py:82
  23.1 3.2 %fusion.21 = f32[1024,640]{0,1:T(8,128)S(1)} fusion(bf16[2,1024,2048]{2,1,0:T(8,128)(2,1)S(1)} %bitcast.83, bf16[2048,64]{1,0:T(8,128)(2,1)S(1)} %copy.37, bf16[2048,64]{1,0:T(8,128)(2,1)S(1)} %copy.36, bf16[2048,512]{1,0:T(8,128)(2,1)S(1)} %get-tuple-element.17), kind=kOutput, calls=%fused_computation.29 | convolution fusion | flops 2692218880 | bytes 9961472 | tf_op jit(solution)/shard_map/dot_general | solution.py:82
  28.6 6.7 %fusion.24 = f32[1024,576]{0,1:T(8,128)} fusion(bf16[2,1024,2048]{2,1,0:T(8,128)(2,1)} %param.12, bf16[2048,64]{1,0:T(8,128)(2,1)S(1)} %copy.38, bf16[2048,512]{1,0:T(8,128)(2,1)S(1)} %get-tuple-element.16), kind=kOutput, calls=%fused_computation.30 | convolution fusion | flops 2420637696 | bytes 8912896 | tf_op jit(solution)/shard_map/dot_general | solution.py:83
  35.3 6.8 %fusion.27 = f32[1024,576]{0,1:T(8,128)} fusion(bf16[2,1024,2048]{2,1,0:T(8,128)(2,1)} %param.12, bf16[2048,64]{1,0:T(8,128)(2,1)S(1)} %copy.38, bf16[2048,512]{1,0:T(8,128)(2,1)S(1)} %get-tuple-element.16), kind=kOutput, calls=%fused_computation.31 | convolution fusion | flops 2420637696 | bytes 8912896 | tf_op jit(solution)/shard_map/dot_general | solution.py:83
  43.3 1.6 convolution_bitcast_fusion.1
  44.9 2.0 %convolution_bitcast_fusion = f32[1024,576]{0,1:T(8,128)S(1)} fusion(bf16[2,1024,256]{2,1,0:T(8,128)(2,1)} %param.13, bf16[256,64]{1,0:T(8,128)(2,1)S(1)} %copy.39, bf16[256,512]{1,0:T(8,128)(2,1)S(1)} %multiply_convert_fusion.2), kind=kOutput, calls=%fused_computation.32 | convolution fusion | flops 302579712 | bytes 3178496 | tf_op jit(solution)/shard_map/dot_general | solution.py:84
  48.3 1.2 fusion.56
  49.4 1.2 fusion.48
  52.5 1.3 fusion.70
  53.8 35.3 %all-reduce.3.cloned.1.call-done = f32[2,1024,16]{1,2,0:T(8,128)} async-done(((f32[2,1024,16]{1,2,0:T(8,128)}), f32[2,1024,16]{1,2,0:T(8,128)}) %all-reduce.3.cloned.1.call-update) | async-done | bytes 131088 | tf_op jit(solution)/shard_map/psum | solution.py:103
  90.1 3.5 %fusion.17 = f32[512,8]{0,1:T(8,128)S(1)} fusion(f32[1024,640]{0,1:T(8,128)} %copy-done.4, f32[1024,16]{0,1:T(8,128)S(1)} %get-tuple-element.5), kind=kOutput, calls=%fused_computation.27 | convolution fusion | flops 50855936 | bytes 2146304 | tf_op jit(solution)/shard_map/dot_general | solution.py:110
  93.6 3.5 %fusion.16 = f32[512,4]{1,0:T(8,128)S(1)} fusion(f32[1024,576]{0,1:T(8,128)} %fusion.24, f32[1024,16]{0,1:T(8,128)S(1)} %get-tuple-element.5), kind=kOutput, calls=%fused_computation.25 | convolution fusion | flops 25690112 | bytes 2121728 | tf_op jit(solution)/shard_map/dot_general | solution.py:112
  97.1 1.8 %fusion.15 = f32[512,4]{1,0:T(8,128)S(1)} fusion(f32[1024,576]{0,1:T(8,128)S(1)} %copy-done.1, f32[1024,16]{0,1:T(8,128)S(1)} %get-tuple-element.5), kind=kOutput, calls=%fused_computation.23 | convolution fusion | flops 25690112 | bytes 2121728 | tf_op jit(solution)/shard_map/dot_general | solution.py:113
  98.9 1.9 %fusion.14 = f32[512,8]{0,1:T(8,128)S(1)} fusion(f32[1024,640]{0,1:T(8,128)S(1)} %copy-done.3, f32[1024,16]{0,1:T(8,128)S(1)} %get-tuple-element.6), kind=kOutput, calls=%fused_computation.21 | convolution fusion | flops 50855936 | bytes 2146304 | tf_op jit(solution)/shard_map/dot_general | solution.py:110
  100.8 1.8 %fusion.13 = f32[512,4]{1,0:T(8,128)S(1)} fusion(f32[1024,576]{0,1:T(8,128)S(1)} %copy-done.5, f32[1024,16]{0,1:T(8,128)S(1)} %get-tuple-element.6), kind=kOutput, calls=%fused_computation.19 | convolution fusion | flops 25690112 | bytes 2121728 | tf_op jit(solution)/shard_map/dot_general | solution.py:112
  102.6 1.8 %fusion.12 = f32[512,4]{1,0:T(8,128)S(1)} fusion(f32[1024,576]{0,1:T(8,128)S(1)} %convolution_bitcast_fusion, f32[1024,16]{0,1:T(8,128)S(1)} %get-tuple-element.6), kind=kOutput, calls=%fused_computation.17 | convolution fusion | flops 25690112 | bytes 2121728 | tf_op jit(solution)/shard_map/dot_general | solution.py:113
  106.2 2.6 %copy.50 = f32[2,8192]{0,1:T(8,128)} copy(f32[2,8192]{1,0:T(2,128)S(1)} %maximum_multiply_fusion) | data formatting | bytes 131072
  110.8 47.9 %reduce-scatter.4.cloned.1.call-done = f32[1024,2]{1,0:T(8,128)} async-done(((f32[8192,2]{1,0:T(8,128)}), f32[1024,2]{1,0:T(8,128)}) %reduce-scatter.4.cloned.1.call-update) | async-done | bytes 8208
  158.7 1.4 fusion.36
  160.0 8.1 %all-reduce = f32[4,1024]{1,0:T(4,128)S(1)} all-reduce(f32[4,1024]{1,0:T(4,128)S(1)} %fusion.36), channel_id=3, replica_groups=mesh['groups'=2,'fsdp'=4,'dp'=2,'rep'=2] {'dp'}, use_global_device_ids=true, to_apply=%region_2.0.clone | all-reduce | flops 4096 | bytes 32768
  (68 shorter events, 12.6 us)
Async XLA Ops:
  6.5 82.5 %all-reduce.3.cloned.1.call-start = ((), (), s32[]{:S(2)}) async-start(), calls=%async_computation.1 | async-start | bytes 262144 | tf_op jit(solution)/shard_map/psum | solution.py:103
  12.5 10.5 %slice-start = ((s8[8388608]{0:T(1024)(128)(4,1)}), s8[4194304]{0:T(1024)(128)(4,1)S(1)}, s32[]{:S(2)}) async-start(s8[8388608]{0:T(1024)(128)(4,1)} %bitcast.82), calls=%async_computation.3 | async-start | bytes 8388608
  17.5 5.5 %slice-start.1 = ((s8[8388608]{0:T(1024)(128)(4,1)}), s8[4194304]{0:T(1024)(128)(4,1)S(1)}, s32[]{:S(2)}) async-start(s8[8388608]{0:T(1024)(128)(4,1)} %bitcast.82), calls=%async_computation.4 | async-start | bytes 8388608
  23.0 4.7 %copy-start.4 = (f32[1024,640]{0,1:T(8,128)}, f32[1024,640]{0,1:T(8,128)S(1)}, u32[]{:S(2)}) copy-start(f32[1024,640]{0,1:T(8,128)S(1)} %fusion.18) | copy-start | bytes 7864324
  23.1 5.3 %copy-start.6 = (bf16[64,2048]{1,0:T(8,128)(2,1)S(1)}, bf16[64,2048]{1,0:T(8,128)(2,1)}, u32[]{:S(2)}) copy-start(bf16[64,2048]{1,0:T(8,128)(2,1)} %param.15) | copy-start | bytes 786436
  26.2 1.9 %copy-start.2 = (f32[1024,640]{0,1:T(8,128)}, f32[1024,640]{0,1:T(8,128)S(1)}, u32[]{:S(2)}) copy-start(f32[1024,640]{0,1:T(8,128)S(1)} %fusion.21) | copy-start | bytes 7864324
  35.3 7.8 %copy-start.7 = (bf16[64,256]{1,0:T(8,128)(2,1)S(1)}, bf16[64,256]{1,0:T(8,128)(2,1)}, u32[]{:S(2)}) copy-start(bf16[64,256]{1,0:T(8,128)(2,1)} %param.17) | copy-start | bytes 98308
  44.9 5.7 %copy-start = (f32[1024,576]{0,1:T(8,128)}, f32[1024,576]{0,1:T(8,128)S(1)}, u32[]{:S(2)}) copy-start(f32[1024,576]{0,1:T(8,128)S(1)} %convolution_bitcast_fusion.1) | copy-start | bytes 7077892
  44.9 6.9 %copy-start.8 = (s32[2]{0:T(128)S(1)}, s32[2]{0:T(128)}, u32[]{:S(2)}) copy-start(s32[2]{0:T(128)} %param.18) | copy-start | bytes 28
  51.8 106.9 %reduce-scatter.4.cloned.1.call-start = ((), (), s32[]{:S(2)}) async-start(), calls=%async_computation.2 | async-start | bytes 4718592
  89.1 8.1 %copy-start.1 = (f32[1024,576]{0,1:T(8,128)S(1)}, f32[1024,576]{0,1:T(8,128)}, u32[]{:S(2)}) copy-start(f32[1024,576]{0,1:T(8,128)} %copy-done) | copy-start | bytes 7077892
  93.6 5.3 %copy-start.3 = (f32[1024,640]{0,1:T(8,128)S(1)}, f32[1024,640]{0,1:T(8,128)}, u32[]{:S(2)}) copy-start(f32[1024,640]{0,1:T(8,128)} %copy-done.2) | copy-start | bytes 7864324
  97.1 3.7 %copy-start.5 = (f32[1024,576]{0,1:T(8,128)S(1)}, f32[1024,576]{0,1:T(8,128)}, u32[]{:S(2)}) copy-start(f32[1024,576]{0,1:T(8,128)} %fusion.27) | copy-start | bytes 7077892
  108.8 0.7 copy-start.9
  108.8 0.7 copy-start.10
Sparse Core Ops, SparseCore 0:
  51.9 37.1 all-reduce.2
  109.0 49.6 reduce-scatter.3
where the time goes:
time: 176 us
  waiting for transfers between devices  83.1 us (47%)
  matrix products  45 us (26%)
  between operations  15.1 us (9%)
  other arithmetic  12.9 us (7%)
  local copies, waits for them, and re-layouts  11.3 us (6%)
  blocking collectives  8.14 us (5%)
    unnamed x3, waiting for transfers between devices  47.9 us
    psum x1, waiting for transfers between devices, per_device(): sides = lax.psum(projected_rank, 'fsdp')  35.3 us
    dot_general x2, matrix products, per_device(): jnp.dot(qgrad, query_weights, preferred_element_type=jnp.float32)  13.5 us
    dot_general x2, matrix products, per_device(): jnp.dot(tokens, token_weights, preferred_element_type=jnp.float32)  8.67 us
    unnamed x1, blocking collectives  8.14 us
    unnamed x31, local copies, waits for them, and re-layouts  6.96 us
    dot_general x2, matrix products, per_device(): pair_blocks = jnp.dot(wide_x.T, side[:, :2 * KR], precision=high)  5.38 us
    dot_general x2, matrix products, per_device(): query_block = jnp.dot(wide_q.T, side[:, 2 * KR:3 * KR], precision=high)  5.3 us
  transfers between devices with their start and end apart: 2, of which 2 were waited for; matrix products, arithmetic and copies ran while one was open for 2% of the time, Pallas kernels for 0%

commit v1 on v0

v1 whole, which is shorter than its diff:
```python
import functools

import jax
import jax.numpy as jnp
from jax import lax
from jax.experimental import pallas as pl
from jax.experimental.pallas import tpu as pltpu
from jax.sharding import PartitionSpec as P

D = 8192
DQ = 8192
DV = 1024
R = 64
KP = 512
KR = 4
LMAX = 2048
BLOCK = 256
SEED_MUL = 668265263
COUNT_MUL = -1640531535
BF16 = jnp.bfloat16
F32 = jnp.float32
SCALARS = 24


def mix_bits(values):
    values = values ^ lax.shift_right_logical(values, 15)
    values = values * -2048144777
    values = values ^ lax.shift_right_logical(values, 13)
    values = values * -1028477379
    return values ^ lax.shift_right_logical(values, 16)


def wrapped(value):
    return (value + 2**31) % 2**32 - 2**31


def centred(counter_hash):
    return (mix_bits(counter_hash) & 255).astype(F32) - 127.5


def split_rows(values):
    high = values.astype(BF16).astype(F32)
    return jnp.concatenate([high, values - high], axis=0).astype(BF16)


def join_rows(product):
    half = product.shape[0] // 2
    return product[:half] + product[half:]


def rank_rows(seed_value, offset, first):
    row = lax.broadcasted_iota(jnp.int32, (2 * KR, R), 0) - first
    col = lax.broadcasted_iota(jnp.int32, (2 * KR, R), 1)
    counter = offset + col * KR + row
    entry = centred(counter * COUNT_MUL + seed_value * SEED_MUL)
    return jnp.where((row >= 0) & (row < KR), entry, 0.0).astype(BF16)


def side_kernel(
    hidden_hbm,
    query_hbm,
    value_hbm,
    query_down_hbm,
    query_up_hbm,
    value_down_hbm,
    value_up_hbm,
    lengths_hbm,
    seed_hbm,
    offsets_hbm,
    side_ref,
    hidden_ref,
    query_ref,
    value_ref,
    query_down,
    query_up,
    value_down,
    value_up,
    lengths,
    seed,
    offsets,
    block_sem,
    factor_sem,
    scalar_sem,
):
    count, rows, _ = hidden_ref.shape
    blocks = rows // BLOCK
    start = lax.axis_index("rep") * rows
    scalars = [
        pltpu.make_async_copy(src, dst, scalar_sem.at[k])
        for k, (src, dst) in enumerate(
            ((lengths_hbm, lengths), (seed_hbm, seed), (offsets_hbm, offsets))
        )
    ]
    factors = [
        pltpu.make_async_copy(src, dst, factor_sem.at[k])
        for k, (src, dst) in enumerate(
            (
                (query_up_hbm, query_up),
                (value_up_hbm, value_up),
                (query_down_hbm, query_down),
                (value_down_hbm, value_down),
            )
        )
    ]
    for copy in scalars + factors:
        copy.start()
    arrays = ((query_hbm, query_ref), (value_hbm, value_ref), (hidden_hbm, hidden_ref))
    copies = [
        [
            [
                pltpu.make_async_copy(
                    src.at[item, pl.ds(block * BLOCK, BLOCK)],
                    dst.at[item, pl.ds(block * BLOCK, BLOCK)],
                    block_sem.at[k, item, block],
                )
                for block in range(blocks)
            ]
            for item in range(count)
        ]
        for k, (src, dst) in enumerate(arrays)
    ]
    scalars[0].wait()
    for per_array in copies:
        for item in range(count):
            for block in range(blocks):

                @pl.when(start + block * BLOCK < lengths[item])
                def _(copy=per_array[item][block]):
                    copy.start()

    for copy in scalars[1:] + factors:
        copy.wait()
    seed_value = seed[0]

    def up_map(factor, k, first):
        table = rank_rows(seed_value, offsets[3 + k], first)
        return jnp.dot(table, factor[...], preferred_element_type=F32)

    def down_map(factor, k, first):
        table = rank_rows(seed_value, offsets[3 + k], first)
        return lax.dot_general(
            table, factor[...], (((1,), (1,)), ((), ())), preferred_element_type=F32
        )

    from_query = split_rows(up_map(query_up, 0, 0))
    from_value = split_rows(up_map(value_up, 1, KR))
    from_hidden = split_rows(down_map(query_down, 2, 0) + down_map(value_down, 3, KR))

    def project(weights, data):
        product = lax.dot_general(
            weights, data, (((1,), (1,)), ((), ())), preferred_element_type=F32
        )
        return join_rows(product)

    def each_block(visit):
        for item in range(count):
            for block in range(blocks):
                live = start + block * BLOCK < lengths[item]
                visit(item, block, pl.ds(block * BLOCK, BLOCK), pl.ds(item * rows + block * BLOCK, BLOCK), live)

    def keep(item, block):
        position = lax.broadcasted_iota(jnp.int32, (2 * KR, BLOCK), 1)
        return position + (start + block * BLOCK) < lengths[item]

    def upper(item, block, here, out, live):
        @pl.when(live)
        def _():
            copies[0][item][block].wait()
            copies[1][item][block].wait()
            rows_ = project(from_query, query_ref[item, here, :])
            rows_ = rows_ + project(from_value, value_ref[item, here, :])
            side_ref[: 2 * KR, out] = jnp.where(keep(item, block), rows_, 0.0)

        @pl.when(jnp.logical_not(live))
        def _():
            side_ref[: 2 * KR, out] = jnp.zeros((2 * KR, BLOCK), F32)
            query_ref[item, here, :] = jnp.zeros((BLOCK, query_ref.shape[2]), BF16)
            value_ref[item, here, :] = jnp.zeros((BLOCK, value_ref.shape[2]), BF16)

    def lower(item, block, here, out, live):
        @pl.when(live)
        def _():
            copies[2][item][block].wait()
            rows_ = project(from_hidden, hidden_ref[item, here, :])
            side_ref[2 * KR :, out] = jnp.where(keep(item, block), rows_, 0.0)

        @pl.when(jnp.logical_not(live))
        def _():
            side_ref[2 * KR :, out] = jnp.zeros((2 * KR, BLOCK), F32)
            hidden_ref[item, here, :] = jnp.zeros((BLOCK, hidden_ref.shape[2]), BF16)

    each_block(upper)
    each_block(lower)


def table_kernel(step_rows, tables, seed_ref, offsets_ref, _, *outs):
    shard = lax.axis_index("fsdp")
    seed_term = seed_ref[0] * SEED_MUL
    for k, out in zip(tables, outs):
        rows = out.shape[0]
        row = lax.broadcasted_iota(jnp.int32, (step_rows, KP), 0)
        col = lax.broadcasted_iota(jnp.int32, (step_rows, KP), 1)
        counter = offsets_ref[k] + (row + shard * rows) * KP + col
        first = counter * COUNT_MUL + seed_term
        stride = wrapped(step_rows * KP * COUNT_MUL)

        def step(i, values, out=out, stride=stride):
            here = pl.ds(pl.multiple_of(i * step_rows, step_rows), step_rows)
            out[here, :] = centred(values).astype(BF16)
            return values + stride

        lax.fori_loop(0, rows // step_rows, step, first, unroll=4)


def feature_kernel(
    side_ref,
    hidden_ref,
    query_ref,
    value_ref,
    wide_in,
    wide_query,
    wide_value,
    owners_hbm,
    out_ref,
    owners,
    owner_sem,
):
    fetch = pltpu.make_async_copy(owners_hbm, owners, owner_sem)
    fetch.start()
    count, rows, _ = hidden_ref.shape
    half = 2 * KR

    def gathered(data_ref, first):
        parts = []
        for item in range(count):
            side = side_ref[first : first + half, item * rows : (item + 1) * rows]
            product = jnp.dot(split_rows(side), data_ref[item], preferred_element_type=F32)
            parts.append(join_rows(product))
        return jnp.concatenate(parts, axis=0)

    def widened(gathered_rows, table):
        product = jnp.dot(split_rows(gathered_rows), table[...], preferred_element_type=F32)
        return join_rows(product)

    side_scale = (R / 3.0) ** (-0.5) / 128.0 * LMAX ** (-0.5) / 128.0
    upper = widened(gathered(hidden_ref, 0), wide_in) * (side_scale * (D / 3.0) ** (-0.5))
    query = widened(gathered(query_ref, half), wide_query) * (side_scale * (DQ / 3.0) ** (-0.5))
    value = widened(gathered(value_ref, half), wide_value) * (side_scale * (DV / 3.0) ** (-0.5))
    group = lax.rem(lax.broadcasted_iota(jnp.int32, query.shape, 0), half)
    lower = jnp.where(group < KR, query, value)
    fetch.wait()
    first = lax.axis_index("dp") * count
    targets = [owners[first + item] for item in range(count)]
    halves, spots, pieces, slot_rows, width = out_ref.shape
    slots = slot_rows // KR
    chunks = halves * pieces
    per_block = KP // width
    zero = jnp.zeros((KR, KP), F32)
    for spot in range(spots):
        for block in range(4):
            source, at = (upper, lower)[block // 2], (block % 2) * KR
            wanted = []
            for slot in range(slots):
                total = zero
                for item in range(count):
                    rows_ = source[item * half + at : item * half + at + KR]
                    total = total + jnp.where(targets[item] == spot * slots + slot, rows_, 0.0)
                wanted.append(total)
            wanted = jnp.concatenate(wanted, axis=0)
            for part in range(per_block):
                chunk = block * per_block + part
                if chunk < chunks:
                    out_ref[chunk % halves, spot, chunk // halves] = wanted[
                        :, part * width : (part + 1) * width
                    ]


def finish_kernel(pieces_ref, out_ref):
    sources, _, width = pieces_ref.shape
    total = pieces_ref[0]
    for source in range(1, sources):
        total = total + pieces_ref[source]
    high = total.astype(BF16).astype(F32)
    rest = total - high
    middle = rest.astype(BF16).astype(F32)
    parts = jnp.concatenate([high, middle, rest - middle], axis=0).astype(BF16)
    row = lax.broadcasted_iota(jnp.int32, (width, width * KR), 0)
    col = lax.broadcasted_iota(jnp.int32, (width, width * KR), 1)
    spread = jnp.where(lax.shift_right_logical(col, 2) == row, 1.0, 0.0).astype(BF16)
    wide = jnp.dot(parts, spread, preferred_element_type=F32)
    count = total.shape[0]
    wide = wide[:count] + wide[count : 2 * count] + wide[2 * count :]
    rank = lax.broadcasted_iota(jnp.int32, wide.shape, 0) & (KR - 1)
    place = lax.broadcasted_iota(jnp.int32, wide.shape, 1) & (KR - 1)
    wide = jnp.where(rank == place, wide, 0.0)
    for slot in range(out_ref.shape[0]):
        out_ref[slot : slot + 1, :] = jnp.sum(
            wide[slot * KR : (slot + 1) * KR], axis=0, keepdims=True
        )


def in_vmem():
    return pl.BlockSpec(memory_space=pltpu.VMEM)


def anywhere():
    return pl.BlockSpec(memory_space=pl.ANY)


def in_smem():
    return pl.BlockSpec(memory_space=pltpu.SMEM)


def per_device(
    hidden_in,
    query_grad,
    value_grad,
    query_down,
    query_up,
    value_down,
    value_up,
    lengths,
    owners,
    proj_seed,
    offsets,
):
    count, rows, in_cols = hidden_in.shape
    q_cols = query_grad.shape[2]
    v_cols = value_grad.shape[2]
    shards = lax.axis_size("fsdp")
    spots = lax.axis_size("dp")
    halves = lax.axis_size("rep")
    side, hidden, query, value = pl.pallas_call(
        side_kernel,
        out_shape=(
            pltpu.VMEM((4 * KR, count * rows), F32),
            pltpu.VMEM(hidden_in.shape, BF16),
            pltpu.VMEM(query_grad.shape, BF16),
            pltpu.VMEM(value_grad.shape, BF16),
        ),
        in_specs=[anywhere()] * 10,
        out_specs=[in_vmem()] * 4,
        scratch_shapes=[
            pltpu.VMEM(query_down.shape, BF16),
            pltpu.VMEM(query_up.shape, BF16),
            pltpu.VMEM(value_down.shape, BF16),
            pltpu.VMEM(value_up.shape, BF16),
            pltpu.SMEM(lengths.shape, jnp.int32),
            pltpu.SMEM(proj_seed.shape, jnp.int32),
            pltpu.SMEM(offsets.shape, jnp.int32),
            pltpu.SemaphoreType.DMA((3, count, rows // BLOCK)),
            pltpu.SemaphoreType.DMA((4,)),
            pltpu.SemaphoreType.DMA((3,)),
        ],
        compiler_params=pltpu.CompilerParams(vmem_limit_bytes=24 * 2**20),
        name="sides",
    )(
        hidden_in,
        query_grad,
        value_grad,
        query_down,
        query_up,
        value_down,
        value_up,
        lengths,
        proj_seed,
        offsets,
    )

    def make_tables(which, sizes, after):
        return pl.pallas_call(
            functools.partial(table_kernel, 32, which),
            out_shape=[pltpu.VMEM((size, KP), BF16) for size in sizes],
            in_specs=[in_smem(), in_smem(), in_vmem()],
            out_specs=[in_vmem()] * len(sizes),
            compiler_params=pltpu.CompilerParams(vmem_limit_bytes=16 * 2**20),
            name="tables",
        )(proj_seed, offsets, after)

    hop = 1
    stages = [side]
    while hop < shards:
        pairs = [(i, i ^ hop) for i in range(shards)]
        stages.append(stages[-1] + lax.ppermute(stages[-1], "fsdp", pairs))
        hop *= 2
    (wide_in,) = make_tables((0,), (in_cols,), stages[0])
    wide_query, wide_value = make_tables((1, 2), (q_cols, v_cols), stages[1])
    examples = owners.shape[0]
    slots = examples // spots
    width = 4 * KP // (shards * halves)
    pieces = pl.pallas_call(
        feature_kernel,
        out_shape=pltpu.VMEM((halves, spots, shards, slots * KR, width), F32),
        in_specs=[in_vmem()] * 7 + [anywhere()],
        out_specs=in_vmem(),
        scratch_shapes=[pltpu.SMEM(owners.shape, jnp.int32), pltpu.SemaphoreType.DMA],
        compiler_params=pltpu.CompilerParams(vmem_limit_bytes=16 * 2**20),
        name="features",
    )(stages[-1], hidden, query, value, wide_in, wide_query, wide_value, owners)
    half = lax.axis_index("rep")
    kept = lax.dynamic_index_in_dim(pieces, half, 0, keepdims=False)
    sent = lax.dynamic_index_in_dim(pieces, 1 - half, 0, keepdims=False)
    both = kept + lax.ppermute(sent, "rep", [(0, 1), (1, 0)])
    parts = both.reshape(spots * shards, slots * KR, width)
    parts = lax.all_to_all(parts, ("dp", "fsdp"), 0, 0)
    return pl.pallas_call(
        finish_kernel,
        out_shape=jax.ShapeDtypeStruct((slots, width * KR), F32),
        in_specs=[in_vmem()],
        out_specs=in_vmem(),
        compiler_params=pltpu.CompilerParams(vmem_limit_bytes=16 * 2**20),
        name="finish",
    )(parts)


def solution(mesh):
    placed = (
        P(("groups", "dp"), "rep", "fsdp"),
        P(("groups", "dp"), "rep", "fsdp"),
        P(("groups", "dp"), "rep", "fsdp"),
        P("fsdp", None),
        P(None, "fsdp"),
        P("fsdp", None),
        P(None, "fsdp"),
        P(("groups", "dp")),
        P("groups"),
        P(),
        P(),
    )
    return jax.shard_map(
        per_device,
        mesh=mesh,
        in_specs=placed,
        out_specs=P(("groups", "dp"), ("fsdp", "rep")),
        check_vma=False,
    )
```

time: 176 us -> 66 us (0.38)
  waiting for transfers between devices: 83.1 us -> 5.31 us
  matrix products: 45 us -> 0 us
  Pallas kernels: 0 us -> 15.4 us
  between operations: 15.1 us -> 0.79 us
  other arithmetic: 12.9 us -> 0.05 us
  local copies, waits for them, and re-layouts: 11.3 us -> 23.3 us
  blocking collectives: 8.14 us -> 16.1 us
  starting transfers between devices: 0.04 us -> 5.51 us
    unnamed x3 -> x0, waiting for transfers between devices: 47.9 us -> none
    dot_general x21 -> x0, matrix products: 45 us -> none  [the longest x2 13.5 us: per_device(): jnp.dot(qgrad, query_weights, preferred_element_type=jnp.float32)]
    psum x1 -> x0, waiting for transfers between devices: 35.3 us -> none  [per_device(): sides = lax.psum(projected_rank, 'fsdp')]
    unnamed x31 -> x26, local copies, waits for them, and re-layouts: 6.96 us -> 23.3 us
    all_to_all x0 -> x1, blocking collectives: none -> 16.1 us  [per_device(): parts = lax.all_to_all(parts, ('dp', 'fsdp'), 0, 0)]
    pallas_call x0 -> x5, Pallas kernels: none -> 15.4 us  [the longest x1 6.4 us: per_device(): pl.pallas_call(side_kernel, out_shape=(pltpu.VMEM((4 * KR, count * rows),...]
    unnamed x1 -> x0, blocking collectives: 8.14 us -> none
    ppermute x0 -> x3, starting transfers between devices: none -> 5.51 us  [the longest x2 5.43 us: per_device(): stages.append(stages[-1] + lax.ppermute(stages[-1], 'fsdp', pairs))]
  transfers between devices with their start and end apart: 2 -> 3, of which waited for: 2 -> 2; matrix products, arithmetic and copies ran while one was open for 2% -> 0% of each run, Pallas kernels for 0% -> 7%
where the time goes in v1:
time: 66 us; the launch traced here: 66.4 us
  local copies, waits for them, and re-layouts  23.3 us (35%)
  blocking collectives  16.1 us (24%)
  Pallas kernels  15.4 us (23%)
  starting transfers between devices  5.51 us (8%)
  waiting for transfers between devices  5.31 us (8%)
  between operations  0.79 us (1%)
    unnamed x26, local copies, waits for them, and re-layouts  23.3 us
    all_to_all x1, blocking collectives, per_device(): parts = lax.all_to_all(parts, ('dp', 'fsdp'), 0, 0)  16.1 us
    pallas_call x1, Pallas kernels, per_device(): pl.pallas_call(side_kernel, out_shape=(pltpu.VMEM((4 * KR, count * rows),...  6.4 us
    ppermute x2, starting transfers between devices, per_device(): stages.append(stages[-1] + lax.ppermute(stages[-1], 'fsdp', pairs))  5.43 us
    pallas_call x2, Pallas kernels, make_tables(): pl.pallas_call(functools.partial(table_kernel, 32, which), out_shape=[plt...  4.9 us
    ppermute x2, waiting for transfers between devices, per_device(): stages.append(stages[-1] + lax.ppermute(stages[-1], 'fsdp', pairs))  4.07 us
    pallas_call x1, Pallas kernels, per_device(): pl.pallas_call(feature_kernel, out_shape=pltpu.VMEM((halves, spots, shard...  3.3 us
  transfers between devices with their start and end apart: 3, of which 2 were waited for; matrix products, arithmetic and copies ran while one was open for 0% of the time, Pallas kernels for 7%

profile of v1, /device:TPU:0, one launch (start us, length us, event | category | flops | bytes accessed | tf_op | source)
XLA Modules:
  0.0 66.4 jit_solution(18436678299657842612)
XLA Ops:
  0.7 1.2 %copy.12.query_down_hbm = bf16[2048,64]{1,0:T(8,128)(2,1)S(1)} copy(bf16[2048,64]{0,1:T(8,128)(2,1)} %param.14) | data formatting | bytes 524288 | tf_op args[3]
  1.9 1.2 %copy.13.value_down_hbm = bf16[2048,64]{1,0:T(8,128)(2,1)S(1)} copy(bf16[2048,64]{0,1:T(8,128)(2,1)} %param.16) | data formatting | bytes 524288 | tf_op args[5]
  3.1 0.0 copy-start.4
  3.1 3.4 %copy-done.4 = bf16[2,1024,2048]{2,1,0:T(8,128)(2,1)S(1)} copy-done((bf16[2,1024,2048]{2,1,0:T(8,128)(2,1)S(1)}, bf16[2,1024,2048]{2,1,0:T(8,128)(2,1)}, u32[]{:S(2)}) %copy-start.4) | copy-done | bytes 8388632
  6.5 1.2 %copy-done.5 = bf16[2,1024,256]{2,1,0:T(8,128)(2,1)S(1)} copy-done((bf16[2,1024,256]{2,1,0:T(8,128)(2,1)S(1)}, bf16[2,1024,256]{2,1,0:T(8,128)(2,1)}, u32[]{:S(2)}) %copy-start.5) | copy-done | bytes 1048600
  7.7 0.9 %copy-done.6 = bf16[64,2048]{1,0:T(8,128)(2,1)S(1)} copy-done((bf16[64,2048]{1,0:T(8,128)(2,1)S(1)}, bf16[64,2048]{1,0:T(8,128)(2,1)}, u32[]{:S(2)}) %copy-start.6) | copy-done | bytes 262168
  8.7 0.8 %copy-done.7 = bf16[64,256]{1,0:T(8,128)(2,1)S(1)} copy-done((bf16[64,256]{1,0:T(8,128)(2,1)S(1)}, bf16[64,256]{1,0:T(8,128)(2,1)}, u32[]{:S(2)}) %copy-start.7) | copy-done | bytes 32792
  9.4 0.7 copy-done.8
  10.1 0.7 copy-done.11
  10.8 6.4 %sides.1 = (f32[16,2048]{1,0:T(8,128)S(1)}, bf16[2,1024,2048]{2,1,0:T(8,128)(2,1)S(1)}, bf16[2,1024,2048]{2,1,0:T(8,128)(2,1)S(1)}, bf16[2,1024,256]{2,1,0:T(8,128)(2,1)S(1)}) custom-call(bf16[2,1024,2048]{2,1,0:T(8,128)(2,1)S(1)} %copy-done.4, bf16[2,1024,2048]{2,1,0:T(8,128)(2,1)} %query_hbm.1, bf16[2,1024,256]{2,1,0:T(8,128)(2,1)S(1)} %copy-done.5, ...), custom_call_target="tpu_custom_call" | custom-call | tf_op jit(solution)/shard_map/sides/pallas_call | solution.py:333
  17.2 3.2 %copy-done = bf16[2,1024,2048]{2,1,0:T(8,128)(2,1)} copy-done((bf16[2,1024,2048]{2,1,0:T(8,128)(2,1)}, bf16[2,1024,2048]{2,1,0:T(8,128)(2,1)S(1)}, u32[]{:S(2)}) %copy-start) | copy-done | bytes 8388632
  20.4 3.2 %copy-done.2 = bf16[2,1024,2048]{2,1,0:T(8,128)(2,1)} copy-done((bf16[2,1024,2048]{2,1,0:T(8,128)(2,1)}, bf16[2,1024,2048]{2,1,0:T(8,128)(2,1)S(1)}, u32[]{:S(2)}) %copy-start.2) | copy-done | bytes 8388632
  23.6 3.0 %collective-permute-start = (f32[16,2048]{1,0:T(8,128)S(1)}, f32[16,2048]{1,0:T(8,128)S(1)}, u32[]{:S(2)}, u32[]{:S(2)}) collective-permute-start(f32[16,2048]{1,0:T(8,128)S(1)} %get-tuple-element.11._), channel_id=1, source_target_pairs={{0,4},{4,0},{8,12},{12,8},{1,5},{5,1},{9,13},{13,9},{2,6},{6,2},{1... | collective-permute-start | bytes 393224 | tf_op jit(solution)/shard_map/ppermute | solution.py:384
  26.7 4.1 %collective-permute-done = f32[16,2048]{1,0:T(8,128)S(1)} collective-permute-done((f32[16,2048]{1,0:T(8,128)S(1)}, f32[16,2048]{1,0:T(8,128)S(1)}, u32[]{:S(2)}, u32[]{:S(2)}) %collective-permute-start) | collective-permute-done | bytes 131104 | tf_op jit(solution)/shard_map/ppermute | solution.py:384
  30.7 2.4 %collective-permute-start.1 = (f32[16,2048]{1,0:T(8,128)S(1)}, f32[16,2048]{1,0:T(8,128)S(1)}, u32[]{:S(2)}, u32[]{:S(2)}) collective-permute-start(f32[16,2048]{1,0:T(8,128)S(1)} %add.17._), channel_id=1, source_target_pairs={{0,8},{4,12},{8,0},{12,4},{1,9},{5,13},{9,1},{13,5},{2,10},{6,14},... | collective-permute-start | bytes 393224 | tf_op jit(solution)/shard_map/ppermute | solution.py:384
  33.1 2.3 %tables.2.wide_in = bf16[2048,512]{1,0:T(8,128)(2,1)S(1)} custom-call(s32[1]{0:T(128)S(6)} %copy.14.seed_hbm.seed_ref, s32[7]{0:T(128)S(1)} %copy-done.8, f32[16,2048]{1,0:T(8,128)S(1)} %get-tuple-element.11._), custom_call_target="tpu_custom_call" | custom-call | tf_op jit(solution)/shard_map/tables/pallas_call | solution.py:371
  35.5 2.6 %tables.3 = (bf16[2048,512]{1,0:T(8,128)(2,1)S(1)}, bf16[256,512]{1,0:T(8,128)(2,1)S(1)}) custom-call(s32[1]{0:T(128)S(6)} %copy.14.seed_hbm.seed_ref, s32[7]{0:T(128)S(1)} %copy-done.9, f32[16,2048]{1,0:T(8,128)S(1)} %add.17._), custom_call_target="tpu_custom_call" | custom-call | tf_op jit(solution)/shard_map/tables/pallas_call | solution.py:371
  38.1 3.4 %copy-done.1 = bf16[2,1024,2048]{2,1,0:T(8,128)(2,1)S(1)} copy-done((bf16[2,1024,2048]{2,1,0:T(8,128)(2,1)S(1)}, bf16[2,1024,2048]{2,1,0:T(8,128)(2,1)}, u32[]{:S(2)}) %copy-start.1) | copy-done | bytes 8388632
  41.5 3.4 %copy-done.3 = bf16[2,1024,2048]{2,1,0:T(8,128)(2,1)S(1)} copy-done((bf16[2,1024,2048]{2,1,0:T(8,128)(2,1)S(1)}, bf16[2,1024,2048]{2,1,0:T(8,128)(2,1)}, u32[]{:S(2)}) %copy-start.3) | copy-done | bytes 8388632
  44.9 3.3 %features.1 = f32[2,2,4,8,256]{4,3,2,1,0:T(8,128)S(1)} custom-call(f32[16,2048]{1,0:T(8,128)S(1)} %add.18.side_ref, bf16[2,1024,2048]{2,1,0:T(8,128)(2,1)S(1)} %copy-done.1, bf16[2,1024,2048]{2,1,0:T(8,128)(2,1)S(1)} %copy-done.3, bf16[2,1024,256]{2,1,0:T(8,128)(2,1)S(1)} %get-tuple-element.14.value_ref, bf16[2048,512]{1,0:T(8,128)(2,1)S(1)} %tables.2.wide_in, ...), custom_call_target="tpu_custom_call" | custom-call | tf_op jit(solution)/shard_map/features/pallas_call | solution.py:391
  48.2 0.1 collective-permute-start.2
  48.3 1.2 %collective-permute-done.2 = f32[2,4,8,256]{3,2,1,0:T(8,128)S(1)} collective-permute-done((f32[2,4,8,256]{3,2,1,0:T(8,128)S(1)}, f32[2,4,8,256]{3,2,1,0:T(8,128)S(1)}, u32[]{:S(2)}, u32[]{:S(2)}) %collective-permute-start.2) | collective-permute-done | bytes 65568 | tf_op jit(solution)/shard_map/ppermute | solution.py:403
  49.5 16.1 %all_to_all.5.pieces_ref = f32[8,8,256]{2,1,0:T(8,128)S(1)} all-to-all(f32[8,8,256]{2,1,0:T(8,128)S(1)} %bitcast.5), channel_id=1, replica_groups=mesh['groups'=2,'fsdp'=4,'dp'=2,'rep'=2] {'dp','fsdp'}, dimensions={0} | all-to-all | bytes 131072 | tf_op jit(solution)/shard_map/all_to_all | solution.py:405
  65.6 0.8 %finish.1 = f32[2,1024]{1,0:T(2,128)} custom-call(f32[8,8,256]{2,1,0:T(8,128)S(1)} %all_to_all.5.pieces_ref), custom_call_target="tpu_custom_call" | custom-call | tf_op jit(solution)/shard_map/finish/pallas_call | solution.py:406
  (18 shorter events, 0.1 us)
Async XLA Ops:
  3.1 3.4 %copy-start.4 = (bf16[2,1024,2048]{2,1,0:T(8,128)(2,1)S(1)}, bf16[2,1024,2048]{2,1,0:T(8,128)(2,1)}, u32[]{:S(2)}) copy-start(bf16[2,1024,2048]{2,1,0:T(8,128)(2,1)} %hidden_hbm.1) | copy-start | bytes 25165828
  6.5 1.2 %copy-start.5 = (bf16[2,1024,256]{2,1,0:T(8,128)(2,1)S(1)}, bf16[2,1024,256]{2,1,0:T(8,128)(2,1)}, u32[]{:S(2)}) copy-start(bf16[2,1024,256]{2,1,0:T(8,128)(2,1)} %value_hbm.1) | copy-start | bytes 3145732
  7.7 0.9 %copy-start.6 = (bf16[64,2048]{1,0:T(8,128)(2,1)S(1)}, bf16[64,2048]{1,0:T(8,128)(2,1)}, u32[]{:S(2)}) copy-start(bf16[64,2048]{1,0:T(8,128)(2,1)} %query_up_hbm.1) | copy-start | bytes 786436
  8.7 0.8 %copy-start.7 = (bf16[64,256]{1,0:T(8,128)(2,1)S(1)}, bf16[64,256]{1,0:T(8,128)(2,1)}, u32[]{:S(2)}) copy-start(bf16[64,256]{1,0:T(8,128)(2,1)} %value_up_hbm.1) | copy-start | bytes 98308
  9.4 0.7 copy-start.8
  10.1 0.7 copy-start.11
  10.7 24.7 %copy-start.9 = (s32[7]{0:T(128)S(1)}, s32[7]{0:T(128)}, u32[]{:S(2)}) copy-start(s32[7]{0:T(128)} %offsets_ref.3) | copy-start | bytes 88
  10.7 27.4 %copy-start.10 = (s32[4]{0:T(128)S(1)}, s32[4]{0:T(128)}, u32[]{:S(2)}) copy-start(s32[4]{0:T(128)} %owners_hbm.1) | copy-start | bytes 52
  17.2 3.2 %copy-start = (bf16[2,1024,2048]{2,1,0:T(8,128)(2,1)}, bf16[2,1024,2048]{2,1,0:T(8,128)(2,1)S(1)}, u32[]{:S(2)}) copy-start(bf16[2,1024,2048]{2,1,0:T(8,128)(2,1)S(1)} %get-tuple-element.12.hidden_ref) | copy-start | bytes 25165828
  20.4 3.2 %copy-start.2 = (bf16[2,1024,2048]{2,1,0:T(8,128)(2,1)}, bf16[2,1024,2048]{2,1,0:T(8,128)(2,1)S(1)}, u32[]{:S(2)}) copy-start(bf16[2,1024,2048]{2,1,0:T(8,128)(2,1)S(1)} %get-tuple-element.13.query_ref) | copy-start | bytes 25165828
  23.6 7.1 %collective-permute-start = (f32[16,2048]{1,0:T(8,128)S(1)}, f32[16,2048]{1,0:T(8,128)S(1)}, u32[]{:S(2)}, u32[]{:S(2)}) collective-permute-start(f32[16,2048]{1,0:T(8,128)S(1)} %get-tuple-element.11._), channel_id=1, source_target_pairs={{0,4},{4,0},{8,12},{12,8},{1,5},{5,1},{9,13},{13,9},{2,6},{6,2},{1... | collective-permute-start | bytes 393224 | tf_op jit(solution)/shard_map/ppermute | solution.py:384
  30.7 7.3 %collective-permute-start.1 = (f32[16,2048]{1,0:T(8,128)S(1)}, f32[16,2048]{1,0:T(8,128)S(1)}, u32[]{:S(2)}, u32[]{:S(2)}) collective-permute-start(f32[16,2048]{1,0:T(8,128)S(1)} %add.17._), channel_id=1, source_target_pairs={{0,8},{4,12},{8,0},{12,4},{1,9},{5,13},{9,1},{13,5},{2,10},{6,14},... | collective-permute-start | bytes 393224 | tf_op jit(solution)/shard_map/ppermute | solution.py:384
  38.1 3.4 %copy-start.1 = (bf16[2,1024,2048]{2,1,0:T(8,128)(2,1)S(1)}, bf16[2,1024,2048]{2,1,0:T(8,128)(2,1)}, u32[]{:S(2)}) copy-start(bf16[2,1024,2048]{2,1,0:T(8,128)(2,1)} %copy-done) | copy-start | bytes 25165828
  41.5 3.4 %copy-start.3 = (bf16[2,1024,2048]{2,1,0:T(8,128)(2,1)S(1)}, bf16[2,1024,2048]{2,1,0:T(8,128)(2,1)}, u32[]{:S(2)}) copy-start(bf16[2,1024,2048]{2,1,0:T(8,128)(2,1)} %copy-done.2) | copy-start | bytes 25165828
  48.2 1.3 %collective-permute-start.2 = (f32[2,4,8,256]{3,2,1,0:T(8,128)S(1)}, f32[2,4,8,256]{3,2,1,0:T(8,128)S(1)}, u32[]{:S(2)}, u32[]{:S(2)}) collective-permute-start(f32[2,4,8,256]{3,2,1,0:T(8,128)S(1)} %dynamic-slice_bitcast_fusion), channel_id=1, source_target_pairs={{0,1},{1,0},{2,3},{3,2},{4,5},{5,4},{6,7},{7,6},{8,9},{9,8},{10,11... | collective-permute-start | bytes 196616 | tf_op jit(solution)/shard_map/ppermute | solution.py:403

commit v2 on v1

--- a/solution.py
+++ b/solution.py
@@ -19,7 +19,6 @@
 COUNT_MUL = -1640531535
 BF16 = jnp.bfloat16
 F32 = jnp.float32
-SCALARS = 24
 
 
 def mix_bits(values):
@@ -67,7 +66,9 @@
     lengths_hbm,
     seed_hbm,
     offsets_hbm,
+    owners_hbm,
     side_ref,
+    scalar_ref,
     hidden_ref,
     query_ref,
     value_ref,
@@ -78,6 +79,7 @@
     lengths,
     seed,
     offsets,
+    owners,
     block_sem,
     factor_sem,
     scalar_sem,
@@ -88,7 +90,12 @@
     scalars = [
         pltpu.make_async_copy(src, dst, scalar_sem.at[k])
         for k, (src, dst) in enumerate(
-            ((lengths_hbm, lengths), (seed_hbm, seed), (offsets_hbm, offsets))
+            (
+                (lengths_hbm, lengths),
+                (seed_hbm, seed),
+                (offsets_hbm, offsets),
+                (owners_hbm, owners),
+            )
         )
     ]
     factors = [
@@ -131,20 +138,20 @@
     for copy in scalars[1:] + factors:
         copy.wait()
     seed_value = seed[0]
-
-    def up_map(factor, k, first):
+    first = lax.axis_index("dp") * count
+    kept = [seed_value * SEED_MUL]
+    kept += [offsets[k] for k in range(3)]
+    kept += [owners[first + item] for item in range(count)]
+    for k, scalar in enumerate(kept):
+        scalar_ref[k : k + 1, :] = jnp.full((1, scalar_ref.shape[1]), scalar, jnp.int32)
+
+    def folded(factor, k, first):
         table = rank_rows(seed_value, offsets[3 + k], first)
         return jnp.dot(table, factor[...], preferred_element_type=F32)
 
-    def down_map(factor, k, first):
-        table = rank_rows(seed_value, offsets[3 + k], first)
-        return lax.dot_general(
-            table, factor[...], (((1,), (1,)), ((), ())), preferred_element_type=F32
-        )
-
-    from_query = split_rows(up_map(query_up, 0, 0))
-    from_value = split_rows(up_map(value_up, 1, KR))
-    from_hidden = split_rows(down_map(query_down, 2, 0) + down_map(value_down, 3, KR))
+    from_query = split_rows(folded(query_up, 0, 0))
+    from_value = split_rows(folded(value_up, 1, KR))
+    from_hidden = split_rows(folded(query_down, 2, 0) + folded(value_down, 3, KR))
 
     def project(weights, data):
         product = lax.dot_general(
@@ -193,14 +200,14 @@
     each_block(lower)
 
 
-def table_kernel(step_rows, tables, seed_ref, offsets_ref, _, *outs):
+def table_kernel(step_rows, tables, scalar_ref, *outs):
     shard = lax.axis_index("fsdp")
-    seed_term = seed_ref[0] * SEED_MUL
+    seed_term = scalar_ref[0:1, 0:1]
     for k, out in zip(tables, outs):
         rows = out.shape[0]
         row = lax.broadcasted_iota(jnp.int32, (step_rows, KP), 0)
         col = lax.broadcasted_iota(jnp.int32, (step_rows, KP), 1)
-        counter = offsets_ref[k] + (row + shard * rows) * KP + col
+        counter = scalar_ref[1 + k : 2 + k, 0:1] + (row + shard * rows) * KP + col
         first = counter * COUNT_MUL + seed_term
         stride = wrapped(step_rows * KP * COUNT_MUL)
 
@@ -220,13 +227,9 @@
     wide_in,
     wide_query,
     wide_value,
-    owners_hbm,
+    scalar_ref,
     out_ref,
-    owners,
-    owner_sem,
 ):
-    fetch = pltpu.make_async_copy(owners_hbm, owners, owner_sem)
-    fetch.start()
     count, rows, _ = hidden_ref.shape
     half = 2 * KR
 
@@ -248,9 +251,7 @@
     value = widened(gathered(value_ref, half), wide_value) * (side_scale * (DV / 3.0) ** (-0.5))
     group = lax.rem(lax.broadcasted_iota(jnp.int32, query.shape, 0), half)
     lower = jnp.where(group < KR, query, value)
-    fetch.wait()
-    first = lax.axis_index("dp") * count
-    targets = [owners[first + item] for item in range(count)]
+    targets = [scalar_ref[4 + item : 5 + item, 0:1] for item in range(count)]
     halves, spots, pieces, slot_rows, width = out_ref.shape
     slots = slot_rows // KR
     chunks = halves * pieces
@@ -303,12 +304,8 @@
     return pl.BlockSpec(memory_space=pltpu.VMEM)
 
 
-def anywhere():
-    return pl.BlockSpec(memory_space=pl.ANY)
-
-
-def in_smem():
-    return pl.BlockSpec(memory_space=pltpu.SMEM)
+def in_hbm():
+    return pl.BlockSpec(memory_space=pltpu.HBM)
 
 
 def per_device(
@@ -330,73 +327,76 @@
     shards = lax.axis_size("fsdp")
     spots = lax.axis_size("dp")
     halves = lax.axis_size("rep")
-    side, hidden, query, value = pl.pallas_call(
+    side, scalars, hidden, query, value = pl.pallas_call(
         side_kernel,
         out_shape=(
             pltpu.VMEM((4 * KR, count * rows), F32),
+            pltpu.VMEM((8, 128), jnp.int32),
             pltpu.VMEM(hidden_in.shape, BF16),
             pltpu.VMEM(query_grad.shape, BF16),
             pltpu.VMEM(value_grad.shape, BF16),
         ),
-        in_specs=[anywhere()] * 10,
-        out_specs=[in_vmem()] * 4,
+        in_specs=[in_hbm()] * 11,
+        out_specs=[in_vmem()] * 5,
         scratch_shapes=[
-            pltpu.VMEM(query_down.shape, BF16),
+            pltpu.VMEM(query_down.shape[::-1], BF16),
             pltpu.VMEM(query_up.shape, BF16),
-            pltpu.VMEM(value_down.shape, BF16),
+            pltpu.VMEM(value_down.shape[::-1], BF16),
             pltpu.VMEM(value_up.shape, BF16),
             pltpu.SMEM(lengths.shape, jnp.int32),
             pltpu.SMEM(proj_seed.shape, jnp.int32),
             pltpu.SMEM(offsets.shape, jnp.int32),
+            pltpu.SMEM(owners.shape, jnp.int32),
             pltpu.SemaphoreType.DMA((3, count, rows // BLOCK)),
             pltpu.SemaphoreType.DMA((4,)),
-            pltpu.SemaphoreType.DMA((3,)),
+            pltpu.SemaphoreType.DMA((4,)),
         ],
-        compiler_params=pltpu.CompilerParams(vmem_limit_bytes=24 * 2**20),
+        compiler_params=pltpu.CompilerParams(vmem_limit_bytes=42 * 2**20),
         name="sides",
     )(
         hidden_in,
         query_grad,
         value_grad,
-        query_down,
+        query_down.T,
         query_up,
-        value_down,
+        value_down.T,
         value_up,
         lengths,
         proj_seed,
         offsets,
+        owners,
     )
 
-    def make_tables(which, sizes, after):
+    def make_tables(which, sizes):
         return pl.pallas_call(
             functools.partial(table_kernel, 32, which),
             out_shape=[pltpu.VMEM((size, KP), BF16) for size in sizes],
-            in_specs=[in_smem(), in_smem(), in_vmem()],
+            in_specs=[in_vmem()],
             out_specs=[in_vmem()] * len(sizes),
             compiler_params=pltpu.CompilerParams(vmem_limit_bytes=16 * 2**20),
             name="tables",
-        )(proj_seed, offsets, after)
-
+        )(scalars)
+
+    (wide_in,) = make_tables((0,), (in_cols,))
     hop = 1
-    stages = [side]
     while hop < shards:
         pairs = [(i, i ^ hop) for i in range(shards)]
-        stages.append(stages[-1] + lax.ppermute(stages[-1], "fsdp", pairs))
+        side = side + lax.ppermute(side, "fsdp", pairs)
+        if hop == 1:
+            side, wide_in = lax.optimization_barrier((side, wide_in))
         hop *= 2
-    (wide_in,) = make_tables((0,), (in_cols,), stages[0])
-    wide_query, wide_value = make_tables((1, 2), (q_cols, v_cols), stages[1])
+    wide_query, wide_value = make_tables((1, 2), (q_cols, v_cols))
     examples = owners.shape[0]
     slots = examples // spots
     width = 4 * KP // (shards * halves)
     pieces = pl.pallas_call(
         feature_kernel,
         out_shape=pltpu.VMEM((halves, spots, shards, slots * KR, width), F32),
-        in_specs=[in_vmem()] * 7 + [anywhere()],
+        in_specs=[in_vmem()] * 8,
         out_specs=in_vmem(),
-        scratch_shapes=[pltpu.SMEM(owners.shape, jnp.int32), pltpu.SemaphoreType.DMA],
         compiler_params=pltpu.CompilerParams(vmem_limit_bytes=16 * 2**20),
         name="features",
-    )(stages[-1], hidden, query, value, wide_in, wide_query, wide_value, owners)
+    )(side, hidden, query, value, wide_in, wide_query, wide_value, scalars)
     half = lax.axis_index("rep")
     kept = lax.dynamic_index_in_dim(pieces, half, 0, keepdims=False)
     sent = lax.dynamic_index_in_dim(pieces, 1 - half, 0, keepdims=False)

time: 66 us -> 59.7 us (0.905)
  local copies, waits for them, and re-layouts: 23.3 us -> 16.1 us
  Pallas kernels: 15.4 us -> 17.1 us
  waiting for transfers between devices: 5.31 us -> 3.76 us
  blocking collectives: 16.1 us -> 15.1 us
  other arithmetic: 0.05 us -> 0.94 us
    unnamed x26 -> x12, local copies, waits for them, and re-layouts: 23.3 us -> 16.1 us
    pallas_call x1, Pallas kernels: 6.4 us -> 9.2 us  [per_device(): pl.pallas_call(side_kernel, out_shape=(pltpu.VMEM((4 * KR, count * rows),...]
    ppermute x2, waiting for transfers between devices: 4.07 us -> 2.52 us  [per_device(): side = side + lax.ppermute(side, 'fsdp', pairs)]
    all_to_all x1, blocking collectives: 16.1 us -> 15.1 us  [per_device(): parts = lax.all_to_all(parts, ('dp', 'fsdp'), 0, 0)]
    pallas_call x2, Pallas kernels: 4.9 us -> 3.89 us  [make_tables(): pl.pallas_call(functools.partial(table_kernel, 32, which), out_shape=[plt...]
    add x2, other arithmetic: 0.04 us -> 0.93 us  [per_device(): side = side + lax.ppermute(side, 'fsdp', pairs)]
  transfers between devices with their start and end apart: 3 -> 3, of which waited for: 2 -> 3; matrix products, arithmetic and copies ran while one was open for 0% -> 0% of each run, Pallas kernels for 7% -> 7%
where the time goes in v2:
time: 59.7 us; the launch traced here: 59.8 us
  Pallas kernels  17.1 us (29%)
  local copies, waits for them, and re-layouts  16.1 us (27%)
  blocking collectives  15.1 us (25%)
  starting transfers between devices  5.95 us (10%)
  waiting for transfers between devices  3.76 us (6%)
  other arithmetic  0.94 us (2%)
  between operations  0.74 us (1%)
    unnamed x12, local copies, waits for them, and re-layouts  16.1 us
    all_to_all x1, blocking collectives, per_device(): parts = lax.all_to_all(parts, ('dp', 'fsdp'), 0, 0)  15.1 us
    pallas_call x1, Pallas kernels, per_device(): pl.pallas_call(side_kernel, out_shape=(pltpu.VMEM((4 * KR, count * rows),...  9.2 us
    ppermute x2, starting transfers between devices, per_device(): side = side + lax.ppermute(side, 'fsdp', pairs)  5.88 us
    pallas_call x2, Pallas kernels, make_tables(): pl.pallas_call(functools.partial(table_kernel, 32, which), out_shape=[plt...  3.89 us
    pallas_call x1, Pallas kernels, per_device(): pl.pallas_call(feature_kernel, out_shape=pltpu.VMEM((halves, spots, shard...  3.25 us
    ppermute x2, waiting for transfers between devices, per_device(): side = side + lax.ppermute(side, 'fsdp', pairs)  2.52 us
    ppermute x1, waiting for transfers between devices, per_device(): both = kept + lax.ppermute(sent, 'rep', [(0, 1), (1, 0)])  1.24 us
  transfers between devices with their start and end apart: 3, of which 3 were waited for; matrix products, arithmetic and copies ran while one was open for 0% of the time, Pallas kernels for 7%

profile of v2, /device:TPU:0, one launch (start us, length us, event | category | flops | bytes accessed | tf_op | source)
XLA Modules:
  0.0 59.8 jit_solution(799113571659789346)
XLA Ops:
  0.7 9.2 %sides.1 = (f32[16,2048]{1,0:T(8,128)S(1)}, s32[8,128]{1,0:T(8,128)S(1)}, bf16[2,1024,2048]{2,1,0:T(8,128)(2,1)S(1)}, bf16[2,1024,2048]{2,1,0:T(8,128)(2,1)S(1)}, bf16[2,1024,256]{2,1,0:T(8,128)(2,1)S(1)}) custom-call(bf16[2,1024,2048]{2,1,0:T(8,128)(2,1)} %hidden_hbm.1, bf16[2,1024,2048]{2,1,0:T(8,128)(2,1)} %query_hbm.1, bf16[2,1024,256]{2,1,0:T(8,128)(2,1)} %value_hbm.1, ...), custom_call_target="tpu_custom_call" | custom-call | tf_op jit(solution)/shard_map/sides/pallas_call | solution.py:330
  9.9 0.0 copy-start
  9.9 3.2 %copy-done = bf16[2,1024,2048]{2,1,0:T(8,128)(2,1)} copy-done((bf16[2,1024,2048]{2,1,0:T(8,128)(2,1)}, bf16[2,1024,2048]{2,1,0:T(8,128)(2,1)S(1)}, u32[]{:S(2)}) %copy-start) | copy-done | bytes 8388632
  13.1 0.0 copy-start.2
  13.1 3.2 %copy-done.2 = bf16[2,1024,2048]{2,1,0:T(8,128)(2,1)} copy-done((bf16[2,1024,2048]{2,1,0:T(8,128)(2,1)}, bf16[2,1024,2048]{2,1,0:T(8,128)(2,1)S(1)}, u32[]{:S(2)}) %copy-start.2) | copy-done | bytes 8388632
  16.3 3.0 %collective-permute-start = (f32[16,2048]{1,0:T(8,128)S(1)}, f32[16,2048]{1,0:T(8,128)S(1)}, u32[]{:S(2)}, u32[]{:S(2)}) collective-permute-start(f32[16,2048]{1,0:T(8,128)S(1)} %get-tuple-element.14), channel_id=1, source_target_pairs={{0,4},{4,0},{8,12},{12,8},{1,5},{5,1},{9,13},{13,9},{2,6},{6,2},{1... | collective-permute-start | bytes 393224 | tf_op jit(solution)/shard_map/ppermute | solution.py:384
  19.3 1.8 %tables.2.wide_in = bf16[2048,512]{1,0:T(8,128)(2,1)S(1)} custom-call(s32[8,128]{1,0:T(8,128)S(1)} %get-tuple-element.15.scalar_ref), custom_call_target="tpu_custom_call" | custom-call | tf_op jit(solution)/shard_map/tables/pallas_call | solution.py:371
  21.2 1.4 %collective-permute-done = f32[16,2048]{1,0:T(8,128)S(1)} collective-permute-done((f32[16,2048]{1,0:T(8,128)S(1)}, f32[16,2048]{1,0:T(8,128)S(1)}, u32[]{:S(2)}, u32[]{:S(2)}) %collective-permute-start) | collective-permute-done | bytes 131104 | tf_op jit(solution)/shard_map/ppermute | solution.py:384
  22.6 2.9 %collective-permute-start.1 = (f32[16,2048]{1,0:T(8,128)S(1)}, f32[16,2048]{1,0:T(8,128)}, u32[]{:S(2)}, u32[]{:S(2)}) collective-permute-start(f32[16,2048]{1,0:T(8,128)S(1)} %add.17), channel_id=1, source_target_pairs={{0,8},{4,12},{8,0},{12,4},{1,9},{5,13},{9,1},{13,5},{2,10},{6,14},... | collective-permute-start | bytes 393224 | tf_op jit(solution)/shard_map/ppermute | solution.py:384
  25.4 2.1 %tables.3 = (bf16[2048,512]{1,0:T(8,128)(2,1)S(1)}, bf16[256,512]{1,0:T(8,128)(2,1)S(1)}) custom-call(s32[8,128]{1,0:T(8,128)S(1)} %get-tuple-element.15.scalar_ref), custom_call_target="tpu_custom_call" | custom-call | tf_op jit(solution)/shard_map/tables/pallas_call | solution.py:371
  27.5 0.0 copy-start.4
  27.5 1.3 %copy-done.4 = bf16[2048,512]{1,0:T(8,128)(2,1)} copy-done((bf16[2048,512]{1,0:T(8,128)(2,1)}, bf16[2048,512]{1,0:T(8,128)(2,1)S(1)}, u32[]{:S(2)}) %copy-start.4) | copy-done | bytes 2097176
  28.8 1.2 %collective-permute-done.1 = f32[16,2048]{1,0:T(8,128)} collective-permute-done((f32[16,2048]{1,0:T(8,128)S(1)}, f32[16,2048]{1,0:T(8,128)}, u32[]{:S(2)}, u32[]{:S(2)}) %collective-permute-start.1) | collective-permute-done | bytes 131104 | tf_op jit(solution)/shard_map/ppermute | solution.py:384
  30.0 0.9 %add.18.side_ref = f32[16,2048]{1,0:T(8,128)S(1)} add(f32[16,2048]{1,0:T(8,128)S(1)} %add.17, f32[16,2048]{1,0:T(8,128)} %collective-permute-done.1) | non-fusion elementwise | flops 32768 | bytes 393216 | tf_op jit(solution)/shard_map/add | solution.py:384
  30.9 0.0 copy-start.1
  30.9 3.4 %copy-done.1 = bf16[2,1024,2048]{2,1,0:T(8,128)(2,1)S(1)} copy-done((bf16[2,1024,2048]{2,1,0:T(8,128)(2,1)S(1)}, bf16[2,1024,2048]{2,1,0:T(8,128)(2,1)}, u32[]{:S(2)}) %copy-start.1) | copy-done | bytes 8388632
  34.3 0.0 copy-start.3
  34.3 3.4 %copy-done.3 = bf16[2,1024,2048]{2,1,0:T(8,128)(2,1)S(1)} copy-done((bf16[2,1024,2048]{2,1,0:T(8,128)(2,1)S(1)}, bf16[2,1024,2048]{2,1,0:T(8,128)(2,1)}, u32[]{:S(2)}) %copy-start.3) | copy-done | bytes 8388632
  37.7 1.6 %copy-done.5 = bf16[2048,512]{1,0:T(8,128)(2,1)S(1)} copy-done((bf16[2048,512]{1,0:T(8,128)(2,1)S(1)}, bf16[2048,512]{1,0:T(8,128)(2,1)}, u32[]{:S(2)}) %copy-start.5) | copy-done | bytes 2097176
  39.3 3.3 %features.1 = f32[2,2,4,8,256]{4,3,2,1,0:T(8,128)S(1)} custom-call(f32[16,2048]{1,0:T(8,128)S(1)} %add.18.side_ref, bf16[2,1024,2048]{2,1,0:T(8,128)(2,1)S(1)} %copy-done.1, bf16[2,1024,2048]{2,1,0:T(8,128)(2,1)S(1)} %copy-done.3, bf16[2,1024,256]{2,1,0:T(8,128)(2,1)S(1)} %get-tuple-element.19.value_ref, bf16[2048,512]{1,0:T(8,128)(2,1)S(1)} %tables.2.wide_in, ...), custom_call_target="tpu_custom_call" | custom-call | tf_op jit(solution)/shard_map/features/pallas_call | solution.py:392
  42.6 0.1 collective-permute-start.2
  42.6 1.2 %collective-permute-done.2 = f32[2,4,8,256]{3,2,1,0:T(8,128)S(1)} collective-permute-done((f32[2,4,8,256]{3,2,1,0:T(8,128)S(1)}, f32[2,4,8,256]{3,2,1,0:T(8,128)S(1)}, u32[]{:S(2)}, u32[]{:S(2)}) %collective-permute-start.2) | collective-permute-done | bytes 65568 | tf_op jit(solution)/shard_map/ppermute | solution.py:403
  43.9 15.1 %all_to_all.5.pieces_ref = f32[8,8,256]{2,1,0:T(8,128)S(1)} all-to-all(f32[8,8,256]{2,1,0:T(8,128)S(1)} %bitcast.9), channel_id=1, replica_groups=mesh['groups'=2,'fsdp'=4,'dp'=2,'rep'=2] {'dp','fsdp'}, dimensions={0} | all-to-all | bytes 131072 | tf_op jit(solution)/shard_map/all_to_all | solution.py:405
  59.0 0.8 %finish.1 = f32[2,1024]{1,0:T(2,128)} custom-call(f32[8,8,256]{2,1,0:T(8,128)S(1)} %all_to_all.5.pieces_ref), custom_call_target="tpu_custom_call" | custom-call | tf_op jit(solution)/shard_map/finish/pallas_call | solution.py:406
  (4 shorter events, 0.0 us)
Async XLA Ops:
  9.9 3.2 %copy-start = (bf16[2,1024,2048]{2,1,0:T(8,128)(2,1)}, bf16[2,1024,2048]{2,1,0:T(8,128)(2,1)S(1)}, u32[]{:S(2)}) copy-start(bf16[2,1024,2048]{2,1,0:T(8,128)(2,1)S(1)} %get-tuple-element.17.hidden_ref) | copy-start | bytes 25165828
  13.1 3.2 %copy-start.2 = (bf16[2,1024,2048]{2,1,0:T(8,128)(2,1)}, bf16[2,1024,2048]{2,1,0:T(8,128)(2,1)S(1)}, u32[]{:S(2)}) copy-start(bf16[2,1024,2048]{2,1,0:T(8,128)(2,1)S(1)} %get-tuple-element.18.query_ref) | copy-start | bytes 25165828
  16.3 6.2 %collective-permute-start = (f32[16,2048]{1,0:T(8,128)S(1)}, f32[16,2048]{1,0:T(8,128)S(1)}, u32[]{:S(2)}, u32[]{:S(2)}) collective-permute-start(f32[16,2048]{1,0:T(8,128)S(1)} %get-tuple-element.14), channel_id=1, source_target_pairs={{0,4},{4,0},{8,12},{12,8},{1,5},{5,1},{9,13},{13,9},{2,6},{6,2},{1... | collective-permute-start | bytes 393224 | tf_op jit(solution)/shard_map/ppermute | solution.py:384
  22.6 7.4 %collective-permute-start.1 = (f32[16,2048]{1,0:T(8,128)S(1)}, f32[16,2048]{1,0:T(8,128)}, u32[]{:S(2)}, u32[]{:S(2)}) collective-permute-start(f32[16,2048]{1,0:T(8,128)S(1)} %add.17), channel_id=1, source_target_pairs={{0,8},{4,12},{8,0},{12,4},{1,9},{5,13},{9,1},{13,5},{2,10},{6,14},... | collective-permute-start | bytes 393224 | tf_op jit(solution)/shard_map/ppermute | solution.py:384
  27.5 1.3 %copy-start.4 = (bf16[2048,512]{1,0:T(8,128)(2,1)}, bf16[2048,512]{1,0:T(8,128)(2,1)S(1)}, u32[]{:S(2)}) copy-start(bf16[2048,512]{1,0:T(8,128)(2,1)S(1)} %get-tuple-element.21.wide_query) | copy-start | bytes 6291460
  30.9 3.4 %copy-start.1 = (bf16[2,1024,2048]{2,1,0:T(8,128)(2,1)S(1)}, bf16[2,1024,2048]{2,1,0:T(8,128)(2,1)}, u32[]{:S(2)}) copy-start(bf16[2,1024,2048]{2,1,0:T(8,128)(2,1)} %copy-done) | copy-start | bytes 25165828
  34.3 3.4 %copy-start.3 = (bf16[2,1024,2048]{2,1,0:T(8,128)(2,1)S(1)}, bf16[2,1024,2048]{2,1,0:T(8,128)(2,1)}, u32[]{:S(2)}) copy-start(bf16[2,1024,2048]{2,1,0:T(8,128)(2,1)} %copy-done.2) | copy-start | bytes 25165828
  37.7 1.6 %copy-start.5 = (bf16[2048,512]{1,0:T(8,128)(2,1)S(1)}, bf16[2048,512]{1,0:T(8,128)(2,1)}, u32[]{:S(2)}) copy-start(bf16[2048,512]{1,0:T(8,128)(2,1)} %copy-done.4) | copy-start | bytes 6291460
  42.6 1.3 %collective-permute-start.2 = (f32[2,4,8,256]{3,2,1,0:T(8,128)S(1)}, f32[2,4,8,256]{3,2,1,0:T(8,128)S(1)}, u32[]{:S(2)}, u32[]{:S(2)}) collective-permute-start(f32[2,4,8,256]{3,2,1,0:T(8,128)S(1)} %dynamic-slice_bitcast_fusion), channel_id=1, source_target_pairs={{0,1},{1,0},{2,3},{3,2},{4,5},{5,4},{6,7},{7,6},{8,9},{9,8},{10,11... | collective-permute-start | bytes 196616 | tf_op jit(solution)/shard_map/ppermute | solution.py:403

commit v3 on v2

--- a/solution.py
+++ b/solution.py
@@ -127,13 +127,13 @@
         for k, (src, dst) in enumerate(arrays)
     ]
     scalars[0].wait()
-    for per_array in copies:
-        for item in range(count):
-            for block in range(blocks):
-
-                @pl.when(start + block * BLOCK < lengths[item])
-                def _(copy=per_array[item][block]):
-                    copy.start()
+    for item in range(count):
+        for block in range(blocks):
+
+            @pl.when(start + block * BLOCK < lengths[item])
+            def _(item=item, block=block):
+                for per_array in copies:
+                    per_array[item][block].start()
 
     for copy in scalars[1:] + factors:
         copy.wait()
@@ -159,45 +159,30 @@
         )
         return join_rows(product)
 
-    def each_block(visit):
-        for item in range(count):
-            for block in range(blocks):
-                live = start + block * BLOCK < lengths[item]
-                visit(item, block, pl.ds(block * BLOCK, BLOCK), pl.ds(item * rows + block * BLOCK, BLOCK), live)
-
-    def keep(item, block):
-        position = lax.broadcasted_iota(jnp.int32, (2 * KR, BLOCK), 1)
-        return position + (start + block * BLOCK) < lengths[item]
-
-    def upper(item, block, here, out, live):
-        @pl.when(live)
-        def _():
-            copies[0][item][block].wait()
-            copies[1][item][block].wait()
-            rows_ = project(from_query, query_ref[item, here, :])
-            rows_ = rows_ + project(from_value, value_ref[item, here, :])
-            side_ref[: 2 * KR, out] = jnp.where(keep(item, block), rows_, 0.0)
-
-        @pl.when(jnp.logical_not(live))
-        def _():
-            side_ref[: 2 * KR, out] = jnp.zeros((2 * KR, BLOCK), F32)
-            query_ref[item, here, :] = jnp.zeros((BLOCK, query_ref.shape[2]), BF16)
-            value_ref[item, here, :] = jnp.zeros((BLOCK, value_ref.shape[2]), BF16)
-
-    def lower(item, block, here, out, live):
-        @pl.when(live)
-        def _():
-            copies[2][item][block].wait()
-            rows_ = project(from_hidden, hidden_ref[item, here, :])
-            side_ref[2 * KR :, out] = jnp.where(keep(item, block), rows_, 0.0)
-
-        @pl.when(jnp.logical_not(live))
-        def _():
-            side_ref[2 * KR :, out] = jnp.zeros((2 * KR, BLOCK), F32)
-            hidden_ref[item, here, :] = jnp.zeros((BLOCK, hidden_ref.shape[2]), BF16)
-
-    each_block(upper)
-    each_block(lower)
+    for item in range(count):
+        for block in range(blocks):
+            first = start + block * BLOCK
+            live = first < lengths[item]
+            here = pl.ds(block * BLOCK, BLOCK)
+            out = pl.ds(item * rows + block * BLOCK, BLOCK)
+
+            @pl.when(live)
+            def _(item=item, block=block, first=first, here=here, out=out):
+                for per_array in copies:
+                    per_array[item][block].wait()
+                upper = project(from_query, query_ref[item, here, :])
+                upper = upper + project(from_value, value_ref[item, here, :])
+                lower = project(from_hidden, hidden_ref[item, here, :])
+                position = first + lax.broadcasted_iota(jnp.int32, (2 * KR, BLOCK), 1)
+                keep = position < lengths[item]
+                side_ref[: 2 * KR, out] = jnp.where(keep, upper, 0.0)
+                side_ref[2 * KR :, out] = jnp.where(keep, lower, 0.0)
+
+            @pl.when(jnp.logical_not(live))
+            def _(item=item, here=here, out=out):
+                side_ref[:, out] = jnp.zeros((4 * KR, BLOCK), F32)
+                for ref in (query_ref, value_ref, hidden_ref):
+                    ref[item, here, :] = jnp.zeros((BLOCK, ref.shape[2]), BF16)
 
 
 def table_kernel(step_rows, tables, scalar_ref, *outs):
@@ -228,7 +213,8 @@
     wide_query,
     wide_value,
     scalar_ref,
-    out_ref,
+    kept_ref,
+    sent_ref,
 ):
     count, rows, _ = hidden_ref.shape
     half = 2 * KR
@@ -252,9 +238,9 @@
     group = lax.rem(lax.broadcasted_iota(jnp.int32, query.shape, 0), half)
     lower = jnp.where(group < KR, query, value)
     targets = [scalar_ref[4 + item : 5 + item, 0:1] for item in range(count)]
-    halves, spots, pieces, slot_rows, width = out_ref.shape
+    spots, pieces, slot_rows, width = kept_ref.shape
     slots = slot_rows // KR
-    chunks = halves * pieces
+    first_half = lax.axis_index("rep") == 0
     per_block = KP // width
     zero = jnp.zeros((KR, KP), F32)
     for spot in range(spots):
@@ -268,12 +254,11 @@
                     total = total + jnp.where(targets[item] == spot * slots + slot, rows_, 0.0)
                 wanted.append(total)
             wanted = jnp.concatenate(wanted, axis=0)
-            for part in range(per_block):
-                chunk = block * per_block + part
-                if chunk < chunks:
-                    out_ref[chunk % halves, spot, chunk // halves] = wanted[
-                        :, part * width : (part + 1) * width
-                    ]
+            for chunk in range(block * per_block, (block + 1) * per_block, 2):
+                at = (chunk % per_block) * width
+                even, odd = wanted[:, at : at + width], wanted[:, at + width : at + 2 * width]
+                kept_ref[spot, chunk // 2] = jnp.where(first_half, even, odd)
+                sent_ref[spot, chunk // 2] = jnp.where(first_half, odd, even)
 
 
 def finish_kernel(pieces_ref, out_ref):
@@ -326,7 +311,6 @@
     v_cols = value_grad.shape[2]
     shards = lax.axis_size("fsdp")
     spots = lax.axis_size("dp")
-    halves = lax.axis_size("rep")
     side, scalars, hidden, query, value = pl.pallas_call(
         side_kernel,
         out_shape=(
@@ -388,18 +372,15 @@
     wide_query, wide_value = make_tables((1, 2), (q_cols, v_cols))
     examples = owners.shape[0]
     slots = examples // spots
-    width = 4 * KP // (shards * halves)
-    pieces = pl.pallas_call(
+    width = 4 * KP // (2 * shards)
+    kept, sent = pl.pallas_call(
         feature_kernel,
-        out_shape=pltpu.VMEM((halves, spots, shards, slots * KR, width), F32),
+        out_shape=[pltpu.VMEM((spots, shards, slots * KR, width), F32)] * 2,
         in_specs=[in_vmem()] * 8,
-        out_specs=in_vmem(),
+        out_specs=[in_vmem()] * 2,
         compiler_params=pltpu.CompilerParams(vmem_limit_bytes=16 * 2**20),
         name="features",
     )(side, hidden, query, value, wide_in, wide_query, wide_value, scalars)
-    half = lax.axis_index("rep")
-    kept = lax.dynamic_index_in_dim(pieces, half, 0, keepdims=False)
-    sent = lax.dynamic_index_in_dim(pieces, 1 - half, 0, keepdims=False)
     both = kept + lax.ppermute(sent, "rep", [(0, 1), (1, 0)])
     parts = both.reshape(spots * shards, slots * KR, width)
     parts = lax.all_to_all(parts, ("dp", "fsdp"), 0, 0)

time: 59.7 us -> 40.6 us (0.68)
  local copies, waits for them, and re-layouts: 16.1 us -> 0 us
  Pallas kernels: 17.1 us -> 15.2 us
  blocking collectives: 15.1 us -> 13.3 us
  other arithmetic: 0.94 us -> 0.05 us
  waiting for transfers between devices: 3.76 us -> 4.63 us
  starting transfers between devices: 5.95 us -> 6.77 us
    unnamed x12 -> x0, local copies, waits for them, and re-layouts: 16.1 us -> none
    pallas_call x1, Pallas kernels: 9.2 us -> 7.27 us  [per_device(): pl.pallas_call(side_kernel, out_shape=(pltpu.VMEM((4 * KR, count * rows),...]
    all_to_all x1, blocking collectives: 15.1 us -> 13.3 us  [per_device(): parts = lax.all_to_all(parts, ('dp', 'fsdp'), 0, 0)]
    add x2, other arithmetic: 0.93 us -> 0.04 us  [per_device(): side = side + lax.ppermute(side, 'fsdp', pairs)]
    ppermute x2, waiting for transfers between devices: 2.52 us -> 3.39 us  [per_device(): side = side + lax.ppermute(side, 'fsdp', pairs)]
    ppermute x2, starting transfers between devices: 5.88 us -> 6.7 us  [per_device(): side = side + lax.ppermute(side, 'fsdp', pairs)]
  transfers between devices with their start and end apart: 3 -> 3, of which waited for: 3 -> 3; matrix products, arithmetic and copies ran while one was open for 0% -> 0% of each run, Pallas kernels for 7% -> 10%
where the time goes in v3:
time: 40.6 us
  Pallas kernels  15.2 us (37%)
  blocking collectives  13.3 us (33%)
  starting transfers between devices  6.77 us (17%)
  waiting for transfers between devices  4.63 us (11%)
  between operations  0.7 us (2%)
    all_to_all x1, blocking collectives, per_device(): parts = lax.all_to_all(parts, ('dp', 'fsdp'), 0, 0)  13.3 us
    pallas_call x1, Pallas kernels, per_device(): pl.pallas_call(side_kernel, out_shape=(pltpu.VMEM((4 * KR, count * rows),...  7.27 us
    ppermute x2, starting transfers between devices, per_device(): side = side + lax.ppermute(side, 'fsdp', pairs)  6.7 us
    pallas_call x2, Pallas kernels, make_tables(): pl.pallas_call(functools.partial(table_kernel, 32, which), out_shape=[plt...  3.89 us
    ppermute x2, waiting for transfers between devices, per_device(): side = side + lax.ppermute(side, 'fsdp', pairs)  3.39 us
    pallas_call x1, Pallas kernels, per_device(): pl.pallas_call(feature_kernel, out_shape=[pltpu.VMEM((spots, shards, slot...  3.26 us
    ppermute x1, waiting for transfers between devices, per_device(): both = kept + lax.ppermute(sent, 'rep', [(0, 1), (1, 0)])  1.24 us
  transfers between devices with their start and end apart: 3, of which 3 were waited for; matrix products, arithmetic and copies ran while one was open for 0% of the time, Pallas kernels for 10%

profile of v3, /device:TPU:0, one launch (start us, length us, event | category | flops | bytes accessed | tf_op | source)
XLA Modules:
  0.0 40.6 jit_solution(15736831799887361809)
XLA Ops:
  0.7 7.3 %sides.1 = (f32[16,2048]{1,0:T(8,128)S(1)}, s32[8,128]{1,0:T(8,128)S(1)}, bf16[2,1024,2048]{2,1,0:T(8,128)(2,1)S(1)}, bf16[2,1024,2048]{2,1,0:T(8,128)(2,1)S(1)}, bf16[2,1024,256]{2,1,0:T(8,128)(2,1)S(1)}) custom-call(bf16[2,1024,2048]{2,1,0:T(8,128)(2,1)} %hidden_hbm.1, bf16[2,1024,2048]{2,1,0:T(8,128)(2,1)} %query_hbm.1, bf16[2,1024,256]{2,1,0:T(8,128)(2,1)} %value_hbm.1, ...), custom_call_target="tpu_custom_call" | custom-call | tf_op jit(solution)/shard_map/sides/pallas_call | solution.py:314
  7.9 3.1 %collective-permute-start = (f32[16,2048]{1,0:T(8,128)S(1)}, f32[16,2048]{1,0:T(8,128)S(1)}, u32[]{:S(2)}, u32[]{:S(2)}) collective-permute-start(f32[16,2048]{1,0:T(8,128)S(1)} %get-tuple-element.16), channel_id=1, source_target_pairs={{0,4},{4,0},{8,12},{12,8},{1,5},{5,1},{9,13},{13,9},{2,6},{6,2},{1... | collective-permute-start | bytes 393224 | tf_op jit(solution)/shard_map/ppermute | solution.py:368
  11.0 1.8 %tables.2.wide_in = bf16[2048,512]{1,0:T(8,128)(2,1)S(1)} custom-call(s32[8,128]{1,0:T(8,128)S(1)} %get-tuple-element.17.scalar_ref), custom_call_target="tpu_custom_call" | custom-call | tf_op jit(solution)/shard_map/tables/pallas_call | solution.py:355
  12.8 1.1 %collective-permute-done = f32[16,2048]{1,0:T(8,128)S(1)} collective-permute-done((f32[16,2048]{1,0:T(8,128)S(1)}, f32[16,2048]{1,0:T(8,128)S(1)}, u32[]{:S(2)}, u32[]{:S(2)}) %collective-permute-start) | collective-permute-done | bytes 131104 | tf_op jit(solution)/shard_map/ppermute | solution.py:368
  14.0 3.6 %collective-permute-start.1 = (f32[16,2048]{1,0:T(8,128)S(1)}, f32[16,2048]{1,0:T(8,128)S(1)}, u32[]{:S(2)}, u32[]{:S(2)}) collective-permute-start(f32[16,2048]{1,0:T(8,128)S(1)} %add.9), channel_id=1, source_target_pairs={{0,8},{4,12},{8,0},{12,4},{1,9},{5,13},{9,1},{13,5},{2,10},{6,14},... | collective-permute-start | bytes 393224 | tf_op jit(solution)/shard_map/ppermute | solution.py:368
  17.6 2.1 %tables.3 = (bf16[2048,512]{1,0:T(8,128)(2,1)S(1)}, bf16[256,512]{1,0:T(8,128)(2,1)S(1)}) custom-call(s32[8,128]{1,0:T(8,128)S(1)} %get-tuple-element.17.scalar_ref), custom_call_target="tpu_custom_call" | custom-call | tf_op jit(solution)/shard_map/tables/pallas_call | solution.py:355
  19.7 2.3 %collective-permute-done.1 = f32[16,2048]{1,0:T(8,128)S(1)} collective-permute-done((f32[16,2048]{1,0:T(8,128)S(1)}, f32[16,2048]{1,0:T(8,128)S(1)}, u32[]{:S(2)}, u32[]{:S(2)}) %collective-permute-start.1) | collective-permute-done | bytes 131104 | tf_op jit(solution)/shard_map/ppermute | solution.py:368
  22.0 3.3 %features.1 = (f32[2,4,8,256]{3,2,1,0:T(8,128)S(1)}, f32[2,4,8,256]{3,2,1,0:T(8,128)S(1)}) custom-call(f32[16,2048]{1,0:T(8,128)S(1)} %add.10.side_ref, bf16[2,1024,2048]{2,1,0:T(8,128)(2,1)S(1)} %get-tuple-element.19.hidden_ref, bf16[2,1024,2048]{2,1,0:T(8,128)(2,1)S(1)} %get-tuple-element.20.query_ref, ...), custom_call_target="tpu_custom_call" | custom-call | tf_op jit(solution)/shard_map/features/pallas_call | solution.py:376
  25.2 0.1 collective-permute-start.2
  25.3 1.2 %collective-permute-done.2 = f32[2,4,8,256]{3,2,1,0:T(8,128)S(1)} collective-permute-done((f32[2,4,8,256]{3,2,1,0:T(8,128)S(1)}, f32[2,4,8,256]{3,2,1,0:T(8,128)S(1)}, u32[]{:S(2)}, u32[]{:S(2)}) %collective-permute-start.2) | collective-permute-done | bytes 65568 | tf_op jit(solution)/shard_map/ppermute | solution.py:384
  26.6 13.3 %all_to_all.5.pieces_ref = f32[8,8,256]{2,1,0:T(8,128)S(1)} all-to-all(f32[8,8,256]{2,1,0:T(8,128)S(1)} %bitcast.5), channel_id=1, replica_groups=mesh['groups'=2,'fsdp'=4,'dp'=2,'rep'=2] {'dp','fsdp'}, dimensions={0} | all-to-all | bytes 131072 | tf_op jit(solution)/shard_map/all_to_all | solution.py:386
  39.8 0.8 %finish.1 = f32[2,1024]{1,0:T(2,128)} custom-call(f32[8,8,256]{2,1,0:T(8,128)S(1)} %all_to_all.5.pieces_ref), custom_call_target="tpu_custom_call" | custom-call | tf_op jit(solution)/shard_map/finish/pallas_call | solution.py:387
  (3 shorter events, 0.0 us)
Async XLA Ops:
  7.9 6.0 %collective-permute-start = (f32[16,2048]{1,0:T(8,128)S(1)}, f32[16,2048]{1,0:T(8,128)S(1)}, u32[]{:S(2)}, u32[]{:S(2)}) collective-permute-start(f32[16,2048]{1,0:T(8,128)S(1)} %get-tuple-element.16), channel_id=1, source_target_pairs={{0,4},{4,0},{8,12},{12,8},{1,5},{5,1},{9,13},{13,9},{2,6},{6,2},{1... | collective-permute-start | bytes 393224 | tf_op jit(solution)/shard_map/ppermute | solution.py:368
  14.0 8.0 %collective-permute-start.1 = (f32[16,2048]{1,0:T(8,128)S(1)}, f32[16,2048]{1,0:T(8,128)S(1)}, u32[]{:S(2)}, u32[]{:S(2)}) collective-permute-start(f32[16,2048]{1,0:T(8,128)S(1)} %add.9), channel_id=1, source_target_pairs={{0,8},{4,12},{8,0},{12,4},{1,9},{5,13},{9,1},{13,5},{2,10},{6,14},... | collective-permute-start | bytes 393224 | tf_op jit(solution)/shard_map/ppermute | solution.py:368
  25.2 1.3 %collective-permute-start.2 = (f32[2,4,8,256]{3,2,1,0:T(8,128)S(1)}, f32[2,4,8,256]{3,2,1,0:T(8,128)S(1)}, u32[]{:S(2)}, u32[]{:S(2)}) collective-permute-start(f32[2,4,8,256]{3,2,1,0:T(8,128)S(1)} %get-tuple-element.26), channel_id=1, source_target_pairs={{0,1},{1,0},{2,3},{3,2},{4,5},{5,4},{6,7},{7,6},{8,9},{9,8},{10,11... | collective-permute-start | bytes 196616 | tf_op jit(solution)/shard_map/ppermute | solution.py:384

commit v4 on v3

--- a/solution.py
+++ b/solution.py
@@ -67,7 +67,8 @@
     seed_hbm,
     offsets_hbm,
     owners_hbm,
-    side_ref,
+    upper_ref,
+    lower_ref,
     scalar_ref,
     hidden_ref,
     query_ref,
@@ -175,12 +176,13 @@
                 lower = project(from_hidden, hidden_ref[item, here, :])
                 position = first + lax.broadcasted_iota(jnp.int32, (2 * KR, BLOCK), 1)
                 keep = position < lengths[item]
-                side_ref[: 2 * KR, out] = jnp.where(keep, upper, 0.0)
-                side_ref[2 * KR :, out] = jnp.where(keep, lower, 0.0)
+                upper_ref[:, out] = jnp.where(keep, upper, 0.0)
+                lower_ref[:, out] = jnp.where(keep, lower, 0.0)
 
             @pl.when(jnp.logical_not(live))
             def _(item=item, here=here, out=out):
-                side_ref[:, out] = jnp.zeros((4 * KR, BLOCK), F32)
+                upper_ref[:, out] = jnp.zeros((2 * KR, BLOCK), F32)
+                lower_ref[:, out] = jnp.zeros((2 * KR, BLOCK), F32)
                 for ref in (query_ref, value_ref, hidden_ref):
                     ref[item, here, :] = jnp.zeros((BLOCK, ref.shape[2]), BF16)
 
@@ -204,41 +206,47 @@
         lax.fori_loop(0, rows // step_rows, step, first, unroll=4)
 
 
+SIDE_SCALE = (R / 3.0) ** (-0.5) / 128.0 * LMAX ** (-0.5) / 128.0
+
+
+def widened(side_ref, data_ref, table, scale):
+    count, rows, _ = data_ref.shape
+    parts = []
+    for item in range(count):
+        side = side_ref[:, item * rows : (item + 1) * rows]
+        product = jnp.dot(split_rows(side), data_ref[item], preferred_element_type=F32)
+        parts.append(join_rows(product))
+    gathered = jnp.concatenate(parts, axis=0)
+    product = jnp.dot(split_rows(gathered), table[...], preferred_element_type=F32)
+    return join_rows(product) * (SIDE_SCALE * scale)
+
+
+def upper_kernel(side_ref, hidden_ref, wide_in, out_ref):
+    out_ref[...] = widened(side_ref, hidden_ref, wide_in, (D / 3.0) ** (-0.5))
+
+
 def feature_kernel(
+    upper_ref,
     side_ref,
-    hidden_ref,
     query_ref,
     value_ref,
-    wide_in,
     wide_query,
     wide_value,
     scalar_ref,
     kept_ref,
     sent_ref,
 ):
-    count, rows, _ = hidden_ref.shape
+    count = query_ref.shape[0]
     half = 2 * KR
-
-    def gathered(data_ref, first):
-        parts = []
-        for item in range(count):
-            side = side_ref[first : first + half, item * rows : (item + 1) * rows]
-            product = jnp.dot(split_rows(side), data_ref[item], preferred_element_type=F32)
-            parts.append(join_rows(product))
-        return jnp.concatenate(parts, axis=0)
-
-    def widened(gathered_rows, table):
-        product = jnp.dot(split_rows(gathered_rows), table[...], preferred_element_type=F32)
-        return join_rows(product)
-
-    side_scale = (R / 3.0) ** (-0.5) / 128.0 * LMAX ** (-0.5) / 128.0
-    upper = widened(gathered(hidden_ref, 0), wide_in) * (side_scale * (D / 3.0) ** (-0.5))
-    query = widened(gathered(query_ref, half), wide_query) * (side_scale * (DQ / 3.0) ** (-0.5))
-    value = widened(gathered(value_ref, half), wide_value) * (side_scale * (DV / 3.0) ** (-0.5))
+    upper = upper_ref[...]
+    query = widened(side_ref, query_ref, wide_query, (DQ / 3.0) ** (-0.5))
+    value = widened(side_ref, value_ref, wide_value, (DV / 3.0) ** (-0.5))
     group = lax.rem(lax.broadcasted_iota(jnp.int32, query.shape, 0), half)
     lower = jnp.where(group < KR, query, value)
     targets = [scalar_ref[4 + item : 5 + item, 0:1] for item in range(count)]
     spots, pieces, slot_rows, width = kept_ref.shape
+    place = lax.axis_index("dp")
+    shard = lax.axis_index("fsdp")
     slots = slot_rows // KR
     first_half = lax.axis_index("rep") == 0
     per_block = KP // width
@@ -257,8 +265,8 @@
             for chunk in range(block * per_block, (block + 1) * per_block, 2):
                 at = (chunk % per_block) * width
                 even, odd = wanted[:, at : at + width], wanted[:, at + width : at + 2 * width]
-                kept_ref[spot, chunk // 2] = jnp.where(first_half, even, odd)
-                sent_ref[spot, chunk // 2] = jnp.where(first_half, odd, even)
+                kept_ref[spot ^ place, (chunk // 2) ^ shard] = jnp.where(first_half, even, odd)
+                sent_ref[spot ^ place, (chunk // 2) ^ shard] = jnp.where(first_half, odd, even)
 
 
 def finish_kernel(pieces_ref, out_ref):
@@ -311,17 +319,18 @@
     v_cols = value_grad.shape[2]
     shards = lax.axis_size("fsdp")
     spots = lax.axis_size("dp")
-    side, scalars, hidden, query, value = pl.pallas_call(
+    upper, lower, scalars, hidden, query, value = pl.pallas_call(
         side_kernel,
         out_shape=(
-            pltpu.VMEM((4 * KR, count * rows), F32),
+            pltpu.VMEM((2 * KR, count * rows), F32),
+            pltpu.VMEM((2 * KR, count * rows), F32),
             pltpu.VMEM((8, 128), jnp.int32),
             pltpu.VMEM(hidden_in.shape, BF16),
             pltpu.VMEM(query_grad.shape, BF16),
             pltpu.VMEM(value_grad.shape, BF16),
         ),
         in_specs=[in_hbm()] * 11,
-        out_specs=[in_vmem()] * 5,
+        out_specs=[in_vmem()] * 6,
         scratch_shapes=[
             pltpu.VMEM(query_down.shape[::-1], BF16),
             pltpu.VMEM(query_up.shape, BF16),
@@ -362,28 +371,46 @@
         )(scalars)
 
     (wide_in,) = make_tables((0,), (in_cols,))
+    wide_query, wide_value = make_tables((1, 2), (q_cols, v_cols))
+
     hop = 1
     while hop < shards:
         pairs = [(i, i ^ hop) for i in range(shards)]
-        side = side + lax.ppermute(side, "fsdp", pairs)
+        moved = lax.ppermute(upper, "fsdp", pairs)
         if hop == 1:
-            side, wide_in = lax.optimization_barrier((side, wide_in))
+            moved, wide_in = lax.optimization_barrier((moved, wide_in))
+        upper = upper + moved
+        lower = lower + lax.ppermute(lower, "fsdp", pairs)
         hop *= 2
-    wide_query, wide_value = make_tables((1, 2), (q_cols, v_cols))
+    upper = pl.pallas_call(
+        upper_kernel,
+        out_shape=pltpu.VMEM((count * 2 * KR, KP), F32),
+        in_specs=[in_vmem()] * 3,
+        out_specs=in_vmem(),
+        compiler_params=pltpu.CompilerParams(vmem_limit_bytes=16 * 2**20),
+        name="upper",
+    )(upper, hidden, wide_in)
     examples = owners.shape[0]
     slots = examples // spots
     width = 4 * KP // (2 * shards)
     kept, sent = pl.pallas_call(
         feature_kernel,
         out_shape=[pltpu.VMEM((spots, shards, slots * KR, width), F32)] * 2,
-        in_specs=[in_vmem()] * 8,
+        in_specs=[in_vmem()] * 7,
         out_specs=[in_vmem()] * 2,
         compiler_params=pltpu.CompilerParams(vmem_limit_bytes=16 * 2**20),
         name="features",
-    )(side, hidden, query, value, wide_in, wide_query, wide_value, scalars)
-    both = kept + lax.ppermute(sent, "rep", [(0, 1), (1, 0)])
-    parts = both.reshape(spots * shards, slots * KR, width)
-    parts = lax.all_to_all(parts, ("dp", "fsdp"), 0, 0)
+    )(upper, lower, query, value, wide_query, wide_value, scalars)
+    mine = kept[0] + lax.ppermute(sent[0], "rep", [(0, 1), (1, 0)])
+    for hop in range(1, spots):
+        straight = [(i, i ^ hop) for i in range(spots)]
+        crossed = [(2 * i + r, 2 * (i ^ hop) + 1 - r) for i in range(spots) for r in range(2)]
+        mine = mine + lax.ppermute(kept[hop], "dp", straight)
+        mine = mine + lax.ppermute(sent[hop], ("dp", "rep"), crossed)
+    parts = [mine[0]]
+    for hop in range(1, shards):
+        parts.append(lax.ppermute(mine[hop], "fsdp", [(i, i ^ hop) for i in range(shards)]))
+    parts = jnp.stack(parts)
     return pl.pallas_call(
         finish_kernel,
         out_shape=jax.ShapeDtypeStruct((slots, width * KR), F32),

time: 40.6 us -> 37.8 us (0.931)
  blocking collectives: 13.3 us -> 0 us
  starting transfers between devices: 6.77 us -> 14.7 us
  waiting for transfers between devices: 4.63 us -> 6.98 us
    all_to_all x1 -> x0, blocking collectives: 13.3 us -> none  [per_device(): parts = lax.all_to_all(parts, ('dp', 'fsdp'), 0, 0)]
    ppermute x3 -> x10, starting transfers between devices: 6.77 us -> 14.7 us  [the longest x2 6.03 us: per_device(): moved = lax.ppermute(upper, 'fsdp', pairs)]
    ppermute x3 -> x10, waiting for transfers between devices: 4.63 us -> 6.98 us  [the longest x3 3.26 us: per_device(): lax.ppermute(mine[hop], 'fsdp', [(i, i ^ hop) for i in range(shards)])]
    pallas_call x1 -> x2, Pallas kernels: 7.27 us -> 8.81 us  [the longest x1 7.27 us: per_device(): pl.pallas_call(side_kernel, out_shape=(pltpu.VMEM((2 * KR, count * rows),...]
    pallas_call x1, Pallas kernels: 3.26 us -> 1.82 us  [per_device(): pl.pallas_call(feature_kernel, out_shape=[pltpu.VMEM((spots, shards, slot...]
  transfers between devices with their start and end apart: 3 -> 10, of which waited for: 3 -> 6; matrix products, arithmetic and copies ran while one was open for 0% -> 0% of each run, Pallas kernels for 10% -> 14%
where the time goes in v4:
time: 37.8 us
  Pallas kernels  15.3 us (40%)
  starting transfers between devices  14.7 us (39%)
  waiting for transfers between devices  6.98 us (18%)
  between operations  0.74 us (2%)
    pallas_call x1, Pallas kernels, per_device(): pl.pallas_call(side_kernel, out_shape=(pltpu.VMEM((2 * KR, count * rows),...  7.27 us
    ppermute x2, starting transfers between devices, per_device(): moved = lax.ppermute(upper, 'fsdp', pairs)  6.03 us
    ppermute x3, starting transfers between devices, per_device(): lax.ppermute(mine[hop], 'fsdp', [(i, i ^ hop) for i in range(shards)])  4.45 us
    pallas_call x2, Pallas kernels, make_tables(): pl.pallas_call(functools.partial(table_kernel, 32, which), out_shape=[plt...  3.89 us
    ppermute x3, waiting for transfers between devices, per_device(): lax.ppermute(mine[hop], 'fsdp', [(i, i ^ hop) for i in range(shards)])  3.26 us
    ppermute x1, starting transfers between devices, per_device(): mine = mine + lax.ppermute(kept[hop], 'dp', straight)  2.23 us
    pallas_call x1, Pallas kernels, per_device(): pl.pallas_call(feature_kernel, out_shape=[pltpu.VMEM((spots, shards, slot...  1.82 us
    ppermute x2, starting transfers between devices, per_device(): lower = lower + lax.ppermute(lower, 'fsdp', pairs)  1.74 us
  transfers between devices with their start and end apart: 10, of which 6 were waited for; matrix products, arithmetic and copies ran while one was open for 0% of the time, Pallas kernels for 14%

profile of v4, /device:TPU:0, one launch (start us, length us, event | category | flops | bytes accessed | tf_op | source)
XLA Modules:
  0.0 37.8 jit_solution(16975127622514396357)
XLA Ops:
  0.7 7.3 %sides.1 = (f32[8,2048]{1,0:T(8,128)S(1)}, f32[8,2048]{1,0:T(8,128)S(1)}, s32[8,128]{1,0:T(8,128)S(1)}, bf16[2,1024,2048]{2,1,0:T(8,128)(2,1)S(1)}, bf16[2,1024,...) custom-call(bf16[2,1024,2048]{2,1,0:T(8,128)(2,1)} %hidden_hbm.1, bf16[2,1024,2048]{2,1,0:T(8,128)(2,1)} %query_hbm.1, ...), custom_call_target="tpu_custom_call" | custom-call | tf_op jit(solution)/shard_map/sides/pallas_call | solution.py:322
  7.9 3.1 %collective-permute-start = (f32[8,2048]{1,0:T(8,128)S(1)}, f32[8,2048]{1,0:T(8,128)S(1)}, u32[]{:S(2)}, u32[]{:S(2)}) collective-permute-start(f32[8,2048]{1,0:T(8,128)S(1)} %get-tuple-element.17), channel_id=1, source_target_pairs={{0,4},{4,0},{8,12},{12,8},{1,5},{5,1},{9,13},{13,9},{2,6},{6,2},{1... | collective-permute-start | bytes 196616 | tf_op jit(solution)/shard_map/ppermute | solution.py:379
  11.0 0.1 collective-permute-start.2
  11.1 1.8 %tables.2.wide_in = bf16[2048,512]{1,0:T(8,128)(2,1)S(1)} custom-call(s32[8,128]{1,0:T(8,128)S(1)} %get-tuple-element.18.scalar_ref), custom_call_target="tpu_custom_call" | custom-call | tf_op jit(solution)/shard_map/tables/pallas_call | solution.py:364
  12.9 0.5 %collective-permute-done = f32[8,2048]{1,0:T(8,128)S(1)} collective-permute-done((f32[8,2048]{1,0:T(8,128)S(1)}, f32[8,2048]{1,0:T(8,128)S(1)}, u32[]{:S(2)}, u32[]{:S(2)}) %collective-permute-start) | collective-permute-done | bytes 65568 | tf_op jit(solution)/shard_map/ppermute | solution.py:379
  13.4 2.9 %collective-permute-start.1 = (f32[8,2048]{1,0:T(8,128)S(1)}, f32[8,2048]{1,0:T(8,128)S(1)}, u32[]{:S(2)}, u32[]{:S(2)}) collective-permute-start(f32[8,2048]{1,0:T(8,128)S(1)} %add.21), channel_id=1, source_target_pairs={{0,8},{4,12},{8,0},{12,4},{1,9},{5,13},{9,1},{13,5},{2,10},{6,14},... | collective-permute-start | bytes 196616 | tf_op jit(solution)/shard_map/ppermute | solution.py:379
  16.4 0.0 collective-permute-done.2
  16.4 1.7 %collective-permute-start.3 = (f32[8,2048]{1,0:T(8,128)S(1)}, f32[8,2048]{1,0:T(8,128)S(1)}, u32[]{:S(2)}, u32[]{:S(2)}) collective-permute-start(f32[8,2048]{1,0:T(8,128)S(1)} %add.23), channel_id=1, source_target_pairs={{0,8},{4,12},{8,0},{12,4},{1,9},{5,13},{9,1},{13,5},{2,10},{6,14},... | collective-permute-start | bytes 196616 | tf_op jit(solution)/shard_map/ppermute | solution.py:383
  18.1 2.1 %tables.3 = (bf16[2048,512]{1,0:T(8,128)(2,1)S(1)}, bf16[256,512]{1,0:T(8,128)(2,1)S(1)}) custom-call(s32[8,128]{1,0:T(8,128)S(1)} %get-tuple-element.18.scalar_ref), custom_call_target="tpu_custom_call" | custom-call | tf_op jit(solution)/shard_map/tables/pallas_call | solution.py:364
  20.1 0.1 collective-permute-done.1
  20.2 1.5 %upper.1.upper_ref = f32[16,512]{1,0:T(8,128)S(1)} custom-call(f32[8,2048]{1,0:T(8,128)S(1)} %add.22.side_ref, bf16[2,1024,2048]{2,1,0:T(8,128)(2,1)S(1)} %get-tuple-element.20.hidden_ref, bf16[2048,512]{1,0:T(8,128)(2,1)S(1)} %tables.2.wide_in), custom_call_target="tpu_custom_call" | custom-call | tf_op jit(solution)/shard_map/upper/pallas_call | solution.py:385
  21.8 0.0 collective-permute-done.3
  21.8 1.8 %features.1 = (f32[2,4,8,256]{3,2,1,0:T(8,128)S(1)}, f32[2,4,8,256]{3,2,1,0:T(8,128)S(1)}) custom-call(f32[16,512]{1,0:T(8,128)S(1)} %upper.1.upper_ref, f32[8,2048]{1,0:T(8,128)S(1)} %add.24.side_ref, bf16[2,1024,2048]{2,1,0:T(8,128)(2,1)S(1)} %get-tuple-element.23.query_ref, bf16[2,1024,256]{2,1,0:T(8,128)(2,1)S(1)} %get-tuple-element.24.value_ref, ...), custom_call_target="tpu_custom_call" | custom-call | tf_op jit(solution)/shard_map/features/pallas_call | solution.py:396
  23.7 2.2 %collective-permute-start.5 = (f32[4,8,256]{2,1,0:T(8,128)S(1)}, f32[4,8,256]{2,1,0:T(8,128)S(1)}, u32[]{:S(2)}, u32[]{:S(2)}) collective-permute-start(f32[4,8,256]{2,1,0:T(8,128)S(1)} %slice_bitcast_fusion.1), channel_id=1, source_target_pairs={{0,2},{2,0},{1,3},{3,1},{4,6},{6,4},{5,7},{7,5},{8,10},{10,8},{9,1... | collective-permute-start | bytes 98312 | tf_op jit(solution)/shard_map/ppermute | solution.py:408
  25.9 0.0 collective-permute-start.4
  25.9 0.2 collective-permute-start.6
  26.1 1.7 %collective-permute-done.5 = f32[4,8,256]{2,1,0:T(8,128)S(1)} collective-permute-done((f32[4,8,256]{2,1,0:T(8,128)S(1)}, f32[4,8,256]{2,1,0:T(8,128)S(1)}, u32[]{:S(2)}, u32[]{:S(2)}) %collective-permute-start.5) | collective-permute-done | bytes 32800 | tf_op jit(solution)/shard_map/ppermute | solution.py:408
  27.8 1.4 %collective-permute-done.6 = f32[4,8,256]{2,1,0:T(8,128)S(1)} collective-permute-done((f32[4,8,256]{2,1,0:T(8,128)S(1)}, f32[4,8,256]{2,1,0:T(8,128)S(1)}, u32[]{:S(2)}, u32[]{:S(2)}) %collective-permute-start.6) | collective-permute-done | bytes 32800 | tf_op jit(solution)/shard_map/ppermute | solution.py:409
  29.3 3.2 %collective-permute-start.9 = (f32[8,256]{1,0:T(8,128)S(1)}, f32[8,256]{1,0:T(8,128)S(1)}, u32[]{:S(2)}, u32[]{:S(2)}) collective-permute-start(f32[8,256]{1,0:T(8,128)S(1)} %get-tuple-element.32), channel_id=1, source_target_pairs={{0,12},{4,8},{8,4},{12,0},{1,13},{5,9},{9,5},{13,1},{2,14},{6,10},... | collective-permute-start | bytes 24584 | tf_op jit(solution)/shard_map/ppermute | solution.py:412
  32.4 0.5 %collective-permute-start.8 = (f32[8,256]{1,0:T(8,128)S(1)}, f32[8,256]{1,0:T(8,128)S(1)}, u32[]{:S(2)}, u32[]{:S(2)}) collective-permute-start(f32[8,256]{1,0:T(8,128)S(1)} %get-tuple-element.33), channel_id=1, source_target_pairs={{0,8},{4,12},{8,0},{12,4},{1,9},{5,13},{9,1},{13,5},{2,10},{6,14},... | collective-permute-start | bytes 24584 | tf_op jit(solution)/shard_map/ppermute | solution.py:412
  33.0 0.8 %collective-permute-start.7 = (f32[8,256]{1,0:T(8,128)S(1)}, f32[8,256]{1,0:T(8,128)S(1)}, u32[]{:S(2)}, u32[]{:S(2)}) collective-permute-start(f32[8,256]{1,0:T(8,128)S(1)} %get-tuple-element.34), channel_id=1, source_target_pairs={{0,4},{4,0},{8,12},{12,8},{1,5},{5,1},{9,13},{13,9},{2,6},{6,2},{1... | collective-permute-start | bytes 24584 | tf_op jit(solution)/shard_map/ppermute | solution.py:412
  33.7 1.1 %collective-permute-done.9 = f32[8,256]{1,0:T(8,128)S(1)} collective-permute-done((f32[8,256]{1,0:T(8,128)S(1)}, f32[8,256]{1,0:T(8,128)S(1)}, u32[]{:S(2)}, u32[]{:S(2)}) %collective-permute-start.9) | collective-permute-done | bytes 8224 | tf_op jit(solution)/shard_map/ppermute | solution.py:412
  34.8 2.2 %collective-permute-done.8 = f32[8,256]{1,0:T(8,128)S(1)} collective-permute-done((f32[8,256]{1,0:T(8,128)S(1)}, f32[8,256]{1,0:T(8,128)S(1)}, u32[]{:S(2)}, u32[]{:S(2)}) %collective-permute-start.8) | collective-permute-done | bytes 8224 | tf_op jit(solution)/shard_map/ppermute | solution.py:412
  37.0 0.8 %finish.1 = f32[2,1024]{1,0:T(2,128)} custom-call(f32[4,8,256]{2,1,0:T(8,128)S(1)} %pad_maximum_fusion.pieces_ref), custom_call_target="tpu_custom_call" | custom-call | tf_op jit(solution)/shard_map/finish/pallas_call | solution.py:414
  (11 shorter events, 0.1 us)
Async XLA Ops:
  7.9 5.5 %collective-permute-start = (f32[8,2048]{1,0:T(8,128)S(1)}, f32[8,2048]{1,0:T(8,128)S(1)}, u32[]{:S(2)}, u32[]{:S(2)}) collective-permute-start(f32[8,2048]{1,0:T(8,128)S(1)} %get-tuple-element.17), channel_id=1, source_target_pairs={{0,4},{4,0},{8,12},{12,8},{1,5},{5,1},{9,13},{13,9},{2,6},{6,2},{1... | collective-permute-start | bytes 196616 | tf_op jit(solution)/shard_map/ppermute | solution.py:379
  11.0 5.4 %collective-permute-start.2 = (f32[8,2048]{1,0:T(8,128)S(1)}, f32[8,2048]{1,0:T(8,128)S(1)}, u32[]{:S(2)}, u32[]{:S(2)}) collective-permute-start(f32[8,2048]{1,0:T(8,128)S(1)} %get-tuple-element.22), channel_id=1, source_target_pairs={{0,4},{4,0},{8,12},{12,8},{1,5},{5,1},{9,13},{13,9},{2,6},{6,2},{1... | collective-permute-start | bytes 196616 | tf_op jit(solution)/shard_map/ppermute | solution.py:383
  13.4 6.8 %collective-permute-start.1 = (f32[8,2048]{1,0:T(8,128)S(1)}, f32[8,2048]{1,0:T(8,128)S(1)}, u32[]{:S(2)}, u32[]{:S(2)}) collective-permute-start(f32[8,2048]{1,0:T(8,128)S(1)} %add.21), channel_id=1, source_target_pairs={{0,8},{4,12},{8,0},{12,4},{1,9},{5,13},{9,1},{13,5},{2,10},{6,14},... | collective-permute-start | bytes 196616 | tf_op jit(solution)/shard_map/ppermute | solution.py:379
  16.4 5.4 %collective-permute-start.3 = (f32[8,2048]{1,0:T(8,128)S(1)}, f32[8,2048]{1,0:T(8,128)S(1)}, u32[]{:S(2)}, u32[]{:S(2)}) collective-permute-start(f32[8,2048]{1,0:T(8,128)S(1)} %add.23), channel_id=1, source_target_pairs={{0,8},{4,12},{8,0},{12,4},{1,9},{5,13},{9,1},{13,5},{2,10},{6,14},... | collective-permute-start | bytes 196616 | tf_op jit(solution)/shard_map/ppermute | solution.py:383
  23.7 4.1 %collective-permute-start.5 = (f32[4,8,256]{2,1,0:T(8,128)S(1)}, f32[4,8,256]{2,1,0:T(8,128)S(1)}, u32[]{:S(2)}, u32[]{:S(2)}) collective-permute-start(f32[4,8,256]{2,1,0:T(8,128)S(1)} %slice_bitcast_fusion.1), channel_id=1, source_target_pairs={{0,2},{2,0},{1,3},{3,1},{4,6},{6,4},{5,7},{7,5},{8,10},{10,8},{9,1... | collective-permute-start | bytes 98312 | tf_op jit(solution)/shard_map/ppermute | solution.py:408
  25.9 1.9 %collective-permute-start.4 = (f32[4,8,256]{2,1,0:T(8,128)S(1)}, f32[4,8,256]{2,1,0:T(8,128)S(1)}, u32[]{:S(2)}, u32[]{:S(2)}) collective-permute-start(f32[4,8,256]{2,1,0:T(8,128)S(1)} %get-tuple-element.29), channel_id=1, source_target_pairs={{0,1},{1,0},{2,3},{3,2},{4,5},{5,4},{6,7},{7,6},{8,9},{9,8},{10,11... | collective-permute-start | bytes 98312 | tf_op jit(solution)/shard_map/ppermute | solution.py:404
  25.9 3.3 %collective-permute-start.6 = (f32[4,8,256]{2,1,0:T(8,128)S(1)}, f32[4,8,256]{2,1,0:T(8,128)S(1)}, u32[]{:S(2)}, u32[]{:S(2)}) collective-permute-start(f32[4,8,256]{2,1,0:T(8,128)S(1)} %get-tuple-element.30), channel_id=1, source_target_pairs={{0,3},{1,2},{2,1},{3,0},{4,7},{5,6},{6,5},{7,4},{8,11},{9,10},{10,... | collective-permute-start | bytes 98312 | tf_op jit(solution)/shard_map/ppermute | solution.py:409
  29.3 5.5 %collective-permute-start.9 = (f32[8,256]{1,0:T(8,128)S(1)}, f32[8,256]{1,0:T(8,128)S(1)}, u32[]{:S(2)}, u32[]{:S(2)}) collective-permute-start(f32[8,256]{1,0:T(8,128)S(1)} %get-tuple-element.32), channel_id=1, source_target_pairs={{0,12},{4,8},{8,4},{12,0},{1,13},{5,9},{9,5},{13,1},{2,14},{6,10},... | collective-permute-start | bytes 24584 | tf_op jit(solution)/shard_map/ppermute | solution.py:412
  32.4 4.5 %collective-permute-start.8 = (f32[8,256]{1,0:T(8,128)S(1)}, f32[8,256]{1,0:T(8,128)S(1)}, u32[]{:S(2)}, u32[]{:S(2)}) collective-permute-start(f32[8,256]{1,0:T(8,128)S(1)} %get-tuple-element.33), channel_id=1, source_target_pairs={{0,8},{4,12},{8,0},{12,4},{1,9},{5,13},{9,1},{13,5},{2,10},{6,14},... | collective-permute-start | bytes 24584 | tf_op jit(solution)/shard_map/ppermute | solution.py:412
  33.0 4.0 %collective-permute-start.7 = (f32[8,256]{1,0:T(8,128)S(1)}, f32[8,256]{1,0:T(8,128)S(1)}, u32[]{:S(2)}, u32[]{:S(2)}) collective-permute-start(f32[8,256]{1,0:T(8,128)S(1)} %get-tuple-element.34), channel_id=1, source_target_pairs={{0,4},{4,0},{8,12},{12,8},{1,5},{5,1},{9,13},{13,9},{2,6},{6,2},{1... | collective-permute-start | bytes 24584 | tf_op jit(solution)/shard_map/ppermute | solution.py:412

commit v5 on v4

--- a/solution.py
+++ b/solution.py
@@ -1,4 +1,5 @@
 import functools
+import math
 
 import jax
 import jax.numpy as jnp
@@ -88,6 +89,10 @@
     count, rows, _ = hidden_ref.shape
     blocks = rows // BLOCK
     start = lax.axis_index("rep") * rows
+
+    def sem_of(ref):
+        return 0 if ref.shape[-1] % 128 == 0 else 1
+
     scalars = [
         pltpu.make_async_copy(src, dst, scalar_sem.at[k])
         for k, (src, dst) in enumerate(
@@ -100,14 +105,12 @@
         )
     ]
     factors = [
-        pltpu.make_async_copy(src, dst, factor_sem.at[k])
-        for k, (src, dst) in enumerate(
-            (
-                (query_up_hbm, query_up),
-                (value_up_hbm, value_up),
-                (query_down_hbm, query_down),
-                (value_down_hbm, value_down),
-            )
+        pltpu.make_async_copy(src, dst, factor_sem.at[sem_of(dst)])
+        for src, dst in (
+            (query_up_hbm, query_up),
+            (value_up_hbm, value_up),
+            (query_down_hbm, query_down),
+            (value_down_hbm, value_down),
         )
     ]
     for copy in scalars + factors:
@@ -119,24 +122,38 @@
                 pltpu.make_async_copy(
                     src.at[item, pl.ds(block * BLOCK, BLOCK)],
                     dst.at[item, pl.ds(block * BLOCK, BLOCK)],
-                    block_sem.at[k, item, block],
+                    block_sem.at[sem_of(dst), item, block],
                 )
                 for block in range(blocks)
             ]
             for item in range(count)
         ]
-        for k, (src, dst) in enumerate(arrays)
+        for src, dst in arrays
     ]
+
+    def wait_all(pending, dsts, sem):
+        amount = sum(math.prod(dst.shape) for dst in dsts if sem_of(dst) == 0)
+        part = hidden_ref.at[0, pl.ds(0, amount // hidden_ref.shape[2])]
+        pltpu.make_async_copy(part, part, sem).wait()
+        for copy, dst in zip(pending, dsts):
+            if sem_of(dst):
+                copy.wait()
+
+    def block_views(item, block):
+        return [dst.at[item, pl.ds(block * BLOCK, BLOCK)] for _, dst in arrays]
+
     scalars[0].wait()
-    for item in range(count):
+    def fetch(item):
         for block in range(blocks):
 
             @pl.when(start + block * BLOCK < lengths[item])
-            def _(item=item, block=block):
+            def _(block=block):
                 for per_array in copies:
                     per_array[item][block].start()
 
-    for copy in scalars[1:] + factors:
+    fetch(0)
+    wait_all(factors, (query_up, value_up, query_down, value_down), factor_sem.at[0])
+    for copy in scalars[1:]:
         copy.wait()
     seed_value = seed[0]
     first = lax.axis_index("dp") * count
@@ -154,11 +171,24 @@
     from_value = split_rows(folded(value_up, 1, KR))
     from_hidden = split_rows(folded(query_down, 2, 0) + folded(value_down, 3, KR))
 
-    def project(weights, data):
-        product = lax.dot_general(
-            weights, data, (((1,), (1,)), ((), ())), preferred_element_type=F32
-        )
-        return join_rows(product)
+    for item in range(1, count):
+        fetch(item)
+
+    def project(weights, ref, item, here):
+        width = weights.shape[1]
+        step = min(512, width)
+        products = [
+            lax.dot_general(
+                weights[:, at : at + step],
+                ref[item, here, at : at + step],
+                (((1,), (1,)), ((), ())),
+                preferred_element_type=F32,
+            )
+            for at in range(0, width, step)
+        ]
+        while len(products) > 1:
+            products = [sum(products[k + 1 : k + 2], products[k]) for k in range(0, len(products), 2)]
+        return join_rows(products[0])
 
     for item in range(count):
         for block in range(blocks):
@@ -169,11 +199,14 @@
 
             @pl.when(live)
             def _(item=item, block=block, first=first, here=here, out=out):
-                for per_array in copies:
-                    per_array[item][block].wait()
-                upper = project(from_query, query_ref[item, here, :])
-                upper = upper + project(from_value, value_ref[item, here, :])
-                lower = project(from_hidden, hidden_ref[item, here, :])
+                wait_all(
+                    [per_array[item][block] for per_array in copies],
+                    block_views(item, block),
+                    block_sem.at[0, item, block],
+                )
+                upper = project(from_query, query_ref, item, here)
+                upper = upper + project(from_value, value_ref, item, here)
+                lower = project(from_hidden, hidden_ref, item, here)
                 position = first + lax.broadcasted_iota(jnp.int32, (2 * KR, BLOCK), 1)
                 keep = position < lengths[item]
                 upper_ref[:, out] = jnp.where(keep, upper, 0.0)
@@ -340,8 +373,8 @@
             pltpu.SMEM(proj_seed.shape, jnp.int32),
             pltpu.SMEM(offsets.shape, jnp.int32),
             pltpu.SMEM(owners.shape, jnp.int32),
-            pltpu.SemaphoreType.DMA((3, count, rows // BLOCK)),
-            pltpu.SemaphoreType.DMA((4,)),
+            pltpu.SemaphoreType.DMA((2, count, rows // BLOCK)),
+            pltpu.SemaphoreType.DMA((2,)),
             pltpu.SemaphoreType.DMA((4,)),
         ],
         compiler_params=pltpu.CompilerParams(vmem_limit_bytes=42 * 2**20),

time: 37.8 us -> 37.5 us (level)
  waiting for transfers between devices: 6.98 us -> 5.58 us
  Pallas kernels: 15.3 us -> 16.4 us
    ppermute x1, starting transfers between devices: 2.23 us -> 0.07 us  [per_device(): mine = mine + lax.ppermute(kept[hop], 'dp', straight)]
    ppermute x1, starting transfers between devices: 0.2 us -> 2.05 us  [per_device(): mine = mine + lax.ppermute(sent[hop], ('dp', 'rep'), crossed)]
    ppermute x1, waiting for transfers between devices: 1.45 us -> 0.01 us  [per_device(): mine = mine + lax.ppermute(sent[hop], ('dp', 'rep'), crossed)]
    ppermute x2, waiting for transfers between devices: 0.01 us -> 1.15 us  [per_device(): lower = lower + lax.ppermute(lower, 'fsdp', pairs)]
    ppermute x3, waiting for transfers between devices: 3.26 us -> 2.13 us  [per_device(): lax.ppermute(mine[hop], 'fsdp', [(i, i ^ hop) for i in range(shards)])]
    pallas_call x1, Pallas kernels: 7.27 us -> 8.31 us  [per_device(): pl.pallas_call(side_kernel, out_shape=(pltpu.VMEM((2 * KR, count * rows),...]
    ppermute x2, starting transfers between devices: 6.03 us -> 6.72 us  [per_device(): moved = lax.ppermute(upper, 'fsdp', pairs)]
    ppermute x2, starting transfers between devices: 1.74 us -> 1.21 us  [per_device(): lower = lower + lax.ppermute(lower, 'fsdp', pairs)]
  transfers between devices with their start and end apart: 10 -> 10, of which waited for: 6 -> 5; matrix products, arithmetic and copies ran while one was open for 0% -> 0% of each run, Pallas kernels for 14% -> 15%
where the time goes in v5:
time: 37.5 us; the launch traced here: 37.3 us
  Pallas kernels  16.4 us (44%)
  starting transfers between devices  14.6 us (39%)
  waiting for transfers between devices  5.58 us (15%)
  between operations  0.76 us (2%)
    pallas_call x1, Pallas kernels, per_device(): pl.pallas_call(side_kernel, out_shape=(pltpu.VMEM((2 * KR, count * rows),...  8.31 us
    ppermute x2, starting transfers between devices, per_device(): moved = lax.ppermute(upper, 'fsdp', pairs)  6.72 us
    ppermute x3, starting transfers between devices, per_device(): lax.ppermute(mine[hop], 'fsdp', [(i, i ^ hop) for i in range(shards)])  4.45 us
    pallas_call x2, Pallas kernels, make_tables(): pl.pallas_call(functools.partial(table_kernel, 32, which), out_shape=[plt...  3.89 us
    ppermute x3, waiting for transfers between devices, per_device(): lax.ppermute(mine[hop], 'fsdp', [(i, i ^ hop) for i in range(shards)])  2.13 us
    ppermute x1, starting transfers between devices, per_device(): mine = mine + lax.ppermute(sent[hop], ('dp', 'rep'), crossed)  2.05 us
    ppermute x1, waiting for transfers between devices, per_device(): mine = mine + lax.ppermute(kept[hop], 'dp', straight)  1.95 us
    pallas_call x1, Pallas kernels, per_device(): pl.pallas_call(feature_kernel, out_shape=[pltpu.VMEM((spots, shards, slot...  1.82 us
  transfers between devices with their start and end apart: 10, of which 5 were waited for; matrix products, arithmetic and copies ran while one was open for 0% of the time, Pallas kernels for 15%

profile of v5, /device:TPU:0, one launch (start us, length us, event | category | flops | bytes accessed | tf_op | source)
XLA Modules:
  0.0 37.3 jit_solution(16676480799410331418)
XLA Ops:
  0.7 8.3 %sides.1 = (f32[8,2048]{1,0:T(8,128)S(1)}, f32[8,2048]{1,0:T(8,128)S(1)}, s32[8,128]{1,0:T(8,128)S(1)}, bf16[2,1024,2048]{2,1,0:T(8,128)(2,1)S(1)}, bf16[2,1024,...) custom-call(bf16[2,1024,2048]{2,1,0:T(8,128)(2,1)} %hidden_hbm.1, bf16[2,1024,2048]{2,1,0:T(8,128)(2,1)} %query_hbm.1, ...), custom_call_target="tpu_custom_call" | custom-call | tf_op jit(solution)/shard_map/sides/pallas_call | solution.py:355
  9.0 3.1 %collective-permute-start = (f32[8,2048]{1,0:T(8,128)S(1)}, f32[8,2048]{1,0:T(8,128)S(1)}, u32[]{:S(2)}, u32[]{:S(2)}) collective-permute-start(f32[8,2048]{1,0:T(8,128)S(1)} %get-tuple-element.17), channel_id=1, source_target_pairs={{0,4},{4,0},{8,12},{12,8},{1,5},{5,1},{9,13},{13,9},{2,6},{6,2},{1... | collective-permute-start | bytes 196616 | tf_op jit(solution)/shard_map/ppermute | solution.py:412
  12.1 0.1 collective-permute-start.2
  12.1 1.8 %tables.2.wide_in = bf16[2048,512]{1,0:T(8,128)(2,1)S(1)} custom-call(s32[8,128]{1,0:T(8,128)S(1)} %get-tuple-element.18.scalar_ref), custom_call_target="tpu_custom_call" | custom-call | tf_op jit(solution)/shard_map/tables/pallas_call | solution.py:397
  14.0 0.3 collective-permute-done
  14.3 3.6 %collective-permute-start.1 = (f32[8,2048]{1,0:T(8,128)S(1)}, f32[8,2048]{1,0:T(8,128)S(1)}, u32[]{:S(2)}, u32[]{:S(2)}) collective-permute-start(f32[8,2048]{1,0:T(8,128)S(1)} %add.21), channel_id=1, source_target_pairs={{0,8},{4,12},{8,0},{12,4},{1,9},{5,13},{9,1},{13,5},{2,10},{6,14},... | collective-permute-start | bytes 196616 | tf_op jit(solution)/shard_map/ppermute | solution.py:412
  18.0 1.1 %collective-permute-start.3 = (f32[8,2048]{1,0:T(8,128)S(1)}, f32[8,2048]{1,0:T(8,128)S(1)}, u32[]{:S(2)}, u32[]{:S(2)}) collective-permute-start(f32[8,2048]{1,0:T(8,128)S(1)} %add.23), channel_id=1, source_target_pairs={{0,8},{4,12},{8,0},{12,4},{1,9},{5,13},{9,1},{13,5},{2,10},{6,14},... | collective-permute-start | bytes 196616 | tf_op jit(solution)/shard_map/ppermute | solution.py:416
  19.1 2.1 %tables.3 = (bf16[2048,512]{1,0:T(8,128)(2,1)S(1)}, bf16[256,512]{1,0:T(8,128)(2,1)S(1)}) custom-call(s32[8,128]{1,0:T(8,128)S(1)} %get-tuple-element.18.scalar_ref), custom_call_target="tpu_custom_call" | custom-call | tf_op jit(solution)/shard_map/tables/pallas_call | solution.py:397
  21.2 0.0 collective-permute-done.1
  21.2 1.5 %upper.1.upper_ref = f32[16,512]{1,0:T(8,128)S(1)} custom-call(f32[8,2048]{1,0:T(8,128)S(1)} %add.22.side_ref, bf16[2,1024,2048]{2,1,0:T(8,128)(2,1)S(1)} %get-tuple-element.20.hidden_ref, bf16[2048,512]{1,0:T(8,128)(2,1)S(1)} %tables.2.wide_in), custom_call_target="tpu_custom_call" | custom-call | tf_op jit(solution)/shard_map/upper/pallas_call | solution.py:418
  22.8 1.1 %collective-permute-done.3 = f32[8,2048]{1,0:T(8,128)S(1)} collective-permute-done((f32[8,2048]{1,0:T(8,128)S(1)}, f32[8,2048]{1,0:T(8,128)S(1)}, u32[]{:S(2)}, u32[]{:S(2)}) %collective-permute-start.3) | collective-permute-done | bytes 65568 | tf_op jit(solution)/shard_map/ppermute | solution.py:416
  23.9 1.8 %features.1 = (f32[2,4,8,256]{3,2,1,0:T(8,128)S(1)}, f32[2,4,8,256]{3,2,1,0:T(8,128)S(1)}) custom-call(f32[16,512]{1,0:T(8,128)S(1)} %upper.1.upper_ref, f32[8,2048]{1,0:T(8,128)S(1)} %add.24.side_ref, bf16[2,1024,2048]{2,1,0:T(8,128)(2,1)S(1)} %get-tuple-element.23.query_ref, bf16[2,1024,256]{2,1,0:T(8,128)(2,1)S(1)} %get-tuple-element.24.value_ref, ...), custom_call_target="tpu_custom_call" | custom-call | tf_op jit(solution)/shard_map/features/pallas_call | solution.py:429
  25.8 0.1 collective-permute-start.5
  25.9 0.1 collective-permute-start.4
  25.9 2.0 %collective-permute-start.6 = (f32[4,8,256]{2,1,0:T(8,128)S(1)}, f32[4,8,256]{2,1,0:T(8,128)S(1)}, u32[]{:S(2)}, u32[]{:S(2)}) collective-permute-start(f32[4,8,256]{2,1,0:T(8,128)S(1)} %get-tuple-element.30), channel_id=1, source_target_pairs={{0,3},{1,2},{2,1},{3,0},{4,7},{5,6},{6,5},{7,4},{8,11},{9,10},{10,... | collective-permute-start | bytes 98312 | tf_op jit(solution)/shard_map/ppermute | solution.py:442
  28.0 1.9 %collective-permute-done.5 = f32[4,8,256]{2,1,0:T(8,128)S(1)} collective-permute-done((f32[4,8,256]{2,1,0:T(8,128)S(1)}, f32[4,8,256]{2,1,0:T(8,128)S(1)}, u32[]{:S(2)}, u32[]{:S(2)}) %collective-permute-start.5) | collective-permute-done | bytes 32800 | tf_op jit(solution)/shard_map/ppermute | solution.py:441
  29.9 0.0 collective-permute-done.4
  29.9 0.0 collective-permute-done.6
  30.0 2.0 %collective-permute-start.9 = (f32[8,256]{1,0:T(8,128)S(1)}, f32[8,256]{1,0:T(8,128)S(1)}, u32[]{:S(2)}, u32[]{:S(2)}) collective-permute-start(f32[8,256]{1,0:T(8,128)S(1)} %get-tuple-element.32), channel_id=1, source_target_pairs={{0,12},{4,8},{8,4},{12,0},{1,13},{5,9},{9,5},{13,1},{2,14},{6,10},... | collective-permute-start | bytes 24584 | tf_op jit(solution)/shard_map/ppermute | solution.py:445
  32.0 0.0 collective-permute-start.8
  32.0 2.4 %collective-permute-start.7 = (f32[8,256]{1,0:T(8,128)S(1)}, f32[8,256]{1,0:T(8,128)S(1)}, u32[]{:S(2)}, u32[]{:S(2)}) collective-permute-start(f32[8,256]{1,0:T(8,128)S(1)} %get-tuple-element.34), channel_id=1, source_target_pairs={{0,4},{4,0},{8,12},{12,8},{1,5},{5,1},{9,13},{13,9},{2,6},{6,2},{1... | collective-permute-start | bytes 24584 | tf_op jit(solution)/shard_map/ppermute | solution.py:445
  34.4 1.1 %collective-permute-done.9 = f32[8,256]{1,0:T(8,128)S(1)} collective-permute-done((f32[8,256]{1,0:T(8,128)S(1)}, f32[8,256]{1,0:T(8,128)S(1)}, u32[]{:S(2)}, u32[]{:S(2)}) %collective-permute-start.9) | collective-permute-done | bytes 8224 | tf_op jit(solution)/shard_map/ppermute | solution.py:445
  35.5 1.0 %collective-permute-done.8 = f32[8,256]{1,0:T(8,128)S(1)} collective-permute-done((f32[8,256]{1,0:T(8,128)S(1)}, f32[8,256]{1,0:T(8,128)S(1)}, u32[]{:S(2)}, u32[]{:S(2)}) %collective-permute-start.8) | collective-permute-done | bytes 8224 | tf_op jit(solution)/shard_map/ppermute | solution.py:445
  36.5 0.8 %finish.1 = f32[2,1024]{1,0:T(2,128)} custom-call(f32[4,8,256]{2,1,0:T(8,128)S(1)} %pad_maximum_fusion.pieces_ref), custom_call_target="tpu_custom_call" | custom-call | tf_op jit(solution)/shard_map/finish/pallas_call | solution.py:447
  (11 shorter events, 0.1 us)
Async XLA Ops:
  9.0 5.3 %collective-permute-start = (f32[8,2048]{1,0:T(8,128)S(1)}, f32[8,2048]{1,0:T(8,128)S(1)}, u32[]{:S(2)}, u32[]{:S(2)}) collective-permute-start(f32[8,2048]{1,0:T(8,128)S(1)} %get-tuple-element.17), channel_id=1, source_target_pairs={{0,4},{4,0},{8,12},{12,8},{1,5},{5,1},{9,13},{13,9},{2,6},{6,2},{1... | collective-permute-start | bytes 196616 | tf_op jit(solution)/shard_map/ppermute | solution.py:412
  12.1 5.9 %collective-permute-start.2 = (f32[8,2048]{1,0:T(8,128)S(1)}, f32[8,2048]{1,0:T(8,128)S(1)}, u32[]{:S(2)}, u32[]{:S(2)}) collective-permute-start(f32[8,2048]{1,0:T(8,128)S(1)} %get-tuple-element.22), channel_id=1, source_target_pairs={{0,4},{4,0},{8,12},{12,8},{1,5},{5,1},{9,13},{13,9},{2,6},{6,2},{1... | collective-permute-start | bytes 196616 | tf_op jit(solution)/shard_map/ppermute | solution.py:416
  14.3 6.9 %collective-permute-start.1 = (f32[8,2048]{1,0:T(8,128)S(1)}, f32[8,2048]{1,0:T(8,128)S(1)}, u32[]{:S(2)}, u32[]{:S(2)}) collective-permute-start(f32[8,2048]{1,0:T(8,128)S(1)} %add.21), channel_id=1, source_target_pairs={{0,8},{4,12},{8,0},{12,4},{1,9},{5,13},{9,1},{13,5},{2,10},{6,14},... | collective-permute-start | bytes 196616 | tf_op jit(solution)/shard_map/ppermute | solution.py:412
  18.0 5.9 %collective-permute-start.3 = (f32[8,2048]{1,0:T(8,128)S(1)}, f32[8,2048]{1,0:T(8,128)S(1)}, u32[]{:S(2)}, u32[]{:S(2)}) collective-permute-start(f32[8,2048]{1,0:T(8,128)S(1)} %add.23), channel_id=1, source_target_pairs={{0,8},{4,12},{8,0},{12,4},{1,9},{5,13},{9,1},{13,5},{2,10},{6,14},... | collective-permute-start | bytes 196616 | tf_op jit(solution)/shard_map/ppermute | solution.py:416
  25.8 4.2 %collective-permute-start.5 = (f32[4,8,256]{2,1,0:T(8,128)S(1)}, f32[4,8,256]{2,1,0:T(8,128)S(1)}, u32[]{:S(2)}, u32[]{:S(2)}) collective-permute-start(f32[4,8,256]{2,1,0:T(8,128)S(1)} %slice_bitcast_fusion.1), channel_id=1, source_target_pairs={{0,2},{2,0},{1,3},{3,1},{4,6},{6,4},{5,7},{7,5},{8,10},{10,8},{9,1... | collective-permute-start | bytes 98312 | tf_op jit(solution)/shard_map/ppermute | solution.py:441
  25.9 4.1 %collective-permute-start.4 = (f32[4,8,256]{2,1,0:T(8,128)S(1)}, f32[4,8,256]{2,1,0:T(8,128)S(1)}, u32[]{:S(2)}, u32[]{:S(2)}) collective-permute-start(f32[4,8,256]{2,1,0:T(8,128)S(1)} %get-tuple-element.29), channel_id=1, source_target_pairs={{0,1},{1,0},{2,3},{3,2},{4,5},{5,4},{6,7},{7,6},{8,9},{9,8},{10,11... | collective-permute-start | bytes 98312 | tf_op jit(solution)/shard_map/ppermute | solution.py:437
  25.9 4.0 %collective-permute-start.6 = (f32[4,8,256]{2,1,0:T(8,128)S(1)}, f32[4,8,256]{2,1,0:T(8,128)S(1)}, u32[]{:S(2)}, u32[]{:S(2)}) collective-permute-start(f32[4,8,256]{2,1,0:T(8,128)S(1)} %get-tuple-element.30), channel_id=1, source_target_pairs={{0,3},{1,2},{2,1},{3,0},{4,7},{5,6},{6,5},{7,4},{8,11},{9,10},{10,... | collective-permute-start | bytes 98312 | tf_op jit(solution)/shard_map/ppermute | solution.py:442
  30.0 5.6 %collective-permute-start.9 = (f32[8,256]{1,0:T(8,128)S(1)}, f32[8,256]{1,0:T(8,128)S(1)}, u32[]{:S(2)}, u32[]{:S(2)}) collective-permute-start(f32[8,256]{1,0:T(8,128)S(1)} %get-tuple-element.32), channel_id=1, source_target_pairs={{0,12},{4,8},{8,4},{12,0},{1,13},{5,9},{9,5},{13,1},{2,14},{6,10},... | collective-permute-start | bytes 24584 | tf_op jit(solution)/shard_map/ppermute | solution.py:445
  32.0 4.5 %collective-permute-start.8 = (f32[8,256]{1,0:T(8,128)S(1)}, f32[8,256]{1,0:T(8,128)S(1)}, u32[]{:S(2)}, u32[]{:S(2)}) collective-permute-start(f32[8,256]{1,0:T(8,128)S(1)} %get-tuple-element.33), channel_id=1, source_target_pairs={{0,8},{4,12},{8,0},{12,4},{1,9},{5,13},{9,1},{13,5},{2,10},{6,14},... | collective-permute-start | bytes 24584 | tf_op jit(solution)/shard_map/ppermute | solution.py:445
  32.0 4.5 %collective-permute-start.7 = (f32[8,256]{1,0:T(8,128)S(1)}, f32[8,256]{1,0:T(8,128)S(1)}, u32[]{:S(2)}, u32[]{:S(2)}) collective-permute-start(f32[8,256]{1,0:T(8,128)S(1)} %get-tuple-element.34), channel_id=1, source_target_pairs={{0,4},{4,0},{8,12},{12,8},{1,5},{5,1},{9,13},{13,9},{2,6},{6,2},{1... | collective-permute-start | bytes 24584 | tf_op jit(solution)/shard_map/ppermute | solution.py:445

commit v6 on v5

--- a/solution.py
+++ b/solution.py
@@ -142,9 +142,19 @@
     def block_views(item, block):
         return [dst.at[item, pl.ds(block * BLOCK, BLOCK)] for _, dst in arrays]
 
+    for per_array in copies:
+        per_array[0][0].start()
     scalars[0].wait()
+
+    def arrive(item, block):
+        wait_all(
+            [per_array[item][block] for per_array in copies],
+            block_views(item, block),
+            block_sem.at[0, item, block],
+        )
+
     def fetch(item):
-        for block in range(blocks):
+        for block in range(1 if item == 0 else 0, blocks):
 
             @pl.when(start + block * BLOCK < lengths[item])
             def _(block=block):
@@ -197,13 +207,13 @@
             here = pl.ds(block * BLOCK, BLOCK)
             out = pl.ds(item * rows + block * BLOCK, BLOCK)
 
+            if not (item or block):
+                arrive(item, block)
+
             @pl.when(live)
             def _(item=item, block=block, first=first, here=here, out=out):
-                wait_all(
-                    [per_array[item][block] for per_array in copies],
-                    block_views(item, block),
-                    block_sem.at[0, item, block],
-                )
+                if item or block:
+                    arrive(item, block)
                 upper = project(from_query, query_ref, item, here)
                 upper = upper + project(from_value, value_ref, item, here)
                 lower = project(from_hidden, hidden_ref, item, here)
@@ -298,8 +308,8 @@
             for chunk in range(block * per_block, (block + 1) * per_block, 2):
                 at = (chunk % per_block) * width
                 even, odd = wanted[:, at : at + width], wanted[:, at + width : at + 2 * width]
-                kept_ref[spot ^ place, (chunk // 2) ^ shard] = jnp.where(first_half, even, odd)
-                sent_ref[spot ^ place, (chunk // 2) ^ shard] = jnp.where(first_half, odd, even)
+                kept_ref[spot ^ place, lax.rem(chunk // 2 + pieces - shard, pieces)] = jnp.where(first_half, even, odd)
+                sent_ref[spot ^ place, lax.rem(chunk // 2 + pieces - shard, pieces)] = jnp.where(first_half, odd, even)
 
 
 def finish_kernel(pieces_ref, out_ref):
@@ -434,15 +444,22 @@
         compiler_params=pltpu.CompilerParams(vmem_limit_bytes=16 * 2**20),
         name="features",
     )(upper, lower, query, value, wide_query, wide_value, scalars)
-    mine = kept[0] + lax.ppermute(sent[0], "rep", [(0, 1), (1, 0)])
+    moved = []
+
+    def add(value, axis, pairs):
+        moved.append(lax.ppermute(value, axis, pairs))
+
     for hop in range(1, spots):
-        straight = [(i, i ^ hop) for i in range(spots)]
+        add(kept[hop], "dp", [(i, i ^ hop) for i in range(spots)])
+    for hop in range(1, spots):
         crossed = [(2 * i + r, 2 * (i ^ hop) + 1 - r) for i in range(spots) for r in range(2)]
-        mine = mine + lax.ppermute(kept[hop], "dp", straight)
-        mine = mine + lax.ppermute(sent[hop], ("dp", "rep"), crossed)
+        add(sent[hop], ("dp", "rep"), crossed)
+    add(sent[0], "rep", [(0, 1), (1, 0)])
+    mine = sum(moved, kept[0])
     parts = [mine[0]]
-    for hop in range(1, shards):
-        parts.append(lax.ppermute(mine[hop], "fsdp", [(i, i ^ hop) for i in range(shards)]))
+    for hop in range(shards - 1, 0, -1):
+        pairs = [(i, (i + hop) % shards) for i in range(shards)]
+        parts.append(lax.ppermute(mine[hop], "fsdp", pairs))
     parts = jnp.stack(parts)
     return pl.pallas_call(
         finish_kernel,

time: 37.5 us -> 36.5 us (0.973)
  Pallas kernels: 16.4 us -> 15.4 us
    ppermute x2, waiting for transfers between devices: 1.15 us -> 0.01 us  [per_device(): lower = lower + lax.ppermute(lower, 'fsdp', pairs)]
    ppermute x6, waiting for transfers between devices: 4.08 us -> 5.09 us  [the longest x3 2.74 us: per_device(): parts.append(lax.ppermute(mine[hop], 'fsdp', pairs))]
    pallas_call x1, Pallas kernels: 8.31 us -> 7.37 us  [per_device(): pl.pallas_call(side_kernel, out_shape=(pltpu.VMEM((2 * KR, count * rows),...]
    ppermute x2, starting transfers between devices: 6.72 us -> 5.96 us  [per_device(): moved = lax.ppermute(upper, 'fsdp', pairs)]
    ppermute x2, starting transfers between devices: 1.21 us -> 1.81 us  [per_device(): lower = lower + lax.ppermute(lower, 'fsdp', pairs)]
  transfers between devices with their start and end apart: 10 -> 10, of which waited for: 5 -> 7; matrix products, arithmetic and copies ran while one was open for 0% -> 0% of each run, Pallas kernels for 15% -> 15%
where the time goes in v6:
time: 36.5 us
  Pallas kernels  15.4 us (42%)
  starting transfers between devices  14.5 us (40%)
  waiting for transfers between devices  5.74 us (16%)
  between operations  0.74 us (2%)
    pallas_call x1, Pallas kernels, per_device(): pl.pallas_call(side_kernel, out_shape=(pltpu.VMEM((2 * KR, count * rows),...  7.37 us
    ppermute x2, starting transfers between devices, per_device(): moved = lax.ppermute(upper, 'fsdp', pairs)  5.96 us
    ppermute x3, starting transfers between devices, per_device(): parts.append(lax.ppermute(mine[hop], 'fsdp', pairs))  4.5 us
    pallas_call x2, Pallas kernels, make_tables(): pl.pallas_call(functools.partial(table_kernel, 32, which), out_shape=[plt...  3.89 us
    ppermute x3, waiting for transfers between devices, per_device(): parts.append(lax.ppermute(mine[hop], 'fsdp', pairs))  2.74 us
    ppermute x3, waiting for transfers between devices, add(): moved.append(lax.ppermute(value, axis, pairs))  2.34 us
    ppermute x3, starting transfers between devices, add(): moved.append(lax.ppermute(value, axis, pairs))  2.21 us
    pallas_call x1, Pallas kernels, per_device(): pl.pallas_call(feature_kernel, out_shape=[pltpu.VMEM((spots, shards, slot...  1.82 us
  transfers between devices with their start and end apart: 10, of which 7 were waited for; matrix products, arithmetic and copies ran while one was open for 0% of the time, Pallas kernels for 15%

profile of v6, /device:TPU:0, one launch (start us, length us, event | category | flops | bytes accessed | tf_op | source)
XLA Modules:
  0.0 36.5 jit_solution(6335374922351030880)
XLA Ops:
  0.7 7.4 %sides.1 = (f32[8,2048]{1,0:T(8,128)S(1)}, f32[8,2048]{1,0:T(8,128)S(1)}, s32[8,128]{1,0:T(8,128)S(1)}, bf16[2,1024,2048]{2,1,0:T(8,128)(2,1)S(1)}, bf16[2,1024,...) custom-call(bf16[2,1024,2048]{2,1,0:T(8,128)(2,1)} %hidden_hbm.1, bf16[2,1024,2048]{2,1,0:T(8,128)(2,1)} %query_hbm.1, ...), custom_call_target="tpu_custom_call" | custom-call | tf_op jit(solution)/shard_map/sides/pallas_call | solution.py:365
  8.0 3.1 %collective-permute-start = (f32[8,2048]{1,0:T(8,128)S(1)}, f32[8,2048]{1,0:T(8,128)S(1)}, u32[]{:S(2)}, u32[]{:S(2)}) collective-permute-start(f32[8,2048]{1,0:T(8,128)S(1)} %get-tuple-element.17), channel_id=1, source_target_pairs={{0,4},{4,0},{8,12},{12,8},{1,5},{5,1},{9,13},{13,9},{2,6},{6,2},{1... | collective-permute-start | bytes 196616 | tf_op jit(solution)/shard_map/ppermute | solution.py:422
  11.1 0.1 collective-permute-start.2
  11.2 1.8 %tables.2.wide_in = bf16[2048,512]{1,0:T(8,128)(2,1)S(1)} custom-call(s32[8,128]{1,0:T(8,128)S(1)} %get-tuple-element.18.scalar_ref), custom_call_target="tpu_custom_call" | custom-call | tf_op jit(solution)/shard_map/tables/pallas_call | solution.py:407
  13.0 0.6 %collective-permute-done = f32[8,2048]{1,0:T(8,128)S(1)} collective-permute-done((f32[8,2048]{1,0:T(8,128)S(1)}, f32[8,2048]{1,0:T(8,128)S(1)}, u32[]{:S(2)}, u32[]{:S(2)}) %collective-permute-start) | collective-permute-done | bytes 65568 | tf_op jit(solution)/shard_map/ppermute | solution.py:422
  13.6 2.9 %collective-permute-start.1 = (f32[8,2048]{1,0:T(8,128)S(1)}, f32[8,2048]{1,0:T(8,128)S(1)}, u32[]{:S(2)}, u32[]{:S(2)}) collective-permute-start(f32[8,2048]{1,0:T(8,128)S(1)} %add.21), channel_id=1, source_target_pairs={{0,8},{4,12},{8,0},{12,4},{1,9},{5,13},{9,1},{13,5},{2,10},{6,14},... | collective-permute-start | bytes 196616 | tf_op jit(solution)/shard_map/ppermute | solution.py:422
  16.5 1.7 %collective-permute-start.3 = (f32[8,2048]{1,0:T(8,128)S(1)}, f32[8,2048]{1,0:T(8,128)S(1)}, u32[]{:S(2)}, u32[]{:S(2)}) collective-permute-start(f32[8,2048]{1,0:T(8,128)S(1)} %add.23), channel_id=1, source_target_pairs={{0,8},{4,12},{8,0},{12,4},{1,9},{5,13},{9,1},{13,5},{2,10},{6,14},... | collective-permute-start | bytes 196616 | tf_op jit(solution)/shard_map/ppermute | solution.py:426
  18.2 2.1 %tables.3 = (bf16[2048,512]{1,0:T(8,128)(2,1)S(1)}, bf16[256,512]{1,0:T(8,128)(2,1)S(1)}) custom-call(s32[8,128]{1,0:T(8,128)S(1)} %get-tuple-element.18.scalar_ref), custom_call_target="tpu_custom_call" | custom-call | tf_op jit(solution)/shard_map/tables/pallas_call | solution.py:407
  20.3 0.1 collective-permute-done.1
  20.4 1.5 %upper.1.upper_ref = f32[16,512]{1,0:T(8,128)S(1)} custom-call(f32[8,2048]{1,0:T(8,128)S(1)} %add.22.side_ref, bf16[2,1024,2048]{2,1,0:T(8,128)(2,1)S(1)} %get-tuple-element.20.hidden_ref, bf16[2048,512]{1,0:T(8,128)(2,1)S(1)} %tables.2.wide_in), custom_call_target="tpu_custom_call" | custom-call | tf_op jit(solution)/shard_map/upper/pallas_call | solution.py:428
  22.0 1.8 %features.1 = (f32[2,4,8,256]{3,2,1,0:T(8,128)S(1)}, f32[2,4,8,256]{3,2,1,0:T(8,128)S(1)}) custom-call(f32[16,512]{1,0:T(8,128)S(1)} %upper.1.upper_ref, f32[8,2048]{1,0:T(8,128)S(1)} %add.24.side_ref, bf16[2,1024,2048]{2,1,0:T(8,128)(2,1)S(1)} %get-tuple-element.23.query_ref, bf16[2,1024,256]{2,1,0:T(8,128)(2,1)S(1)} %get-tuple-element.24.value_ref, ...), custom_call_target="tpu_custom_call" | custom-call | tf_op jit(solution)/shard_map/features/pallas_call | solution.py:439
  23.8 0.9 %collective-permute-start.4 = (f32[4,8,256]{2,1,0:T(8,128)S(1)}, f32[4,8,256]{2,1,0:T(8,128)S(1)}, u32[]{:S(2)}, u32[]{:S(2)}) collective-permute-start(f32[4,8,256]{2,1,0:T(8,128)S(1)} %slice_bitcast_fusion.2), channel_id=1, source_target_pairs={{0,2},{2,0},{1,3},{3,1},{4,6},{6,4},{5,7},{7,5},{8,10},{10,8},{9,1... | collective-permute-start | bytes 98312 | tf_op jit(solution)/shard_map/ppermute | solution.py:450
  24.7 0.0 collective-permute-start.5
  24.7 1.3 %collective-permute-start.6 = (f32[4,8,256]{2,1,0:T(8,128)S(1)}, f32[4,8,256]{2,1,0:T(8,128)S(1)}, u32[]{:S(2)}, u32[]{:S(2)}) collective-permute-start(f32[4,8,256]{2,1,0:T(8,128)S(1)} %get-tuple-element.30), channel_id=1, source_target_pairs={{0,1},{1,0},{2,3},{3,2},{4,5},{5,4},{6,7},{7,6},{8,9},{9,8},{10,11... | collective-permute-start | bytes 98312 | tf_op jit(solution)/shard_map/ppermute | solution.py:450
  26.0 1.9 %collective-permute-done.4 = f32[4,8,256]{2,1,0:T(8,128)S(1)} collective-permute-done((f32[4,8,256]{2,1,0:T(8,128)S(1)}, f32[4,8,256]{2,1,0:T(8,128)S(1)}, u32[]{:S(2)}, u32[]{:S(2)}) %collective-permute-start.4) | collective-permute-done | bytes 32800 | tf_op jit(solution)/shard_map/ppermute | solution.py:450
  27.9 0.4 %collective-permute-done.5 = f32[4,8,256]{2,1,0:T(8,128)S(1)} collective-permute-done((f32[4,8,256]{2,1,0:T(8,128)S(1)}, f32[4,8,256]{2,1,0:T(8,128)S(1)}, u32[]{:S(2)}, u32[]{:S(2)}) %collective-permute-start.5) | collective-permute-done | bytes 32800 | tf_op jit(solution)/shard_map/ppermute | solution.py:450
  28.4 0.0 collective-permute-done.6
  28.4 1.9 %collective-permute-start.9 = (f32[8,256]{1,0:T(8,128)S(1)}, f32[8,256]{1,0:T(8,128)S(1)}, u32[]{:S(2)}, u32[]{:S(2)}) collective-permute-start(f32[8,256]{1,0:T(8,128)S(1)} %get-tuple-element.32), channel_id=1, source_target_pairs={{0,4},{4,8},{8,12},{12,0},{1,5},{5,9},{9,13},{13,1},{2,6},{6,10},{... | collective-permute-start | bytes 24584 | tf_op jit(solution)/shard_map/ppermute | solution.py:462
  30.3 1.7 %collective-permute-start.8 = (f32[8,256]{1,0:T(8,128)S(1)}, f32[8,256]{1,0:T(8,128)S(1)}, u32[]{:S(2)}, u32[]{:S(2)}) collective-permute-start(f32[8,256]{1,0:T(8,128)S(1)} %get-tuple-element.33), channel_id=1, source_target_pairs={{0,8},{4,12},{8,0},{12,4},{1,9},{5,13},{9,1},{13,5},{2,10},{6,14},... | collective-permute-start | bytes 24584 | tf_op jit(solution)/shard_map/ppermute | solution.py:462
  32.0 0.9 %collective-permute-start.7 = (f32[8,256]{1,0:T(8,128)S(1)}, f32[8,256]{1,0:T(8,128)S(1)}, u32[]{:S(2)}, u32[]{:S(2)}) collective-permute-start(f32[8,256]{1,0:T(8,128)S(1)} %get-tuple-element.34), channel_id=1, source_target_pairs={{0,12},{4,0},{8,4},{12,8},{1,13},{5,1},{9,5},{13,9},{2,14},{6,2},{... | collective-permute-start | bytes 24584 | tf_op jit(solution)/shard_map/ppermute | solution.py:462
  32.9 1.1 %collective-permute-done.9 = f32[8,256]{1,0:T(8,128)S(1)} collective-permute-done((f32[8,256]{1,0:T(8,128)S(1)}, f32[8,256]{1,0:T(8,128)S(1)}, u32[]{:S(2)}, u32[]{:S(2)}) %collective-permute-start.9) | collective-permute-done | bytes 8224 | tf_op jit(solution)/shard_map/ppermute | solution.py:462
  34.0 0.8 %collective-permute-done.8 = f32[8,256]{1,0:T(8,128)S(1)} collective-permute-done((f32[8,256]{1,0:T(8,128)S(1)}, f32[8,256]{1,0:T(8,128)S(1)}, u32[]{:S(2)}, u32[]{:S(2)}) %collective-permute-start.8) | collective-permute-done | bytes 8224 | tf_op jit(solution)/shard_map/ppermute | solution.py:462
  34.8 0.8 %collective-permute-done.7 = f32[8,256]{1,0:T(8,128)S(1)} collective-permute-done((f32[8,256]{1,0:T(8,128)S(1)}, f32[8,256]{1,0:T(8,128)S(1)}, u32[]{:S(2)}, u32[]{:S(2)}) %collective-permute-start.7) | collective-permute-done | bytes 8224 | tf_op jit(solution)/shard_map/ppermute | solution.py:462
  35.7 0.8 %finish.1 = f32[2,1024]{1,0:T(2,128)} custom-call(f32[4,8,256]{2,1,0:T(8,128)S(1)} %pad_maximum_fusion.pieces_ref), custom_call_target="tpu_custom_call" | custom-call | tf_op jit(solution)/shard_map/finish/pallas_call | solution.py:464
  (11 shorter events, 0.1 us)
Async XLA Ops:
  8.0 5.6 %collective-permute-start = (f32[8,2048]{1,0:T(8,128)S(1)}, f32[8,2048]{1,0:T(8,128)S(1)}, u32[]{:S(2)}, u32[]{:S(2)}) collective-permute-start(f32[8,2048]{1,0:T(8,128)S(1)} %get-tuple-element.17), channel_id=1, source_target_pairs={{0,4},{4,0},{8,12},{12,8},{1,5},{5,1},{9,13},{13,9},{2,6},{6,2},{1... | collective-permute-start | bytes 196616 | tf_op jit(solution)/shard_map/ppermute | solution.py:422
  11.1 5.4 %collective-permute-start.2 = (f32[8,2048]{1,0:T(8,128)S(1)}, f32[8,2048]{1,0:T(8,128)S(1)}, u32[]{:S(2)}, u32[]{:S(2)}) collective-permute-start(f32[8,2048]{1,0:T(8,128)S(1)} %get-tuple-element.22), channel_id=1, source_target_pairs={{0,4},{4,0},{8,12},{12,8},{1,5},{5,1},{9,13},{13,9},{2,6},{6,2},{1... | collective-permute-start | bytes 196616 | tf_op jit(solution)/shard_map/ppermute | solution.py:426
  13.6 6.8 %collective-permute-start.1 = (f32[8,2048]{1,0:T(8,128)S(1)}, f32[8,2048]{1,0:T(8,128)S(1)}, u32[]{:S(2)}, u32[]{:S(2)}) collective-permute-start(f32[8,2048]{1,0:T(8,128)S(1)} %add.21), channel_id=1, source_target_pairs={{0,8},{4,12},{8,0},{12,4},{1,9},{5,13},{9,1},{13,5},{2,10},{6,14},... | collective-permute-start | bytes 196616 | tf_op jit(solution)/shard_map/ppermute | solution.py:422
  16.5 5.5 %collective-permute-start.3 = (f32[8,2048]{1,0:T(8,128)S(1)}, f32[8,2048]{1,0:T(8,128)S(1)}, u32[]{:S(2)}, u32[]{:S(2)}) collective-permute-start(f32[8,2048]{1,0:T(8,128)S(1)} %add.23), channel_id=1, source_target_pairs={{0,8},{4,12},{8,0},{12,4},{1,9},{5,13},{9,1},{13,5},{2,10},{6,14},... | collective-permute-start | bytes 196616 | tf_op jit(solution)/shard_map/ppermute | solution.py:426
  23.8 4.1 %collective-permute-start.4 = (f32[4,8,256]{2,1,0:T(8,128)S(1)}, f32[4,8,256]{2,1,0:T(8,128)S(1)}, u32[]{:S(2)}, u32[]{:S(2)}) collective-permute-start(f32[4,8,256]{2,1,0:T(8,128)S(1)} %slice_bitcast_fusion.2), channel_id=1, source_target_pairs={{0,2},{2,0},{1,3},{3,1},{4,6},{6,4},{5,7},{7,5},{8,10},{10,8},{9,1... | collective-permute-start | bytes 98312 | tf_op jit(solution)/shard_map/ppermute | solution.py:450
  24.7 3.7 %collective-permute-start.5 = (f32[4,8,256]{2,1,0:T(8,128)S(1)}, f32[4,8,256]{2,1,0:T(8,128)S(1)}, u32[]{:S(2)}, u32[]{:S(2)}) collective-permute-start(f32[4,8,256]{2,1,0:T(8,128)S(1)} %get-tuple-element.29), channel_id=1, source_target_pairs={{0,3},{1,2},{2,1},{3,0},{4,7},{5,6},{6,5},{7,4},{8,11},{9,10},{10,... | collective-permute-start | bytes 98312 | tf_op jit(solution)/shard_map/ppermute | solution.py:450
  24.7 3.7 %collective-permute-start.6 = (f32[4,8,256]{2,1,0:T(8,128)S(1)}, f32[4,8,256]{2,1,0:T(8,128)S(1)}, u32[]{:S(2)}, u32[]{:S(2)}) collective-permute-start(f32[4,8,256]{2,1,0:T(8,128)S(1)} %get-tuple-element.30), channel_id=1, source_target_pairs={{0,1},{1,0},{2,3},{3,2},{4,5},{5,4},{6,7},{7,6},{8,9},{9,8},{10,11... | collective-permute-start | bytes 98312 | tf_op jit(solution)/shard_map/ppermute | solution.py:450
  28.4 5.6 %collective-permute-start.9 = (f32[8,256]{1,0:T(8,128)S(1)}, f32[8,256]{1,0:T(8,128)S(1)}, u32[]{:S(2)}, u32[]{:S(2)}) collective-permute-start(f32[8,256]{1,0:T(8,128)S(1)} %get-tuple-element.32), channel_id=1, source_target_pairs={{0,4},{4,8},{8,12},{12,0},{1,5},{5,9},{9,13},{13,1},{2,6},{6,10},{... | collective-permute-start | bytes 24584 | tf_op jit(solution)/shard_map/ppermute | solution.py:462
  30.3 4.5 %collective-permute-start.8 = (f32[8,256]{1,0:T(8,128)S(1)}, f32[8,256]{1,0:T(8,128)S(1)}, u32[]{:S(2)}, u32[]{:S(2)}) collective-permute-start(f32[8,256]{1,0:T(8,128)S(1)} %get-tuple-element.33), channel_id=1, source_target_pairs={{0,8},{4,12},{8,0},{12,4},{1,9},{5,13},{9,1},{13,5},{2,10},{6,14},... | collective-permute-start | bytes 24584 | tf_op jit(solution)/shard_map/ppermute | solution.py:462
  32.0 3.7 %collective-permute-start.7 = (f32[8,256]{1,0:T(8,128)S(1)}, f32[8,256]{1,0:T(8,128)S(1)}, u32[]{:S(2)}, u32[]{:S(2)}) collective-permute-start(f32[8,256]{1,0:T(8,128)S(1)} %get-tuple-element.34), channel_id=1, source_target_pairs={{0,12},{4,0},{8,4},{12,8},{1,13},{5,1},{9,5},{13,9},{2,14},{6,2},{... | collective-permute-start | bytes 24584 | tf_op jit(solution)/shard_map/ppermute | solution.py:462

commit v7 on v6

--- a/solution.py
+++ b/solution.py
@@ -105,12 +105,12 @@
         )
     ]
     factors = [
-        pltpu.make_async_copy(src, dst, factor_sem.at[sem_of(dst)])
-        for src, dst in (
-            (query_up_hbm, query_up),
-            (value_up_hbm, value_up),
-            (query_down_hbm, query_down),
-            (value_down_hbm, value_down),
+        pltpu.make_async_copy(src, dst, factor_sem.at[k])
+        for src, dst, k in (
+            (query_up_hbm, query_up, 0),
+            (query_down_hbm, query_down, 0),
+            (value_down_hbm, value_down, 0),
+            (value_up_hbm, value_up, 1),
         )
     ]
     for copy in scalars + factors:
@@ -162,7 +162,8 @@
                     per_array[item][block].start()
 
     fetch(0)
-    wait_all(factors, (query_up, value_up, query_down, value_down), factor_sem.at[0])
+    wait_all(factors[:3], (query_up, query_down, value_down), factor_sem.at[0])
+    factors[3].wait()
     for copy in scalars[1:]:
         copy.wait()
     seed_value = seed[0]
@@ -420,10 +421,11 @@
     while hop < shards:
         pairs = [(i, i ^ hop) for i in range(shards)]
         moved = lax.ppermute(upper, "fsdp", pairs)
+        lower_moved = lax.ppermute(lower, "fsdp", pairs)
         if hop == 1:
-            moved, wide_in = lax.optimization_barrier((moved, wide_in))
+            lower_moved, wide_in = lax.optimization_barrier((lower_moved, wide_in))
         upper = upper + moved
-        lower = lower + lax.ppermute(lower, "fsdp", pairs)
+        lower = lower + lower_moved
         hop *= 2
     upper = pl.pallas_call(
         upper_kernel,

time: 36.5 us -> 37.1 us (1.016); the launches traced: 36.5 us -> 36.5 us
  Pallas kernels: 15.4 us -> 14.8 us
  waiting for transfers between devices: 5.74 us -> 6.23 us
    ppermute x3, waiting for transfers between devices: 2.34 us -> 3.15 us  [add(): moved.append(lax.ppermute(value, axis, pairs))]
    pallas_call x1, Pallas kernels: 7.37 us -> 6.79 us  [per_device(): pl.pallas_call(side_kernel, out_shape=(pltpu.VMEM((2 * KR, count * rows),...]
where the time goes in v7:
time: 37.1 us; the launch traced here: 36.5 us
  Pallas kernels  14.8 us (40%)
  starting transfers between devices  14.6 us (39%)
  waiting for transfers between devices  6.23 us (17%)
  between operations  0.74 us (2%)
    pallas_call x1, Pallas kernels, per_device(): pl.pallas_call(side_kernel, out_shape=(pltpu.VMEM((2 * KR, count * rows),...  6.79 us
    ppermute x2, starting transfers between devices, per_device(): moved = lax.ppermute(upper, 'fsdp', pairs)  6.02 us
    ppermute x3, starting transfers between devices, per_device(): parts.append(lax.ppermute(mine[hop], 'fsdp', pairs))  4.57 us
    pallas_call x2, Pallas kernels, make_tables(): pl.pallas_call(functools.partial(table_kernel, 32, which), out_shape=[plt...  3.89 us
    ppermute x3, waiting for transfers between devices, add(): moved.append(lax.ppermute(value, axis, pairs))  3.15 us
    ppermute x3, waiting for transfers between devices, per_device(): parts.append(lax.ppermute(mine[hop], 'fsdp', pairs))  2.49 us
    ppermute x3, starting transfers between devices, add(): moved.append(lax.ppermute(value, axis, pairs))  2.27 us
    pallas_call x1, Pallas kernels, per_device(): pl.pallas_call(feature_kernel, out_shape=[pltpu.VMEM((spots, shards, slot...  1.82 us
  transfers between devices with their start and end apart: 10, of which 7 were waited for; matrix products, arithmetic and copies ran while one was open for 0% of the time, Pallas kernels for 15%

profile of v7, /device:TPU:0, one launch (start us, length us, event | category | flops | bytes accessed | tf_op | source)
XLA Modules:
  0.0 36.5 jit_solution(10171318977048703743)
XLA Ops:
  0.7 6.8 %sides.1 = (f32[8,2048]{1,0:T(8,128)S(1)}, f32[8,2048]{1,0:T(8,128)S(1)}, s32[8,128]{1,0:T(8,128)S(1)}, bf16[2,1024,2048]{2,1,0:T(8,128)(2,1)S(1)}, bf16[2,1024,...) custom-call(bf16[2,1024,2048]{2,1,0:T(8,128)(2,1)} %hidden_hbm.1, bf16[2,1024,2048]{2,1,0:T(8,128)(2,1)} %query_hbm.1, ...), custom_call_target="tpu_custom_call" | custom-call | tf_op jit(solution)/shard_map/sides/pallas_call | solution.py:366
  7.4 3.1 %collective-permute-start = (f32[8,2048]{1,0:T(8,128)S(1)}, f32[8,2048]{1,0:T(8,128)S(1)}, u32[]{:S(2)}, u32[]{:S(2)}) collective-permute-start(f32[8,2048]{1,0:T(8,128)S(1)} %get-tuple-element.17), channel_id=1, source_target_pairs={{0,4},{4,0},{8,12},{12,8},{1,5},{5,1},{9,13},{13,9},{2,6},{6,2},{1... | collective-permute-start | bytes 196616 | tf_op jit(solution)/shard_map/ppermute | solution.py:423
  10.5 0.1 collective-permute-start.2
  10.6 1.8 %tables.2.wide_in = bf16[2048,512]{1,0:T(8,128)(2,1)S(1)} custom-call(s32[8,128]{1,0:T(8,128)S(1)} %get-tuple-element.20.scalar_ref), custom_call_target="tpu_custom_call" | custom-call | tf_op jit(solution)/shard_map/tables/pallas_call | solution.py:408
  12.4 0.5 %collective-permute-done = f32[8,2048]{1,0:T(8,128)S(1)} collective-permute-done((f32[8,2048]{1,0:T(8,128)S(1)}, f32[8,2048]{1,0:T(8,128)S(1)}, u32[]{:S(2)}, u32[]{:S(2)}) %collective-permute-start) | collective-permute-done | bytes 65568 | tf_op jit(solution)/shard_map/ppermute | solution.py:423
  13.0 2.9 %collective-permute-start.1 = (f32[8,2048]{1,0:T(8,128)S(1)}, f32[8,2048]{1,0:T(8,128)S(1)}, u32[]{:S(2)}, u32[]{:S(2)}) collective-permute-start(f32[8,2048]{1,0:T(8,128)S(1)} %add.21), channel_id=1, source_target_pairs={{0,8},{4,12},{8,0},{12,4},{1,9},{5,13},{9,1},{13,5},{2,10},{6,14},... | collective-permute-start | bytes 196616 | tf_op jit(solution)/shard_map/ppermute | solution.py:423
  15.9 0.0 collective-permute-done.2
  15.9 1.7 %collective-permute-start.3 = (f32[8,2048]{1,0:T(8,128)S(1)}, f32[8,2048]{1,0:T(8,128)S(1)}, u32[]{:S(2)}, u32[]{:S(2)}) collective-permute-start(f32[8,2048]{1,0:T(8,128)S(1)} %add.23), channel_id=1, source_target_pairs={{0,8},{4,12},{8,0},{12,4},{1,9},{5,13},{9,1},{13,5},{2,10},{6,14},... | collective-permute-start | bytes 196616 | tf_op jit(solution)/shard_map/ppermute | solution.py:424
  17.6 2.1 %tables.3 = (bf16[2048,512]{1,0:T(8,128)(2,1)S(1)}, bf16[256,512]{1,0:T(8,128)(2,1)S(1)}) custom-call(s32[8,128]{1,0:T(8,128)S(1)} %get-tuple-element.20.scalar_ref), custom_call_target="tpu_custom_call" | custom-call | tf_op jit(solution)/shard_map/tables/pallas_call | solution.py:408
  19.7 0.1 collective-permute-done.1
  19.8 1.5 %upper.1.upper_ref = f32[16,512]{1,0:T(8,128)S(1)} custom-call(f32[8,2048]{1,0:T(8,128)S(1)} %add.22.side_ref, bf16[2,1024,2048]{2,1,0:T(8,128)(2,1)S(1)} %get-tuple-element.18.hidden_ref, bf16[2048,512]{1,0:T(8,128)(2,1)S(1)} %tables.2.wide_in), custom_call_target="tpu_custom_call" | custom-call | tf_op jit(solution)/shard_map/upper/pallas_call | solution.py:430
  21.3 1.8 %features.1 = (f32[2,4,8,256]{3,2,1,0:T(8,128)S(1)}, f32[2,4,8,256]{3,2,1,0:T(8,128)S(1)}) custom-call(f32[16,512]{1,0:T(8,128)S(1)} %upper.1.upper_ref, f32[8,2048]{1,0:T(8,128)S(1)} %add.24.side_ref, bf16[2,1024,2048]{2,1,0:T(8,128)(2,1)S(1)} %get-tuple-element.23.query_ref, bf16[2,1024,256]{2,1,0:T(8,128)(2,1)S(1)} %get-tuple-element.24.value_ref, ...), custom_call_target="tpu_custom_call" | custom-call | tf_op jit(solution)/shard_map/features/pallas_call | solution.py:441
  23.2 2.1 %collective-permute-start.4 = (f32[4,8,256]{2,1,0:T(8,128)S(1)}, f32[4,8,256]{2,1,0:T(8,128)S(1)}, u32[]{:S(2)}, u32[]{:S(2)}) collective-permute-start(f32[4,8,256]{2,1,0:T(8,128)S(1)} %slice_bitcast_fusion.2), channel_id=1, source_target_pairs={{0,2},{2,0},{1,3},{3,1},{4,6},{6,4},{5,7},{7,5},{8,10},{10,8},{9,1... | collective-permute-start | bytes 98312 | tf_op jit(solution)/shard_map/ppermute | solution.py:452
  25.3 0.2 collective-permute-start.6
  25.5 1.7 %collective-permute-done.4 = f32[4,8,256]{2,1,0:T(8,128)S(1)} collective-permute-done((f32[4,8,256]{2,1,0:T(8,128)S(1)}, f32[4,8,256]{2,1,0:T(8,128)S(1)}, u32[]{:S(2)}, u32[]{:S(2)}) %collective-permute-start.4) | collective-permute-done | bytes 32800 | tf_op jit(solution)/shard_map/ppermute | solution.py:452
  27.2 1.4 %collective-permute-done.5 = f32[4,8,256]{2,1,0:T(8,128)S(1)} collective-permute-done((f32[4,8,256]{2,1,0:T(8,128)S(1)}, f32[4,8,256]{2,1,0:T(8,128)S(1)}, u32[]{:S(2)}, u32[]{:S(2)}) %collective-permute-start.5) | collective-permute-done | bytes 32800 | tf_op jit(solution)/shard_map/ppermute | solution.py:452
  28.6 0.0 collective-permute-done.6
  28.6 1.4 %collective-permute-start.9 = (f32[8,256]{1,0:T(8,128)S(1)}, f32[8,256]{1,0:T(8,128)S(1)}, u32[]{:S(2)}, u32[]{:S(2)}) collective-permute-start(f32[8,256]{1,0:T(8,128)S(1)} %get-tuple-element.32), channel_id=1, source_target_pairs={{0,4},{4,8},{8,12},{12,0},{1,5},{5,9},{9,13},{13,1},{2,6},{6,10},{... | collective-permute-start | bytes 24584 | tf_op jit(solution)/shard_map/ppermute | solution.py:464
  30.1 2.0 %collective-permute-start.8 = (f32[8,256]{1,0:T(8,128)S(1)}, f32[8,256]{1,0:T(8,128)S(1)}, u32[]{:S(2)}, u32[]{:S(2)}) collective-permute-start(f32[8,256]{1,0:T(8,128)S(1)} %get-tuple-element.33), channel_id=1, source_target_pairs={{0,8},{4,12},{8,0},{12,4},{1,9},{5,13},{9,1},{13,5},{2,10},{6,14},... | collective-permute-start | bytes 24584 | tf_op jit(solution)/shard_map/ppermute | solution.py:464
  32.0 1.2 %collective-permute-start.7 = (f32[8,256]{1,0:T(8,128)S(1)}, f32[8,256]{1,0:T(8,128)S(1)}, u32[]{:S(2)}, u32[]{:S(2)}) collective-permute-start(f32[8,256]{1,0:T(8,128)S(1)} %get-tuple-element.34), channel_id=1, source_target_pairs={{0,12},{4,0},{8,4},{12,8},{1,13},{5,1},{9,5},{13,9},{2,14},{6,2},{... | collective-permute-start | bytes 24584 | tf_op jit(solution)/shard_map/ppermute | solution.py:464
  33.2 0.9 %collective-permute-done.9 = f32[8,256]{1,0:T(8,128)S(1)} collective-permute-done((f32[8,256]{1,0:T(8,128)S(1)}, f32[8,256]{1,0:T(8,128)S(1)}, u32[]{:S(2)}, u32[]{:S(2)}) %collective-permute-start.9) | collective-permute-done | bytes 8224 | tf_op jit(solution)/shard_map/ppermute | solution.py:464
  34.1 0.5 %collective-permute-done.8 = f32[8,256]{1,0:T(8,128)S(1)} collective-permute-done((f32[8,256]{1,0:T(8,128)S(1)}, f32[8,256]{1,0:T(8,128)S(1)}, u32[]{:S(2)}, u32[]{:S(2)}) %collective-permute-start.8) | collective-permute-done | bytes 8224 | tf_op jit(solution)/shard_map/ppermute | solution.py:464
  34.6 1.1 %collective-permute-done.7 = f32[8,256]{1,0:T(8,128)S(1)} collective-permute-done((f32[8,256]{1,0:T(8,128)S(1)}, f32[8,256]{1,0:T(8,128)S(1)}, u32[]{:S(2)}, u32[]{:S(2)}) %collective-permute-start.7) | collective-permute-done | bytes 8224 | tf_op jit(solution)/shard_map/ppermute | solution.py:464
  35.7 0.8 %finish.1 = f32[2,1024]{1,0:T(2,128)} custom-call(f32[4,8,256]{2,1,0:T(8,128)S(1)} %pad_maximum_fusion.pieces_ref), custom_call_target="tpu_custom_call" | custom-call | tf_op jit(solution)/shard_map/finish/pallas_call | solution.py:466
  (11 shorter events, 0.1 us)
Async XLA Ops:
  7.4 5.5 %collective-permute-start = (f32[8,2048]{1,0:T(8,128)S(1)}, f32[8,2048]{1,0:T(8,128)S(1)}, u32[]{:S(2)}, u32[]{:S(2)}) collective-permute-start(f32[8,2048]{1,0:T(8,128)S(1)} %get-tuple-element.17), channel_id=1, source_target_pairs={{0,4},{4,0},{8,12},{12,8},{1,5},{5,1},{9,13},{13,9},{2,6},{6,2},{1... | collective-permute-start | bytes 196616 | tf_op jit(solution)/shard_map/ppermute | solution.py:423
  10.5 5.4 %collective-permute-start.2 = (f32[8,2048]{1,0:T(8,128)S(1)}, f32[8,2048]{1,0:T(8,128)S(1)}, u32[]{:S(2)}, u32[]{:S(2)}) collective-permute-start(f32[8,2048]{1,0:T(8,128)S(1)} %get-tuple-element.19), channel_id=1, source_target_pairs={{0,4},{4,0},{8,12},{12,8},{1,5},{5,1},{9,13},{13,9},{2,6},{6,2},{1... | collective-permute-start | bytes 196616 | tf_op jit(solution)/shard_map/ppermute | solution.py:424
  13.0 6.8 %collective-permute-start.1 = (f32[8,2048]{1,0:T(8,128)S(1)}, f32[8,2048]{1,0:T(8,128)S(1)}, u32[]{:S(2)}, u32[]{:S(2)}) collective-permute-start(f32[8,2048]{1,0:T(8,128)S(1)} %add.21), channel_id=1, source_target_pairs={{0,8},{4,12},{8,0},{12,4},{1,9},{5,13},{9,1},{13,5},{2,10},{6,14},... | collective-permute-start | bytes 196616 | tf_op jit(solution)/shard_map/ppermute | solution.py:423
  15.9 5.4 %collective-permute-start.3 = (f32[8,2048]{1,0:T(8,128)S(1)}, f32[8,2048]{1,0:T(8,128)S(1)}, u32[]{:S(2)}, u32[]{:S(2)}) collective-permute-start(f32[8,2048]{1,0:T(8,128)S(1)} %add.23), channel_id=1, source_target_pairs={{0,8},{4,12},{8,0},{12,4},{1,9},{5,13},{9,1},{13,5},{2,10},{6,14},... | collective-permute-start | bytes 196616 | tf_op jit(solution)/shard_map/ppermute | solution.py:424
  23.2 4.0 %collective-permute-start.4 = (f32[4,8,256]{2,1,0:T(8,128)S(1)}, f32[4,8,256]{2,1,0:T(8,128)S(1)}, u32[]{:S(2)}, u32[]{:S(2)}) collective-permute-start(f32[4,8,256]{2,1,0:T(8,128)S(1)} %slice_bitcast_fusion.2), channel_id=1, source_target_pairs={{0,2},{2,0},{1,3},{3,1},{4,6},{6,4},{5,7},{7,5},{8,10},{10,8},{9,1... | collective-permute-start | bytes 98312 | tf_op jit(solution)/shard_map/ppermute | solution.py:452
  25.3 3.3 %collective-permute-start.5 = (f32[4,8,256]{2,1,0:T(8,128)S(1)}, f32[4,8,256]{2,1,0:T(8,128)S(1)}, u32[]{:S(2)}, u32[]{:S(2)}) collective-permute-start(f32[4,8,256]{2,1,0:T(8,128)S(1)} %get-tuple-element.29), channel_id=1, source_target_pairs={{0,3},{1,2},{2,1},{3,0},{4,7},{5,6},{6,5},{7,4},{8,11},{9,10},{10,... | collective-permute-start | bytes 98312 | tf_op jit(solution)/shard_map/ppermute | solution.py:452
  25.3 3.3 %collective-permute-start.6 = (f32[4,8,256]{2,1,0:T(8,128)S(1)}, f32[4,8,256]{2,1,0:T(8,128)S(1)}, u32[]{:S(2)}, u32[]{:S(2)}) collective-permute-start(f32[4,8,256]{2,1,0:T(8,128)S(1)} %get-tuple-element.30), channel_id=1, source_target_pairs={{0,1},{1,0},{2,3},{3,2},{4,5},{5,4},{6,7},{7,6},{8,9},{9,8},{10,11... | collective-permute-start | bytes 98312 | tf_op jit(solution)/shard_map/ppermute | solution.py:452
  28.6 5.5 %collective-permute-start.9 = (f32[8,256]{1,0:T(8,128)S(1)}, f32[8,256]{1,0:T(8,128)S(1)}, u32[]{:S(2)}, u32[]{:S(2)}) collective-permute-start(f32[8,256]{1,0:T(8,128)S(1)} %get-tuple-element.32), channel_id=1, source_target_pairs={{0,4},{4,8},{8,12},{12,0},{1,5},{5,9},{9,13},{13,1},{2,6},{6,10},{... | collective-permute-start | bytes 24584 | tf_op jit(solution)/shard_map/ppermute | solution.py:464
  30.1 4.5 %collective-permute-start.8 = (f32[8,256]{1,0:T(8,128)S(1)}, f32[8,256]{1,0:T(8,128)S(1)}, u32[]{:S(2)}, u32[]{:S(2)}) collective-permute-start(f32[8,256]{1,0:T(8,128)S(1)} %get-tuple-element.33), channel_id=1, source_target_pairs={{0,8},{4,12},{8,0},{12,4},{1,9},{5,13},{9,1},{13,5},{2,10},{6,14},... | collective-permute-start | bytes 24584 | tf_op jit(solution)/shard_map/ppermute | solution.py:464
  32.0 3.7 %collective-permute-start.7 = (f32[8,256]{1,0:T(8,128)S(1)}, f32[8,256]{1,0:T(8,128)S(1)}, u32[]{:S(2)}, u32[]{:S(2)}) collective-permute-start(f32[8,256]{1,0:T(8,128)S(1)} %get-tuple-element.34), channel_id=1, source_target_pairs={{0,12},{4,0},{8,4},{12,8},{1,13},{5,1},{9,5},{13,9},{2,14},{6,2},{... | collective-permute-start | bytes 24584 | tf_op jit(solution)/shard_map/ppermute | solution.py:464

commit v8 on v7

--- a/solution.py
+++ b/solution.py
@@ -452,11 +452,11 @@
         moved.append(lax.ppermute(value, axis, pairs))
 
     for hop in range(1, spots):
-        add(kept[hop], "dp", [(i, i ^ hop) for i in range(spots)])
-    for hop in range(1, spots):
         crossed = [(2 * i + r, 2 * (i ^ hop) + 1 - r) for i in range(spots) for r in range(2)]
         add(sent[hop], ("dp", "rep"), crossed)
     add(sent[0], "rep", [(0, 1), (1, 0)])
+    for hop in range(1, spots):
+        add(kept[hop], "dp", [(i, i ^ hop) for i in range(spots)])
     mine = sum(moved, kept[0])
     parts = [mine[0]]
     for hop in range(shards - 1, 0, -1):

time: 37.1 us -> 36.7 us (0.989); the launches traced: 36.5 us -> 36.5 us
  Pallas kernels: 14.8 us -> 15.4 us
  waiting for transfers between devices: 6.23 us -> 5.72 us
    ppermute x3, waiting for transfers between devices: 3.15 us -> 2.2 us  [add(): moved.append(lax.ppermute(value, axis, pairs))]
    pallas_call x1, Pallas kernels: 6.79 us -> 7.37 us  [per_device(): pl.pallas_call(side_kernel, out_shape=(pltpu.VMEM((2 * KR, count * rows),...]
    ppermute x2, starting transfers between devices: 6.02 us -> 6.56 us  [per_device(): moved = lax.ppermute(upper, 'fsdp', pairs)]
    ppermute x2, starting transfers between devices: 1.75 us -> 1.27 us  [per_device(): lower_moved = lax.ppermute(lower, 'fsdp', pairs)]
    ppermute x2, waiting for transfers between devices: 0.01 us -> 0.4 us  [per_device(): lower_moved = lax.ppermute(lower, 'fsdp', pairs)]
where the time goes in v8:
time: 36.7 us; the launch traced here: 36.5 us
  Pallas kernels  15.4 us (42%)
  starting transfers between devices  14.5 us (40%)
  waiting for transfers between devices  5.72 us (16%)
  between operations  0.75 us (2%)
    pallas_call x1, Pallas kernels, per_device(): pl.pallas_call(side_kernel, out_shape=(pltpu.VMEM((2 * KR, count * rows),...  7.37 us
    ppermute x2, starting transfers between devices, per_device(): moved = lax.ppermute(upper, 'fsdp', pairs)  6.56 us
    ppermute x3, starting transfers between devices, per_device(): parts.append(lax.ppermute(mine[hop], 'fsdp', pairs))  4.5 us
    pallas_call x2, Pallas kernels, make_tables(): pl.pallas_call(functools.partial(table_kernel, 32, which), out_shape=[plt...  3.89 us
    ppermute x3, waiting for transfers between devices, per_device(): parts.append(lax.ppermute(mine[hop], 'fsdp', pairs))  2.77 us
    ppermute x3, starting transfers between devices, add(): moved.append(lax.ppermute(value, axis, pairs))  2.21 us
    ppermute x3, waiting for transfers between devices, add(): moved.append(lax.ppermute(value, axis, pairs))  2.2 us
    pallas_call x1, Pallas kernels, per_device(): pl.pallas_call(feature_kernel, out_shape=[pltpu.VMEM((spots, shards, slot...  1.82 us
  transfers between devices with their start and end apart: 10, of which 7 were waited for; matrix products, arithmetic and copies ran while one was open for 0% of the time, Pallas kernels for 15%

profile of v8, /device:TPU:0, one launch (start us, length us, event | category | flops | bytes accessed | tf_op | source)
XLA Modules:
  0.0 36.5 jit_solution(14624912979031325709)
XLA Ops:
  0.7 7.4 %sides.1 = (f32[8,2048]{1,0:T(8,128)S(1)}, f32[8,2048]{1,0:T(8,128)S(1)}, s32[8,128]{1,0:T(8,128)S(1)}, bf16[2,1024,2048]{2,1,0:T(8,128)(2,1)S(1)}, bf16[2,1024,...) custom-call(bf16[2,1024,2048]{2,1,0:T(8,128)(2,1)} %hidden_hbm.1, bf16[2,1024,2048]{2,1,0:T(8,128)(2,1)} %query_hbm.1, ...), custom_call_target="tpu_custom_call" | custom-call | tf_op jit(solution)/shard_map/sides/pallas_call | solution.py:366
  8.0 3.1 %collective-permute-start = (f32[8,2048]{1,0:T(8,128)S(1)}, f32[8,2048]{1,0:T(8,128)S(1)}, u32[]{:S(2)}, u32[]{:S(2)}) collective-permute-start(f32[8,2048]{1,0:T(8,128)S(1)} %get-tuple-element.17), channel_id=1, source_target_pairs={{0,4},{4,0},{8,12},{12,8},{1,5},{5,1},{9,13},{13,9},{2,6},{6,2},{1... | collective-permute-start | bytes 196616 | tf_op jit(solution)/shard_map/ppermute | solution.py:423
  11.1 0.1 collective-permute-start.2
  11.2 1.8 %tables.2.wide_in = bf16[2048,512]{1,0:T(8,128)(2,1)S(1)} custom-call(s32[8,128]{1,0:T(8,128)S(1)} %get-tuple-element.20.scalar_ref), custom_call_target="tpu_custom_call" | custom-call | tf_op jit(solution)/shard_map/tables/pallas_call | solution.py:408
  13.0 0.3 collective-permute-done
  13.4 3.5 %collective-permute-start.1 = (f32[8,2048]{1,0:T(8,128)S(1)}, f32[8,2048]{1,0:T(8,128)S(1)}, u32[]{:S(2)}, u32[]{:S(2)}) collective-permute-start(f32[8,2048]{1,0:T(8,128)S(1)} %add.21), channel_id=1, source_target_pairs={{0,8},{4,12},{8,0},{12,4},{1,9},{5,13},{9,1},{13,5},{2,10},{6,14},... | collective-permute-start | bytes 196616 | tf_op jit(solution)/shard_map/ppermute | solution.py:423
  16.8 0.0 collective-permute-done.2
  16.9 1.2 %collective-permute-start.3 = (f32[8,2048]{1,0:T(8,128)S(1)}, f32[8,2048]{1,0:T(8,128)S(1)}, u32[]{:S(2)}, u32[]{:S(2)}) collective-permute-start(f32[8,2048]{1,0:T(8,128)S(1)} %add.23), channel_id=1, source_target_pairs={{0,8},{4,12},{8,0},{12,4},{1,9},{5,13},{9,1},{13,5},{2,10},{6,14},... | collective-permute-start | bytes 196616 | tf_op jit(solution)/shard_map/ppermute | solution.py:424
  18.0 2.1 %tables.3 = (bf16[2048,512]{1,0:T(8,128)(2,1)S(1)}, bf16[256,512]{1,0:T(8,128)(2,1)S(1)}) custom-call(s32[8,128]{1,0:T(8,128)S(1)} %get-tuple-element.20.scalar_ref), custom_call_target="tpu_custom_call" | custom-call | tf_op jit(solution)/shard_map/tables/pallas_call | solution.py:408
  20.2 1.5 %upper.1.upper_ref = f32[16,512]{1,0:T(8,128)S(1)} custom-call(f32[8,2048]{1,0:T(8,128)S(1)} %add.22.side_ref, bf16[2,1024,2048]{2,1,0:T(8,128)(2,1)S(1)} %get-tuple-element.18.hidden_ref, bf16[2048,512]{1,0:T(8,128)(2,1)S(1)} %tables.2.wide_in), custom_call_target="tpu_custom_call" | custom-call | tf_op jit(solution)/shard_map/upper/pallas_call | solution.py:430
  21.7 0.4 %collective-permute-done.3 = f32[8,2048]{1,0:T(8,128)S(1)} collective-permute-done((f32[8,2048]{1,0:T(8,128)S(1)}, f32[8,2048]{1,0:T(8,128)S(1)}, u32[]{:S(2)}, u32[]{:S(2)}) %collective-permute-start.3) | collective-permute-done | bytes 65568 | tf_op jit(solution)/shard_map/ppermute | solution.py:424
  22.1 1.8 %features.1 = (f32[2,4,8,256]{3,2,1,0:T(8,128)S(1)}, f32[2,4,8,256]{3,2,1,0:T(8,128)S(1)}) custom-call(f32[16,512]{1,0:T(8,128)S(1)} %upper.1.upper_ref, f32[8,2048]{1,0:T(8,128)S(1)} %add.24.side_ref, bf16[2,1024,2048]{2,1,0:T(8,128)(2,1)S(1)} %get-tuple-element.23.query_ref, bf16[2,1024,256]{2,1,0:T(8,128)(2,1)S(1)} %get-tuple-element.24.value_ref, ...), custom_call_target="tpu_custom_call" | custom-call | tf_op jit(solution)/shard_map/features/pallas_call | solution.py:441
  24.0 0.7 %collective-permute-start.6 = (f32[4,8,256]{2,1,0:T(8,128)S(1)}, f32[4,8,256]{2,1,0:T(8,128)S(1)}, u32[]{:S(2)}, u32[]{:S(2)}) collective-permute-start(f32[4,8,256]{2,1,0:T(8,128)S(1)} %slice_bitcast_fusion), channel_id=1, source_target_pairs={{0,2},{2,0},{1,3},{3,1},{4,6},{6,4},{5,7},{7,5},{8,10},{10,8},{9,1... | collective-permute-start | bytes 98312 | tf_op jit(solution)/shard_map/ppermute | solution.py:452
  24.7 1.5 %collective-permute-start.5 = (f32[4,8,256]{2,1,0:T(8,128)S(1)}, f32[4,8,256]{2,1,0:T(8,128)S(1)}, u32[]{:S(2)}, u32[]{:S(2)}) collective-permute-start(f32[4,8,256]{2,1,0:T(8,128)S(1)} %get-tuple-element.30), channel_id=1, source_target_pairs={{0,1},{1,0},{2,3},{3,2},{4,5},{5,4},{6,7},{7,6},{8,9},{9,8},{10,11... | collective-permute-start | bytes 98312 | tf_op jit(solution)/shard_map/ppermute | solution.py:452
  26.2 2.0 %collective-permute-done.6 = f32[4,8,256]{2,1,0:T(8,128)S(1)} collective-permute-done((f32[4,8,256]{2,1,0:T(8,128)S(1)}, f32[4,8,256]{2,1,0:T(8,128)S(1)}, u32[]{:S(2)}, u32[]{:S(2)}) %collective-permute-start.6) | collective-permute-done | bytes 32800 | tf_op jit(solution)/shard_map/ppermute | solution.py:452
  28.2 0.2 collective-permute-done.4
  28.4 0.0 collective-permute-done.5
  28.4 1.9 %collective-permute-start.9 = (f32[8,256]{1,0:T(8,128)S(1)}, f32[8,256]{1,0:T(8,128)S(1)}, u32[]{:S(2)}, u32[]{:S(2)}) collective-permute-start(f32[8,256]{1,0:T(8,128)S(1)} %get-tuple-element.32), channel_id=1, source_target_pairs={{0,4},{4,8},{8,12},{12,0},{1,5},{5,9},{9,13},{13,1},{2,6},{6,10},{... | collective-permute-start | bytes 24584 | tf_op jit(solution)/shard_map/ppermute | solution.py:464
  30.3 1.8 %collective-permute-start.8 = (f32[8,256]{1,0:T(8,128)S(1)}, f32[8,256]{1,0:T(8,128)S(1)}, u32[]{:S(2)}, u32[]{:S(2)}) collective-permute-start(f32[8,256]{1,0:T(8,128)S(1)} %get-tuple-element.33), channel_id=1, source_target_pairs={{0,8},{4,12},{8,0},{12,4},{1,9},{5,13},{9,1},{13,5},{2,10},{6,14},... | collective-permute-start | bytes 24584 | tf_op jit(solution)/shard_map/ppermute | solution.py:464
  32.0 0.9 %collective-permute-start.7 = (f32[8,256]{1,0:T(8,128)S(1)}, f32[8,256]{1,0:T(8,128)S(1)}, u32[]{:S(2)}, u32[]{:S(2)}) collective-permute-start(f32[8,256]{1,0:T(8,128)S(1)} %get-tuple-element.34), channel_id=1, source_target_pairs={{0,12},{4,0},{8,4},{12,8},{1,13},{5,1},{9,5},{13,9},{2,14},{6,2},{... | collective-permute-start | bytes 24584 | tf_op jit(solution)/shard_map/ppermute | solution.py:464
  32.9 1.0 %collective-permute-done.9 = f32[8,256]{1,0:T(8,128)S(1)} collective-permute-done((f32[8,256]{1,0:T(8,128)S(1)}, f32[8,256]{1,0:T(8,128)S(1)}, u32[]{:S(2)}, u32[]{:S(2)}) %collective-permute-start.9) | collective-permute-done | bytes 8224 | tf_op jit(solution)/shard_map/ppermute | solution.py:464
  33.9 0.9 %collective-permute-done.8 = f32[8,256]{1,0:T(8,128)S(1)} collective-permute-done((f32[8,256]{1,0:T(8,128)S(1)}, f32[8,256]{1,0:T(8,128)S(1)}, u32[]{:S(2)}, u32[]{:S(2)}) %collective-permute-start.8) | collective-permute-done | bytes 8224 | tf_op jit(solution)/shard_map/ppermute | solution.py:464
  34.8 0.9 %collective-permute-done.7 = f32[8,256]{1,0:T(8,128)S(1)} collective-permute-done((f32[8,256]{1,0:T(8,128)S(1)}, f32[8,256]{1,0:T(8,128)S(1)}, u32[]{:S(2)}, u32[]{:S(2)}) %collective-permute-start.7) | collective-permute-done | bytes 8224 | tf_op jit(solution)/shard_map/ppermute | solution.py:464
  35.7 0.8 %finish.1 = f32[2,1024]{1,0:T(2,128)} custom-call(f32[4,8,256]{2,1,0:T(8,128)S(1)} %pad_maximum_fusion.pieces_ref), custom_call_target="tpu_custom_call" | custom-call | tf_op jit(solution)/shard_map/finish/pallas_call | solution.py:466
  (11 shorter events, 0.1 us)
Async XLA Ops:
  8.0 5.3 %collective-permute-start = (f32[8,2048]{1,0:T(8,128)S(1)}, f32[8,2048]{1,0:T(8,128)S(1)}, u32[]{:S(2)}, u32[]{:S(2)}) collective-permute-start(f32[8,2048]{1,0:T(8,128)S(1)} %get-tuple-element.17), channel_id=1, source_target_pairs={{0,4},{4,0},{8,12},{12,8},{1,5},{5,1},{9,13},{13,9},{2,6},{6,2},{1... | collective-permute-start | bytes 196616 | tf_op jit(solution)/shard_map/ppermute | solution.py:423
  11.1 5.7 %collective-permute-start.2 = (f32[8,2048]{1,0:T(8,128)S(1)}, f32[8,2048]{1,0:T(8,128)S(1)}, u32[]{:S(2)}, u32[]{:S(2)}) collective-permute-start(f32[8,2048]{1,0:T(8,128)S(1)} %get-tuple-element.19), channel_id=1, source_target_pairs={{0,4},{4,0},{8,12},{12,8},{1,5},{5,1},{9,13},{13,9},{2,6},{6,2},{1... | collective-permute-start | bytes 196616 | tf_op jit(solution)/shard_map/ppermute | solution.py:424
  13.4 6.8 %collective-permute-start.1 = (f32[8,2048]{1,0:T(8,128)S(1)}, f32[8,2048]{1,0:T(8,128)S(1)}, u32[]{:S(2)}, u32[]{:S(2)}) collective-permute-start(f32[8,2048]{1,0:T(8,128)S(1)} %add.21), channel_id=1, source_target_pairs={{0,8},{4,12},{8,0},{12,4},{1,9},{5,13},{9,1},{13,5},{2,10},{6,14},... | collective-permute-start | bytes 196616 | tf_op jit(solution)/shard_map/ppermute | solution.py:423
  16.9 5.2 %collective-permute-start.3 = (f32[8,2048]{1,0:T(8,128)S(1)}, f32[8,2048]{1,0:T(8,128)S(1)}, u32[]{:S(2)}, u32[]{:S(2)}) collective-permute-start(f32[8,2048]{1,0:T(8,128)S(1)} %add.23), channel_id=1, source_target_pairs={{0,8},{4,12},{8,0},{12,4},{1,9},{5,13},{9,1},{13,5},{2,10},{6,14},... | collective-permute-start | bytes 196616 | tf_op jit(solution)/shard_map/ppermute | solution.py:424
  24.0 4.2 %collective-permute-start.6 = (f32[4,8,256]{2,1,0:T(8,128)S(1)}, f32[4,8,256]{2,1,0:T(8,128)S(1)}, u32[]{:S(2)}, u32[]{:S(2)}) collective-permute-start(f32[4,8,256]{2,1,0:T(8,128)S(1)} %slice_bitcast_fusion), channel_id=1, source_target_pairs={{0,2},{2,0},{1,3},{3,1},{4,6},{6,4},{5,7},{7,5},{8,10},{10,8},{9,1... | collective-permute-start | bytes 98312 | tf_op jit(solution)/shard_map/ppermute | solution.py:452
  24.7 3.7 %collective-permute-start.4 = (f32[4,8,256]{2,1,0:T(8,128)S(1)}, f32[4,8,256]{2,1,0:T(8,128)S(1)}, u32[]{:S(2)}, u32[]{:S(2)}) collective-permute-start(f32[4,8,256]{2,1,0:T(8,128)S(1)} %get-tuple-element.29), channel_id=1, source_target_pairs={{0,3},{1,2},{2,1},{3,0},{4,7},{5,6},{6,5},{7,4},{8,11},{9,10},{10,... | collective-permute-start | bytes 98312 | tf_op jit(solution)/shard_map/ppermute | solution.py:452
  24.7 3.7 %collective-permute-start.5 = (f32[4,8,256]{2,1,0:T(8,128)S(1)}, f32[4,8,256]{2,1,0:T(8,128)S(1)}, u32[]{:S(2)}, u32[]{:S(2)}) collective-permute-start(f32[4,8,256]{2,1,0:T(8,128)S(1)} %get-tuple-element.30), channel_id=1, source_target_pairs={{0,1},{1,0},{2,3},{3,2},{4,5},{5,4},{6,7},{7,6},{8,9},{9,8},{10,11... | collective-permute-start | bytes 98312 | tf_op jit(solution)/shard_map/ppermute | solution.py:452
  28.4 5.5 %collective-permute-start.9 = (f32[8,256]{1,0:T(8,128)S(1)}, f32[8,256]{1,0:T(8,128)S(1)}, u32[]{:S(2)}, u32[]{:S(2)}) collective-permute-start(f32[8,256]{1,0:T(8,128)S(1)} %get-tuple-element.32), channel_id=1, source_target_pairs={{0,4},{4,8},{8,12},{12,0},{1,5},{5,9},{9,13},{13,1},{2,6},{6,10},{... | collective-permute-start | bytes 24584 | tf_op jit(solution)/shard_map/ppermute | solution.py:464
  30.3 4.5 %collective-permute-start.8 = (f32[8,256]{1,0:T(8,128)S(1)}, f32[8,256]{1,0:T(8,128)S(1)}, u32[]{:S(2)}, u32[]{:S(2)}) collective-permute-start(f32[8,256]{1,0:T(8,128)S(1)} %get-tuple-element.33), channel_id=1, source_target_pairs={{0,8},{4,12},{8,0},{12,4},{1,9},{5,13},{9,1},{13,5},{2,10},{6,14},... | collective-permute-start | bytes 24584 | tf_op jit(solution)/shard_map/ppermute | solution.py:464
  32.0 3.7 %collective-permute-start.7 = (f32[8,256]{1,0:T(8,128)S(1)}, f32[8,256]{1,0:T(8,128)S(1)}, u32[]{:S(2)}, u32[]{:S(2)}) collective-permute-start(f32[8,256]{1,0:T(8,128)S(1)} %get-tuple-element.34), channel_id=1, source_target_pairs={{0,12},{4,0},{8,4},{12,8},{1,13},{5,1},{9,5},{13,9},{2,14},{6,2},{... | collective-permute-start | bytes 24584 | tf_op jit(solution)/shard_map/ppermute | solution.py:464
